TPU v7x, 32 devices: a whole 2x2x4 slice. The times are simulated.
32 devices in a mesh: dp: 8 (over z, x), tensor: 4 (over y, core).
Axes of the slice: x: 2, y: 2, z: 4, core: 2. Of those that a mesh axis runs over, the one named last changes fastest.
Arguments:
- tokens: bfloat16 [1024, 4096], P('dp', 'tensor'), may hold values from -6 to 6
- out_grad: bfloat16 [1024, 4096], P('dp', 'tensor'), may hold values from -6 to 6
- up_weight: bfloat16 [4096, 3584], P('dp', 'tensor'), may hold values from -0.09375 to 0.09375
- down_weight: bfloat16 [3584, 4096], P('tensor', 'dp'), may hold values from -0.09375 to 0.09375
- up_accum: float32 [8, 256, 3584], P('dp', None, 'tensor'), may hold values from -6 to 6
- down_accum: float32 [8, 3584, 256], P('dp', 'tensor'), may hold values from -6 to 6
- up_q: float32 [3584, 32], P('tensor'), may hold values from -6 to 6
- down_q: float32 [256, 32], replicated, may hold values from -6 to 6
Outputs:
- input_grad: bfloat16 [1024, 4096], P('dp', 'tensor')
- up_error: float32 [8, 256, 3584], P('dp', None, 'tensor')
- up_left: float32 [256, 32], replicated
- up_right: float32 [3584, 32], P('tensor')
- down_error: float32 [8, 3584, 256], P('dp', 'tensor')
- down_left: float32 [3584, 32], P('tensor')
- down_right: float32 [256, 32], replicated
All inputs are finite; a program needn't handle non-finite values.
Results may differ from a plain program's by a relative error of at most 0.02.
Values may be sent and summed in bfloat16 or wider, within the bound.
No kernel may reach another device: no remote copies, remote signals or barrier semaphores. Data moves between devices by JAX's collectives and lax.ppermute only.
A program may use at most 128 MiB of HBM per device.

v0:
```python
import math

import jax
import jax.numpy as jnp
from jax import lax
from jax.sharding import PartitionSpec as P


def contract_first(left_arr, right_arr):
    return lax.dot_general(
        left_arr,
        right_arr,
        (((0,), (0,)), ((), ())),
        preferred_element_type=jnp.float32,
        precision=lax.Precision.HIGHEST,
    )


def contract_last(left_arr, right_arr):
    return lax.dot_general(
        left_arr, right_arr, (((1,), (1,)), ((), ())), preferred_element_type=jnp.float32
    )


def solve_rows(gram, left_rows):
    lower_factor = jnp.linalg.cholesky(gram)
    return lax.linalg.triangular_solve(
        lower_factor, left_rows, left_side=False, lower=True, transpose_a=True
    )


def shards(tokens, out_grad, up_weight, down_weight, up_accum, down_accum, up_q, down_q):
    highest = lax.Precision.HIGHEST
    full_tokens, full_grads = (
        lax.all_gather(tokens, "tensor", axis=1, tiled=True),
        lax.all_gather(out_grad, "tensor", axis=1, tiled=True),
    )
    full_up = lax.all_gather(up_weight, "dp", axis=0, tiled=True)
    preact = jnp.dot(full_tokens, full_up, preferred_element_type=jnp.float32)
    back_act = contract_last(full_grads, lax.all_gather(down_weight, "dp", axis=1, tiled=True))
    squash = jax.nn.sigmoid(preact)
    act_out = (preact * squash).astype(jnp.bfloat16)
    hidden_grad = (back_act * squash * (1.0 + preact * (1.0 - squash))).astype(jnp.bfloat16)
    input_part = contract_last(hidden_grad, full_up)
    input_grad = lax.psum_scatter(
        input_part.astype(jnp.bfloat16), "tensor", scatter_dimension=1, tiled=True
    )
    window = up_accum.shape[1]
    grad_scale = 1.0 / math.sqrt(tokens.shape[0])
    replicas = lax.axis_size("dp")
    up_matrix = up_accum[0] + contract_first(full_tokens[:, :window], hidden_grad) * grad_scale
    down_matrix = down_accum[0] + contract_first(act_out, full_grads[:, :window]) * grad_scale
    up_partial = jnp.dot(up_matrix, up_q, precision=highest)
    down_partial = jnp.dot(down_matrix, down_q, precision=highest)
    up_sum = lax.psum(up_partial, ("dp", "tensor"))
    down_sum = lax.psum(down_partial.astype(jnp.bfloat16), "dp").astype(jnp.float32)
    up_left = solve_rows(jnp.dot(up_sum.T, up_sum, precision=highest), up_sum)
    down_gram = lax.psum(jnp.dot(down_sum.T, down_sum, precision=highest), "tensor")
    down_left = solve_rows(down_gram, down_sum)
    up_term = contract_first(up_matrix, up_left)
    down_term = contract_first(down_matrix, down_left)
    up_right = lax.psum(up_term.astype(jnp.bfloat16), "dp").astype(jnp.float32)
    down_right = lax.psum(down_term, ("dp", "tensor"))
    up_right = up_right / replicas
    down_right = down_right / replicas
    up_error = up_matrix - jnp.dot(up_left, up_right.T, precision=highest)
    down_error = down_matrix - jnp.dot(down_left, down_right.T, precision=highest)
    return (input_grad, up_error[None], up_left, up_right, down_error[None], down_left, down_right)


def solution(mesh):
    return jax.shard_map(
        shards,
        mesh=mesh,
        in_specs=(
            P("dp", "tensor"),
            P("dp", "tensor"),
            P("dp", "tensor"),
            P("tensor", "dp"),
            P("dp", None, "tensor"),
            P("dp", "tensor", None),
            P("tensor", None),
            P(),
        ),
        out_specs=(
            P("dp", "tensor"),
            P("dp", None, "tensor"),
            P(),
            P("tensor", None),
            P("dp", "tensor", None),
            P("tensor", None),
            P(),
        ),
        check_vma=False,
    )
```

profile of v0, /device:TPU:0, one launch (start us, length us, event | category | flops | bytes accessed | tf_op | source)
XLA Modules:
  0.0 458.4 jit_solution(11313580831145833314)
XLA Ops:
  7.2 0.0 all-gather.9.cloned.1.call-start
  7.2 0.7 all-gather.9.cloned.1.call-update
  7.9 0.0 all-gather.11.cloned.1.call-start
  8.0 0.7 all-gather.11.cloned.1.call-update
  8.7 0.0 all-gather.5.cloned.1.call-start
  8.7 0.7 all-gather.5.cloned.1.call-update
  9.4 0.0 all-gather.7.cloned.1.call-start
  9.4 0.5 all-gather.7.cloned.1.call-update
  10.0 0.0 all-reduce.3.cloned.1.call-start
  10.0 1.5 copy.15
  11.5 17.5 %all-gather.9.cloned.1.call-done = bf16[128,4096]{1,0:T(8,128)(2,1)} async-done(((bf16[128,1024]{1,0:T(8,128)(2,1)}), bf16[128,4096]{1,0:T(8,128)(2,1)}) %all-gather.9.cloned.1.call-update) | async-done | bytes 1048592 | tf_op jit(solution)/shard_map/all_gather | solution.py:35
  29.0 114.2 %all-gather.11.cloned.1.call-done = bf16[4096,896]{1,0:T(8,128)(2,1)} async-done(((bf16[512,896]{1,0:T(8,128)(2,1)}), bf16[4096,896]{1,0:T(8,128)(2,1)}) %all-gather.11.cloned.1.call-update) | async-done | bytes 7340048 | tf_op jit(solution)/shard_map/all_gather | solution.py:38
  143.3 4.7 %fusion.19 = f32[128,896]{1,0:T(8,128)S(1)} fusion(bf16[128,4096]{1,0:T(8,128)(2,1)} %all-gather.9.cloned.1.call-done, bf16[4096,896]{1,0:T(8,128)(2,1)} %all-gather.11.cloned.1.call-done), kind=kOutput, calls=%fused_computation.41 | convolution fusion | flops 939524096 | bytes 8847360 | tf_op jit(solution)/shard_map/dot_general | solution.py:39
  147.9 11.8 %all-gather.5.cloned.1.call-done = bf16[128,4096]{1,0:T(8,128)(2,1)} async-done(((bf16[128,1024]{1,0:T(8,128)(2,1)}), bf16[128,4096]{1,0:T(8,128)(2,1)}) %all-gather.5.cloned.1.call-update) | async-done | bytes 1048592 | tf_op jit(solution)/shard_map/all_gather | solution.py:36
  159.8 1.6 fusion.1
  161.3 0.9 convolution_convert_fusion.1
  162.3 38.6 %psum.37 = bf16[896,32]{0,1:T(8,128)(2,1)S(1)} all-reduce(bf16[896,32]{0,1:T(8,128)(2,1)S(1)} %convolution_convert_fusion.1), channel_id=1, replica_groups=mesh['dp'=8,'tensor'=4] {'dp'}, use_global_device_ids=true, to_apply=%region_5.0 | all-reduce | flops 28672 | bytes 114688 | tf_op jit(solution)/shard_map/psum | solution.py:56
  200.9 0.1 fusion.22
  201.0 10.5 %psum.38 = f32[32,32]{0,1:T(8,128)S(1)} all-reduce(f32[32,32]{0,1:T(8,128)S(1)} %fusion.22), channel_id=1, replica_groups=mesh['dp'=8,'tensor'=4] {'tensor'}, use_global_device_ids=true, to_apply=%region_6.8 | all-reduce | flops 1024 | bytes 8192 | tf_op jit(solution)/shard_map/psum | solution.py:58
  211.5 0.1 copy.19
  211.6 2.9 cholesky.55
  214.6 0.6 compare_reduce_fusion
  215.2 0.7 fusion.11
  215.9 2.4 custom-call.9
  218.3 0.3 fusion.12
  218.6 1.2 fusion.23
  219.8 55.8 %all-gather.7.cloned.1.call-done = bf16[896,4096]{1,0:T(8,128)(2,1)} async-done(((bf16[896,512]{1,0:T(8,128)(2,1)}), bf16[896,4096]{1,0:T(8,128)(2,1)}) %all-gather.7.cloned.1.call-update) | async-done | bytes 7340048 | tf_op jit(solution)/shard_map/all_gather | solution.py:40
  275.6 5.9 %fusion.6 = bf16[128,896]{1,0:T(8,128)(2,1)S(1)} fusion(bf16[128,4096]{1,0:T(8,128)(2,1)} %all-gather.5.cloned.1.call-done, bf16[896,4096]{1,0:T(8,128)(2,1)} %all-gather.7.cloned.1.call-done, f32[128,896]{1,0:T(8,128)S(1)} %fusion.19), kind=kOutput, calls=%fused_computation.12 | convolution fusion | flops 940556288 | bytes 9076736 | tf_op jit(solution)/shard_map/dot_general | solution.py:20
  281.5 1.2 fusion.4
  282.7 1.2 fusion.20
  283.9 0.0 all-reduce.3.cloned.1.call-update
  283.9 0.0 reduce-scatter.2.cloned.1.call-start
  284.0 6.5 %convolution_convert_fusion = bf16[128,4096]{1,0:T(8,128)(2,1)} fusion(bf16[128,896]{1,0:T(8,128)(2,1)S(1)} %fusion.6, bf16[4096,896]{1,0:T(8,128)(2,1)} %all-gather.11.cloned.1.call-done), kind=kOutput, calls=%fused_computation | convolution fusion | flops 940048384 | bytes 8617984 | tf_op jit(solution)/shard_map/dot_general | solution.py:20
  290.5 0.0 reduce-scatter.2.cloned.1.call-update
  290.5 110.0 %all-reduce.3.cloned.1.call-done = (f32[256,32]{0,1:T(8,128)}, f32[256,32]{0,1:T(8,128)}) async-done(((f32[256,32]{0,1:T(8,128)}, f32[256,32]{0,1:T(8,128)}), (f32[256,32]{0,1:T(8,128)}, f32[256,32]{0,1:T(8,128)})) %all-reduce.3.cloned.1.call-update) | async-done | bytes 65552 | tf_op jit(solution)/shard_map/psum | solution.py:55
  400.5 1.0 fusion.21
  401.5 0.1 copy.16
  401.5 2.9 cholesky.44
  404.5 0.6 compare_reduce_fusion.1
  405.1 0.7 fusion.10
  405.8 2.4 custom-call.8
  408.2 1.0 fusion.15
  409.3 0.9 convolution_convert_fusion.2
  410.2 36.6 %psum.36 = bf16[896,32]{0,1:T(8,128)(2,1)S(1)} all-reduce(bf16[896,32]{0,1:T(8,128)(2,1)S(1)} %convolution_convert_fusion.2), channel_id=1, replica_groups=mesh['dp'=8,'tensor'=4] {'dp'}, use_global_device_ids=true, to_apply=%region_4.0 | all-reduce | flops 28672 | bytes 114688 | tf_op jit(solution)/shard_map/psum | solution.py:62
  446.8 0.9 fusion.2
  447.7 1.2 copy.20
  448.9 0.8 broadcast_multiply_fusion
  449.7 1.9 fusion
  (18 shorter events, 0.1 us)
Async XLA Ops:
  7.2 275.5 %copy-start = (f32[896,32]{0,1:T(8,128)S(1)}, f32[896,32]{0,1:T(8,128)}, u32[]{:S(2)}) copy-start(f32[896,32]{0,1:T(8,128)} %param.15) | copy-start | bytes 344068
  7.2 21.9 %all-gather.9.cloned.1.call-start = ((), (), s32[]{:S(2)}) async-start(), calls=%async_computation.3 | async-start | bytes 1310720 | tf_op jit(solution)/shard_map/all_gather | solution.py:35
  7.9 135.3 %all-gather.11.cloned.1.call-start = ((), (), s32[]{:S(2)}) async-start(), calls=%async_computation.4 | async-start | bytes 8257536 | tf_op jit(solution)/shard_map/all_gather | solution.py:38
  8.7 151.1 %all-gather.5.cloned.1.call-start = ((), (), s32[]{:S(2)}) async-start(), calls=%async_computation.1 | async-start | bytes 1310720 | tf_op jit(solution)/shard_map/all_gather | solution.py:36
  9.4 266.2 %all-gather.7.cloned.1.call-start = ((), (), s32[]{:S(2)}) async-start(), calls=%async_computation.2 | async-start | bytes 8257536 | tf_op jit(solution)/shard_map/all_gather | solution.py:40
  10.0 390.5 %all-reduce.3.cloned.1.call-start = ((), (), s32[]{:S(2)}) async-start(), calls=%async_computation.6 | async-start | bytes 131072 | tf_op jit(solution)/shard_map/psum | solution.py:55
  11.5 149.8 %copy-start.5 = (f32[256,32]{0,1:T(8,128)S(1)}, f32[256,32]{0,1:T(8,128)}, u32[]{:S(2)}) copy-start(f32[256,32]{0,1:T(8,128)} %param.16) | copy-start | bytes 98308
  218.6 231.1 %copy-start.1 = (f32[896,32]{0,1:T(8,128)}, f32[896,32]{0,1:T(8,128)S(1)}, u32[]{:S(2)}) copy-start(f32[896,32]{0,1:T(8,128)S(1)} %fusion.12) | copy-start | bytes 344068
  283.9 167.6 %reduce-scatter.2.cloned.1.call-start = ((), (), s32[]{:S(2)}) async-start(), calls=%async_computation.5 | async-start | bytes 1310720 | tf_op jit(solution)/shard_map/reduce_scatter | solution.py:45
  409.2 42.3 %copy-start.3 = (f32[256,32]{0,1:T(8,128)}, f32[256,32]{0,1:T(8,128)S(1)}, u32[]{:S(2)}) copy-start(f32[256,32]{0,1:T(8,128)S(1)} %fusion.15) | copy-start | bytes 98308
  446.8 4.8 %copy-start.2 = (f32[896,32]{0,1:T(8,128)}, f32[896,32]{0,1:T(8,128)S(1)}, u32[]{:S(2)}) copy-start(f32[896,32]{0,1:T(8,128)S(1)} %convert_multiply_fusion) | copy-start | bytes 344068
  449.7 1.9 copy-start.4
Sparse Core Ops, SparseCore 0:
  9.6 19.4 all-gather.8
  31.2 111.9 all-gather.10
  144.8 14.9 all-gather.4
  161.7 113.9 all-gather.6
  284.0 116.3 all-reduce.2
  403.4 26.1 reduce-scatter.1
where the time goes:
time: 459 us; the launch traced here: 458 us
  waiting for transfers between devices  312 us (68%)
  blocking collectives  85.7 us (19%)
  matrix products  29.2 us (6%)
  between operations  14.3 us (3%)
  other arithmetic  14.2 us (3%)
    all_gather x1, waiting for transfers between devices, shards(): full_up = lax.all_gather(up_weight, 'dp', axis=0, tiled=True)  114 us
    psum x1, waiting for transfers between devices, shards(): up_sum = lax.psum(up_partial, ('dp', 'tensor'))  110 us
    all_gather x1, waiting for transfers between devices, shards(): lax.all_gather(down_weight, 'dp', axis=1, tiled=True)  55.8 us
    psum x1, blocking collectives, shards(): lax.psum(down_partial.astype(jnp.bfloat16), 'dp').astype(jnp.float32)  38.6 us
    psum x1, blocking collectives, shards(): up_right = lax.psum(up_term.astype(jnp.bfloat16), 'dp').astype(jnp.float32)  36.6 us
    all_gather x1, waiting for transfers between devices, shards(): lax.all_gather(tokens, 'tensor', axis=1, tiled=True)  17.5 us
    dot_general x2, matrix products, contract_last(): lax.dot_general(left_arr, right_arr, (((1,), (1,)), ((), ())), preferred_...  12.4 us
    all_gather x1, waiting for transfers between devices, shards(): lax.all_gather(out_grad, 'tensor', axis=1, tiled=True)  11.8 us
  transfers between devices with their start and end apart: 6, of which 5 were waited for; matrix products, arithmetic and copies ran while one was open for 8% of the time, Pallas kernels for 0%

commit v1 on v0

v1 whole, which is shorter than its diff:
```python
import math

import jax
import jax.numpy as jnp
from jax import lax
from jax.sharding import PartitionSpec as P

BF = jnp.bfloat16
F32 = jnp.float32
HIGHEST = lax.Precision.HIGHEST


def flip(arr, axis, mask):
    size = lax.axis_size(axis)
    return lax.ppermute(arr, axis, [(i, i ^ mask) for i in range(size)])


def bits_of(size):
    return [1 << b for b in range(size.bit_length() - 1)]


def dot(a, b, dims=((1,), (0,)), precision=None):
    return lax.dot_general(a, b, (dims, ((), ())), preferred_element_type=F32, precision=precision)


def allsum(arr, axis, masks):
    for mask in masks:
        arr = arr + flip(arr, axis, mask)
    return arr


def broadcast_first(arr, axis):
    arr = jnp.where(lax.axis_index(axis) == 0, arr, jnp.zeros_like(arr))
    for mask in bits_of(lax.axis_size(axis)):
        arr = arr + lax.ppermute(arr, axis, [(i, i + mask) for i in range(mask)])
    return arr


def inverse_factor(gram):
    lower = jnp.linalg.cholesky(gram)
    return lax.linalg.triangular_solve(
        lower, jnp.eye(gram.shape[0], dtype=F32), left_side=False, lower=True, transpose_a=True
    )


def spread(arr, half, core, zrel, zbits, tbits):
    rows, width = arr.shape
    lo, hi = arr[:, : width // 2], arr[:, width // 2 :]
    mine = jnp.where(half == 0, lo, hi)
    other = jnp.where(half == 0, hi, lo)
    blocks = jnp.stack([mine, flip(other, "tensor", 1)])
    for mask in tbits[1:]:
        blocks = jnp.concatenate([blocks, flip(blocks, "tensor", mask)])
    count = blocks.shape[0]
    kept = []
    for k in range(count):
        piece = lax.dynamic_index_in_dim(blocks, zrel ^ k, 0, keepdims=False)
        kept.append(piece if k == 0 else flip(piece, "dp", 2 * k))
    kept = jnp.stack(kept)
    return kept, flip(kept, "tensor", 1)


def reduce_z(part_of, zbits):
    count = 2 ** len(zbits)
    first = zbits[0]
    out_ks = [k for k in range(count) if k & first]
    keep_ks = [k for k in range(count) if not k & first]
    got = flip(part_of(out_ks).astype(BF), "dp", 2 * first)
    acc = part_of(keep_ks) + got.astype(F32)
    for bit in zbits[1:]:
        sel = [n for n, k in enumerate(keep_ks) if k & bit]
        stay = [n for n, k in enumerate(keep_ks) if not k & bit]
        send = jnp.stack([acc[n] for n in sel]).astype(BF)
        acc = jnp.stack([acc[n] for n in stay]) + flip(send, "dp", 2 * bit).astype(F32)
        keep_ks = [keep_ks[n] for n in stay]
    return acc[0]


def shards(tokens, out_grad, up_weight, down_weight, up_accum, down_accum, up_q, down_q):
    replicas, columns = lax.axis_size("dp"), lax.axis_size("tensor")
    dp_i, t_i = lax.axis_index("dp"), lax.axis_index("tensor")
    x_i, z_i = dp_i % 2, dp_i // 2
    core = t_i % 2
    zcount = replicas // 2
    zbits, tbits, dbits = bits_of(zcount), bits_of(columns), bits_of(replicas)
    rows, width = tokens.shape
    window = up_accum.shape[1]
    scale = 1.0 / math.sqrt(rows)
    half = core ^ x_i
    zrel = z_i ^ t_i

    up_other = flip(up_weight, "dp", 1)
    tok_keep, tok_other = spread(tokens, half, core, zrel, zbits, tbits)
    down_other = flip(down_weight, "dp", 1)
    grad_keep, grad_other = spread(out_grad, half, core, zrel, zbits, tbits)
    windows = broadcast_first(jnp.stack([tokens[:, :window], out_grad[:, :window]]), "tensor")
    tok_win, grad_win = windows[0], windows[1]

    def partial(kept, other, own_w, par_w, dims):
        lhs_own = jnp.where(core == 0, kept, other)
        lhs_par = jnp.where(core == 0, other, kept)

        def part_of(ks):
            a = jnp.concatenate([lhs_own[k] for k in ks])
            b = jnp.concatenate([lhs_par[k] for k in ks])
            return (dot(a, own_w, dims) + dot(b, par_w, dims)).reshape(len(ks), rows, -1)

        return part_of

    preact = reduce_z(partial(tok_keep, tok_other, up_weight, up_other, ((1,), (0,))), zbits)
    back_act = reduce_z(partial(grad_keep, grad_other, down_weight, down_other, ((1,), (1,))), zbits)
    squash = jax.nn.sigmoid(preact)
    act_out = (preact * squash).astype(BF)
    hidden = (back_act * squash * (1.0 + preact * (1.0 - squash))).astype(BF)

    down_matrix = down_accum[0] + dot(act_out, grad_win, ((0,), (0,))) * scale
    down_sum = allsum(dot(down_matrix, down_q, precision=HIGHEST), "dp", dbits)
    down_gram = dot(down_sum, down_sum, ((0,), (0,)), HIGHEST)
    down_term = dot(down_matrix, down_sum, ((0,), (0,)), HIGHEST)
    both = allsum(jnp.concatenate([down_term, down_gram]), "tensor", tbits)
    down_gram = both[window:]
    down_term = allsum(both[:window], "dp", dbits)
    down_inv = inverse_factor(down_gram)
    down_left = dot(down_sum, down_inv, precision=HIGHEST)
    down_right = dot(down_term, down_inv, precision=HIGHEST) / replicas
    down_error = down_matrix - dot(down_left, down_right, ((1,), (1,)), HIGHEST)

    gathered = {0: hidden}
    for bit in reversed(zbits):
        ks = sorted(gathered)
        got = flip(jnp.stack([gathered[k] for k in ks]), "dp", 2 * bit)
        for n, k in enumerate(ks):
            gathered[k | bit] = got[n]
    up_matrix = up_accum[0] + dot(tok_win, hidden, ((0,), (0,))) * scale
    up_sum = allsum(allsum(dot(up_matrix, up_q, precision=HIGHEST), "tensor", tbits), "dp", dbits)
    up_term = allsum(dot(up_matrix, up_sum, ((0,), (0,)), HIGHEST), "dp", dbits)
    up_inv = inverse_factor(dot(up_sum, up_sum, ((0,), (0,)), HIGHEST))
    up_left = dot(up_sum, up_inv, precision=HIGHEST)
    up_right = dot(up_term, up_inv, precision=HIGHEST) / replicas
    up_error = up_matrix - dot(up_left, up_right, ((1,), (1,)), HIGHEST)

    hid = jnp.concatenate([gathered[k] for k in range(zcount)])
    w_keep = jnp.where(core == 0, up_weight, up_other)
    w_send = jnp.where(core == 0, up_other, up_weight)
    send = dot(hid, w_send, ((1,), (1,))).astype(BF)
    keep = dot(hid, w_keep, ((1,), (1,))).astype(BF)
    mine = (keep.astype(F32) + flip(send, "tensor", 1).astype(F32)).astype(BF)
    mine = mine.reshape(zcount, 1, rows, width // 2)
    for bit in zbits:
        mine = mine.reshape((mine.shape[0] // 2, 2) + mine.shape[1:])
        got = flip(mine[:, 1], "dp", 2 * bit)
        mine = jnp.concatenate([mine[:, 0], got], axis=1)
    blocks = mine[0]
    blocks = jnp.stack(
        [lax.dynamic_index_in_dim(blocks, zrel ^ j, 0, keepdims=False) for j in range(columns)]
    )
    for mask in reversed(tbits[1:]):
        n = blocks.shape[0] // 2
        got = flip(blocks[n:], "tensor", mask)
        blocks = (blocks[:n].astype(F32) + got.astype(F32)).astype(BF)
    got = flip(blocks[1], "tensor", 1)
    input_grad = jnp.concatenate(
        [jnp.where(half == 0, blocks[0], got), jnp.where(half == 0, got, blocks[0])], axis=1
    )
    return (input_grad, up_error[None], up_left, up_right, down_error[None], down_left, down_right)


def solution(mesh):
    return jax.shard_map(
        shards,
        mesh=mesh,
        in_specs=(
            P("dp", "tensor"),
            P("dp", "tensor"),
            P("dp", "tensor"),
            P("tensor", "dp"),
            P("dp", None, "tensor"),
            P("dp", "tensor", None),
            P("tensor", None),
            P(),
        ),
        out_specs=(
            P("dp", "tensor"),
            P("dp", None, "tensor"),
            P(),
            P("tensor", None),
            P("dp", "tensor", None),
            P("tensor", None),
            P(),
        ),
        check_vma=False,
    )
```

time: 459 us -> 227 us (0.49)
  waiting for transfers between devices: 312 us -> 116 us
  blocking collectives: 85.7 us -> 0 us
  starting transfers between devices: 0.23 us -> 56.4 us
  between operations: 14.3 us -> 1.35 us
  other arithmetic: 14.2 us -> 26.5 us
  matrix products: 29.2 us -> 19.8 us
    all_gather x4 -> x0, waiting for transfers between devices: 199 us -> none  [the longest x1 114 us: shards(): full_up = lax.all_gather(up_weight, 'dp', axis=0, tiled=True)]
    ppermute x0 -> x43, waiting for transfers between devices: none -> 116 us  [the longest x41 116 us: flip(): return lax.ppermute(arr, axis, [(i, i ^ mask) for i in range(size)])]
    psum x1 -> x0, waiting for transfers between devices: 110 us -> none  [shards(): up_sum = lax.psum(up_partial, ('dp', 'tensor'))]
    psum x3 -> x0, blocking collectives: 85.7 us -> none  [the longest x1 38.6 us: shards(): lax.psum(down_partial.astype(jnp.bfloat16), 'dp').astype(jnp.float32)]
    ppermute x0 -> x43, starting transfers between devices: none -> 56.4 us  [the longest x41 52.3 us: flip(): return lax.ppermute(arr, axis, [(i, i ^ mask) for i in range(size)])]
    dot_general x13 -> x24, matrix products: 27.9 us -> 19.4 us  [dot(): lax.dot_general(a, b, (dims, ((), ())), preferred_element_type=F32, preci...]
    another operation x10 -> x18, other arithmetic: 13.4 us -> 21 us  [the longest x6 7.9 us: inverse_factor(): lower = jnp.linalg.cholesky(gram)]
  transfers between devices with their start and end apart: 6 -> 43, of which waited for: 5 -> 20; matrix products, arithmetic and copies ran while one was open for 8% -> 21% of each run, Pallas kernels for 0% -> 0%
where the time goes in v1:
time: 227 us; the launch traced here: 226 us
  waiting for transfers between devices  116 us (51%)
  starting transfers between devices  56.4 us (25%)
  other arithmetic  26.5 us (12%)
  matrix products  19.8 us (9%)
  local copies, waits for them, and re-layouts  5.62 us (2%)
    ppermute x41, waiting for transfers between devices, flip(): return lax.ppermute(arr, axis, [(i, i ^ mask) for i in range(size)])  116 us
    ppermute x41, starting transfers between devices, flip(): return lax.ppermute(arr, axis, [(i, i ^ mask) for i in range(size)])  52.3 us
    dot_general x24, matrix products, dot(): lax.dot_general(a, b, (dims, ((), ())), preferred_element_type=F32, preci...  19.4 us
    another operation x6, other arithmetic, inverse_factor(): lower = jnp.linalg.cholesky(gram)  7.9 us
    another operation x4, other arithmetic, inverse_factor(): lax.linalg.triangular_solve(lower, jnp.eye(gram.shape[0], dtype=F32), lef...  7.49 us
  transfers between devices with their start and end apart: 43, of which 20 were waited for; matrix products, arithmetic and copies ran while one was open for 21% of the time, Pallas kernels for 0%

profile of v1, /device:TPU:0, one launch (start us, length us, event | category | flops | bytes accessed | tf_op | source)
XLA Modules:
  0.0 226.0 jit_solution(488767117492028215)
XLA Ops:
  3.4 3.0 %collective-permute-start.10 = (bf16[2,128,512]{2,1,0:T(8,128)(2,1)S(1)}, bf16[2,128,512]{2,1,0:T(8,128)(2,1)S(1)}, u32[]{:S(2)}, u32[]{:S(2)}) collective-permute-start(bf16[2,128,512]{2,1,0:T(8,128)(2,1)S(1)} %pad_maximum_fusion.7), channel_id=1, source_target_pairs={{0,2},{1,3},{2,0},{3,1},{4,6},{5,7},{6,4},{7,5},{8,10},{9,11},{10,... | collective-permute-start | bytes 786440 | tf_op jit(solution)/shard_map/ppermute | solution.py:15
  7.4 6.1 %collective-permute-done.10 = bf16[2,128,512]{2,1,0:T(8,128)(2,1)S(1)} collective-permute-done((bf16[2,128,512]{2,1,0:T(8,128)(2,1)S(1)}, bf16[2,128,512]{2,1,0:T(8,128)(2,1)S(1)}, u32[]{:S(2)}, u32[]{:S(2)}) %collective-permute-start.10) | collective-permute-done | bytes 262176 | tf_op jit(solution)/shard_map/ppermute | solution.py:15
  13.6 4.2 %collective-permute-start.13 = (bf16[128,512]{1,0:T(8,128)(2,1)S(1)}, bf16[128,512]{1,0:T(8,128)(2,1)S(1)}, u32[]{:S(2)}, u32[]{:S(2)}) collective-permute-start(bf16[128,512]{1,0:T(8,128)(2,1)S(1)} %get-tuple-element.30), channel_id=1, source_target_pairs={{0,24},{4,28},{8,16},{12,20},{16,8},{20,12},{24,0},{28,4},{1,25},{... | collective-permute-start | bytes 393224 | tf_op jit(solution)/shard_map/ppermute | solution.py:15
  18.6 3.9 %collective-permute-start.4 = (bf16[128,512]{1,0:T(8,128)(2,1)S(1)}, bf16[128,512]{1,0:T(8,128)(2,1)S(1)}, u32[]{:S(2)}, u32[]{:S(2)}) collective-permute-start(bf16[128,512]{1,0:T(8,128)(2,1)S(1)} %get-tuple-element.42), channel_id=1, source_target_pairs={{0,24},{4,28},{8,16},{12,20},{16,8},{20,12},{24,0},{28,4},{1,25},{... | collective-permute-start | bytes 393224 | tf_op jit(solution)/shard_map/ppermute | solution.py:15
  22.5 7.2 %collective-permute-start.2 = (bf16[128,512]{1,0:T(8,128)(2,1)S(1)}, bf16[128,512]{1,0:T(8,128)(2,1)S(1)}, u32[]{:S(2)}, u32[]{:S(2)}) collective-permute-start(bf16[128,512]{1,0:T(8,128)(2,1)S(1)} %get-tuple-element.44), channel_id=1, source_target_pairs={{0,8},{4,12},{8,0},{12,4},{16,24},{20,28},{24,16},{28,20},{1,9},{5... | collective-permute-start | bytes 393224 | tf_op jit(solution)/shard_map/ppermute | solution.py:15
  30.5 3.4 %collective-permute-done.12 = bf16[128,512]{1,0:T(8,128)(2,1)S(1)} collective-permute-done((bf16[128,512]{1,0:T(8,128)(2,1)S(1)}, bf16[128,512]{1,0:T(8,128)(2,1)S(1)}, u32[]{:S(2)}, u32[]{:S(2)}) %collective-permute-start.12) | collective-permute-done | bytes 131104 | tf_op jit(solution)/shard_map/ppermute | solution.py:15
  34.9 3.7 %collective-permute-done.3 = bf16[128,512]{1,0:T(8,128)(2,1)S(1)} collective-permute-done((bf16[128,512]{1,0:T(8,128)(2,1)S(1)}, bf16[128,512]{1,0:T(8,128)(2,1)S(1)}, u32[]{:S(2)}, u32[]{:S(2)}) %collective-permute-start.3) | collective-permute-done | bytes 131104 | tf_op jit(solution)/shard_map/ppermute | solution.py:15
  40.9 2.4 %collective-permute-start.25 = (bf16[2,128,256]{2,1,0:T(8,128)(2,1)}, bf16[2,128,256]{2,1,0:T(8,128)(2,1)S(1)}, u32[]{:S(2)}, u32[]{:S(2)}) collective-permute-start(bf16[2,128,256]{2,1,0:T(8,128)(2,1)} %maximum_select_fusion), channel_id=1, source_target_pairs={{0,1},{4,5},{8,9},{12,13},{16,17},{20,21},{24,25},{28,29}} | collective-permute-start | bytes 393224 | tf_op jit(solution)/shard_map/ppermute | solution.py:35
  43.4 1.6 collective-permute-start.15
  45.5 1.7 collective-permute-start.26
  47.2 1.6 broadcast_select_fusion
  49.4 35.5 %collective-permute-done.6 = bf16[896,512]{1,0:T(8,128)(2,1)} collective-permute-done((bf16[896,512]{1,0:T(8,128)(2,1)S(1)}, bf16[896,512]{1,0:T(8,128)(2,1)}, u32[]{:S(2)}, u32[]{:S(2)}) %collective-permute-start.6) | collective-permute-done | bytes 917536 | tf_op jit(solution)/shard_map/ppermute | solution.py:15
  84.8 1.6 fusion.7
  87.6 2.1 collective-permute-start.16
  90.1 1.6 convolution_add_fusion.3
  92.7 9.8 %collective-permute-done.7 = bf16[2,128,896]{2,1,0:T(8,128)(2,1)S(1)} collective-permute-done((bf16[2,128,896]{2,1,0:T(8,128)(2,1)S(1)}, bf16[2,128,896]{2,1,0:T(8,128)(2,1)S(1)}, u32[]{:S(2)}, u32[]{:S(2)}) %collective-permute-start.7) | collective-permute-done | bytes 458784 | tf_op jit(solution)/shard_map/ppermute | solution.py:15
  103.2 8.2 %collective-permute-done.16 = bf16[2,128,896]{2,1,0:T(8,128)(2,1)S(1)} collective-permute-done((bf16[2,128,896]{2,1,0:T(8,128)(2,1)S(1)}, bf16[2,128,896]{2,1,0:T(8,128)(2,1)S(1)}, u32[]{:S(2)}, u32[]{:S(2)}) %collective-permute-start.16) | collective-permute-done | bytes 458784 | tf_op jit(solution)/shard_map/ppermute | solution.py:15
  111.7 7.7 %collective-permute-done.8 = bf16[1,128,896]{2,1,0:T(8,128)(2,1)S(1)} collective-permute-done((bf16[1,128,896]{2,1,0:T(8,128)(2,1)S(1)}, bf16[1,128,896]{2,1,0:T(8,128)(2,1)S(1)}, u32[]{:S(2)}, u32[]{:S(2)}) %collective-permute-start.8) | collective-permute-done | bytes 229408 | tf_op jit(solution)/shard_map/ppermute | solution.py:15
  119.4 4.2 %collective-permute-done.17 = bf16[1,128,896]{2,1,0:T(8,128)(2,1)S(1)} collective-permute-done((bf16[1,128,896]{2,1,0:T(8,128)(2,1)S(1)}, bf16[1,128,896]{2,1,0:T(8,128)(2,1)S(1)}, u32[]{:S(2)}, u32[]{:S(2)}) %collective-permute-start.17) | collective-permute-done | bytes 229408 | tf_op jit(solution)/shard_map/ppermute | solution.py:15
  126.4 2.9 %collective-permute-start.28 = (f32[256,32]{0,1:T(8,128)S(1)}, f32[256,32]{0,1:T(8,128)S(1)}, u32[]{:S(2)}, u32[]{:S(2)}) collective-permute-start(f32[256,32]{0,1:T(8,128)S(1)} %add.165), channel_id=1, source_target_pairs={{0,2},{1,3},{2,0},{3,1},{4,6},{5,7},{6,4},{7,5},{8,10},{9,11},{10,... | collective-permute-start | bytes 98312 | tf_op jit(solution)/shard_map/ppermute | solution.py:15
  129.3 1.9 collective-permute-done.28
  131.2 1.6 collective-permute-start.29
  133.1 2.1 collective-permute-done.29
  136.4 1.6 collective-permute-start.35
  137.9 2.8 %collective-permute-done.30 = f32[256,32]{0,1:T(8,128)S(1)} collective-permute-done((f32[256,32]{0,1:T(8,128)S(1)}, f32[256,32]{0,1:T(8,128)S(1)}, u32[]{:S(2)}, u32[]{:S(2)}) %collective-permute-start.30) | collective-permute-done | bytes 32800 | tf_op jit(solution)/shard_map/ppermute | solution.py:15
  142.0 2.5 %collective-permute-start.36 = (f32[896,32]{0,1:T(8,128)S(1)}, f32[896,32]{0,1:T(8,128)S(1)}, u32[]{:S(2)}, u32[]{:S(2)}) collective-permute-start(f32[896,32]{0,1:T(8,128)S(1)} %add.174), channel_id=1, source_target_pairs={{0,8},{4,12},{8,0},{12,4},{16,24},{20,28},{24,16},{28,20},{1,9},{5... | collective-permute-start | bytes 344072 | tf_op jit(solution)/shard_map/ppermute | solution.py:15
  146.4 2.9 %cholesky.44 = f32[32,32]{1,0:T(8,128)S(1)} custom-call(f32[32,32]{1,0:T(8,128)S(1)} %fusion.66), custom_call_target="Cholesky" | custom-call | tf_op jit(solution)/shard_map/jit(cholesky)/cholesky | solution.py:40
  150.7 2.4 %custom-call.6 = f32[1,32,32]{1,2,0:T(8,128)S(1)} custom-call(f32[1,32,32]{2,1,0:T(8,128)S(1)} %fusion.61), custom_call_target="InvertDiagBlocksLowerTriangular" | custom-call | tf_op jit(solution)/shard_map/triangular_solve/custom-call.0 | solution.py:41
  153.1 1.5 collective-permute-start.32
  155.0 1.8 pad_maximum_fusion.5
  156.8 2.5 %collective-permute-start.19 = (bf16[2,128,896]{2,1,0:T(8,128)(2,1)}, bf16[2,128,896]{2,1,0:T(8,128)(2,1)}, u32[]{:S(2)}, u32[]{:S(2)}) collective-permute-start(bf16[2,128,896]{2,1,0:T(8,128)(2,1)} %pad_maximum_fusion.5), channel_id=1, source_target_pairs={{0,8},{4,12},{8,0},{12,4},{16,24},{20,28},{24,16},{28,20},{1,9},{5... | collective-permute-start | bytes 1376264 | tf_op jit(solution)/shard_map/ppermute | solution.py:15
  159.2 2.1 collective-permute-done.37
  163.6 2.3 %collective-permute-start.39 = (f32[288,32]{0,1:T(8,128)S(1)}, f32[288,32]{0,1:T(8,128)S(1)}, u32[]{:S(2)}, u32[]{:S(2)}) collective-permute-start(f32[288,32]{0,1:T(8,128)S(1)} %fusion.78), channel_id=1, source_target_pairs={{0,2},{1,3},{2,0},{3,1},{4,6},{5,7},{6,4},{7,5},{8,10},{9,11},{10,... | collective-permute-start | bytes 110600 | tf_op jit(solution)/shard_map/ppermute | solution.py:15
  166.0 4.0 %collective-permute-done.33 = f32[896,32]{0,1:T(8,128)S(1)} collective-permute-done((f32[896,32]{0,1:T(8,128)S(1)}, f32[896,32]{0,1:T(8,128)S(1)}, u32[]{:S(2)}, u32[]{:S(2)}) %collective-permute-start.33) | collective-permute-done | bytes 114720 | tf_op jit(solution)/shard_map/ppermute | solution.py:15
  170.1 1.7 collective-permute-start.34
  174.6 2.5 %convolution_convert_fusion = bf16[512,512]{1,0:T(8,128)(2,1)} fusion(bf16[512,896]{1,0:T(8,128)(2,1)S(1)} %copy-done.4, bf16[512,896]{1,0:T(8,128)(2,1)S(1)} %copy-done.2, pred[]{:T(512)S(6)} %eq.14, bf16[128,896]{1,0:T(8,128)(2,1)S(1)} %get-tuple-element.46, bf16[128,896]{1,0:T(8,128)(2,1)} %bitcast.39, bf16[128,896]{1,0:T(8,128)(2,1)S(1)} %get-tuple-element.45, ...), kind=kOutput, calls=%fused_computation.12 | convolution fusion | flops 474152960 | bytes 3276801 | tf_op jit(solution)/shard_map/dot_general | solution.py:23
  178.4 3.6 %cholesky.55 = f32[32,32]{1,0:T(8,128)S(1)} custom-call(f32[32,32]{1,0:T(8,128)} %fusion.64), custom_call_target="Cholesky" | custom-call | tf_op jit(solution)/shard_map/jit(cholesky)/cholesky | solution.py:40
  182.7 1.3 fusion.62
  183.9 3.2 %custom-call.7 = f32[1,32,32]{1,2,0:T(8,128)S(1)} custom-call(f32[1,32,32]{2,1,0:T(8,128)} %fusion.62), custom_call_target="InvertDiagBlocksLowerTriangular" | custom-call | tf_op jit(solution)/shard_map/triangular_solve/custom-call.0 | solution.py:41
  187.6 2.1 fusion.6
  192.2 6.7 %collective-permute-done.21 = bf16[2,1,128,512]{3,2,0,1:T(8,128)(2,1)S(1)} collective-permute-done((bf16[2,1,128,512]{3,2,0,1:T(8,128)(2,1)S(1)}, bf16[2,1,128,512]{3,2,0,1:T(8,128)(2,1)S(1)}, u32[]{:S(2)}, u32[]{:S(2)}) %collective-permute-start.21) | collective-permute-done | bytes 262176 | tf_op jit(solution)/shard_map/ppermute | solution.py:15
  199.1 1.3 collective-permute-start.22
  200.9 1.7 collective-permute-start.42
  202.8 11.1 %collective-permute-done.22 = bf16[1,2,128,512]{3,2,1,0:T(8,128)(2,1)S(1)} collective-permute-done((bf16[1,2,128,512]{3,2,1,0:T(8,128)(2,1)S(1)}, bf16[1,2,128,512]{3,2,1,0:T(8,128)(2,1)S(1)}, u32[]{:S(2)}, u32[]{:S(2)}) %collective-permute-start.22) | collective-permute-done | bytes 262176 | tf_op jit(solution)/shard_map/ppermute | solution.py:15
  214.2 3.8 %collective-permute-start.23 = (bf16[2,128,512]{2,1,0:T(8,128)(2,1)S(1)}, bf16[2,128,512]{2,1,0:T(8,128)(2,1)S(1)}, u32[]{:S(2)}, u32[]{:S(2)}) collective-permute-start(bf16[2,128,512]{2,1,0:T(8,128)(2,1)S(1)} %pad_maximum_fusion.8), channel_id=1, source_target_pairs={{0,2},{1,3},{2,0},{3,1},{4,6},{5,7},{6,4},{7,5},{8,10},{9,11},{10,... | collective-permute-start | bytes 786440 | tf_op jit(solution)/shard_map/ppermute | solution.py:15
  218.0 1.9 fusion.2
  220.1 3.1 %collective-permute-done.23 = bf16[2,128,512]{2,1,0:T(8,128)(2,1)S(1)} collective-permute-done((bf16[2,128,512]{2,1,0:T(8,128)(2,1)S(1)}, bf16[2,128,512]{2,1,0:T(8,128)(2,1)S(1)}, u32[]{:S(2)}, u32[]{:S(2)}) %collective-permute-start.23) | collective-permute-done | bytes 262176 | tf_op jit(solution)/shard_map/ppermute | solution.py:15
  223.4 1.9 fusion
  (172 shorter events, 34.3 us)
Async XLA Ops:
  0.6 123.5 %copy-start = (f32[896,32]{0,1:T(8,128)S(1)}, f32[896,32]{0,1:T(8,128)}, u32[]{:S(2)}) copy-start(f32[896,32]{0,1:T(8,128)} %param.17) | copy-start | bytes 344068
  1.7 1.6 collective-permute-start.9
  3.2 3.2 %collective-permute-start = (bf16[128,512]{1,0:T(8,128)(2,1)S(1)}, bf16[128,512]{1,0:T(8,128)(2,1)S(1)}, u32[]{:S(2)}, u32[]{:S(2)}) collective-permute-start(bf16[128,512]{1,0:T(8,128)(2,1)S(1)} %get-tuple-element.52), channel_id=1, source_target_pairs={{0,1},{1,0},{2,3},{3,2},{4,5},{5,4},{6,7},{7,6},{8,9},{9,8},{10,11... | collective-permute-start | bytes 393224 | tf_op jit(solution)/shard_map/ppermute | solution.py:15
  3.4 10.1 %collective-permute-start.10 = (bf16[2,128,512]{2,1,0:T(8,128)(2,1)S(1)}, bf16[2,128,512]{2,1,0:T(8,128)(2,1)S(1)}, u32[]{:S(2)}, u32[]{:S(2)}) collective-permute-start(bf16[2,128,512]{2,1,0:T(8,128)(2,1)S(1)} %pad_maximum_fusion.7), channel_id=1, source_target_pairs={{0,2},{1,3},{2,0},{3,1},{4,6},{5,7},{6,4},{7,5},{8,10},{9,11},{10,... | collective-permute-start | bytes 786440 | tf_op jit(solution)/shard_map/ppermute | solution.py:15
  6.4 12.1 %collective-permute-start.1 = (bf16[2,128,512]{2,1,0:T(8,128)(2,1)S(1)}, bf16[2,128,512]{2,1,0:T(8,128)(2,1)S(1)}, u32[]{:S(2)}, u32[]{:S(2)}) collective-permute-start(bf16[2,128,512]{2,1,0:T(8,128)(2,1)S(1)} %pad_maximum_fusion.6), channel_id=1, source_target_pairs={{0,2},{1,3},{2,0},{3,1},{4,6},{5,7},{6,4},{7,5},{8,10},{9,11},{10,... | collective-permute-start | bytes 786440 | tf_op jit(solution)/shard_map/ppermute | solution.py:15
  13.6 8.9 %collective-permute-start.13 = (bf16[128,512]{1,0:T(8,128)(2,1)S(1)}, bf16[128,512]{1,0:T(8,128)(2,1)S(1)}, u32[]{:S(2)}, u32[]{:S(2)}) collective-permute-start(bf16[128,512]{1,0:T(8,128)(2,1)S(1)} %get-tuple-element.30), channel_id=1, source_target_pairs={{0,24},{4,28},{8,16},{12,20},{16,8},{20,12},{24,0},{28,4},{1,25},{... | collective-permute-start | bytes 393224 | tf_op jit(solution)/shard_map/ppermute | solution.py:15
  17.8 16.1 %collective-permute-start.12 = (bf16[128,512]{1,0:T(8,128)(2,1)S(1)}, bf16[128,512]{1,0:T(8,128)(2,1)S(1)}, u32[]{:S(2)}, u32[]{:S(2)}) collective-permute-start(bf16[128,512]{1,0:T(8,128)(2,1)S(1)} %get-tuple-element.31), channel_id=1, source_target_pairs={{0,16},{4,20},{8,24},{12,28},{16,0},{20,4},{24,8},{28,12},{1,17},{... | collective-permute-start | bytes 393224 | tf_op jit(solution)/shard_map/ppermute | solution.py:15
  17.8 16.1 %collective-permute-start.11 = (bf16[128,512]{1,0:T(8,128)(2,1)S(1)}, bf16[128,512]{1,0:T(8,128)(2,1)S(1)}, u32[]{:S(2)}, u32[]{:S(2)}) collective-permute-start(bf16[128,512]{1,0:T(8,128)(2,1)S(1)} %get-tuple-element.32), channel_id=1, source_target_pairs={{0,8},{4,12},{8,0},{12,4},{16,24},{20,28},{24,16},{28,20},{1,9},{5... | collective-permute-start | bytes 393224 | tf_op jit(solution)/shard_map/ppermute | solution.py:15
  18.6 16.2 %collective-permute-start.4 = (bf16[128,512]{1,0:T(8,128)(2,1)S(1)}, bf16[128,512]{1,0:T(8,128)(2,1)S(1)}, u32[]{:S(2)}, u32[]{:S(2)}) collective-permute-start(bf16[128,512]{1,0:T(8,128)(2,1)S(1)} %get-tuple-element.42), channel_id=1, source_target_pairs={{0,24},{4,28},{8,16},{12,20},{16,8},{20,12},{24,0},{28,4},{1,25},{... | collective-permute-start | bytes 393224 | tf_op jit(solution)/shard_map/ppermute | solution.py:15
  22.5 16.0 %collective-permute-start.3 = (bf16[128,512]{1,0:T(8,128)(2,1)S(1)}, bf16[128,512]{1,0:T(8,128)(2,1)S(1)}, u32[]{:S(2)}, u32[]{:S(2)}) collective-permute-start(bf16[128,512]{1,0:T(8,128)(2,1)S(1)} %get-tuple-element.43), channel_id=1, source_target_pairs={{0,16},{4,20},{8,24},{12,28},{16,0},{20,4},{24,8},{28,12},{1,17},{... | collective-permute-start | bytes 393224 | tf_op jit(solution)/shard_map/ppermute | solution.py:15
  22.5 16.0 %collective-permute-start.2 = (bf16[128,512]{1,0:T(8,128)(2,1)S(1)}, bf16[128,512]{1,0:T(8,128)(2,1)S(1)}, u32[]{:S(2)}, u32[]{:S(2)}) collective-permute-start(bf16[128,512]{1,0:T(8,128)(2,1)S(1)} %get-tuple-element.44), channel_id=1, source_target_pairs={{0,8},{4,12},{8,0},{12,4},{16,24},{20,28},{24,16},{28,20},{1,9},{5... | collective-permute-start | bytes 393224 | tf_op jit(solution)/shard_map/ppermute | solution.py:15
  34.8 12.3 %collective-permute-start.14 = (bf16[4,128,512]{2,1,0:T(8,128)(2,1)}, bf16[4,128,512]{2,1,0:T(8,128)(2,1)}, u32[]{:S(2)}, u32[]{:S(2)}) collective-permute-start(bf16[4,128,512]{2,1,0:T(8,128)(2,1)} %pad_maximum_fusion.4), channel_id=1, source_target_pairs={{0,1},{1,0},{2,3},{3,2},{4,5},{5,4},{6,7},{7,6},{8,9},{9,8},{10,11... | collective-permute-start | bytes 1572872 | tf_op jit(solution)/shard_map/ppermute | solution.py:15
  39.4 7.8 %collective-permute-start.5 = (bf16[4,128,512]{2,1,0:T(8,128)(2,1)}, bf16[4,128,512]{2,1,0:T(8,128)(2,1)}, u32[]{:S(2)}, u32[]{:S(2)}) collective-permute-start(bf16[4,128,512]{2,1,0:T(8,128)(2,1)} %pad_maximum_fusion.2), channel_id=1, source_target_pairs={{0,1},{1,0},{2,3},{3,2},{4,5},{5,4},{6,7},{7,6},{8,9},{9,8},{10,11... | collective-permute-start | bytes 1572872 | tf_op jit(solution)/shard_map/ppermute | solution.py:15
  40.9 4.5 %collective-permute-start.25 = (bf16[2,128,256]{2,1,0:T(8,128)(2,1)}, bf16[2,128,256]{2,1,0:T(8,128)(2,1)S(1)}, u32[]{:S(2)}, u32[]{:S(2)}) collective-permute-start(bf16[2,128,256]{2,1,0:T(8,128)(2,1)} %maximum_select_fusion), channel_id=1, source_target_pairs={{0,1},{4,5},{8,9},{12,13},{16,17},{20,21},{24,25},{28,29}} | collective-permute-start | bytes 393224 | tf_op jit(solution)/shard_map/ppermute | solution.py:35
  43.4 43.7 %collective-permute-start.15 = (bf16[512,896]{1,0:T(8,128)(2,1)S(1)}, bf16[512,896]{1,0:T(8,128)(2,1)S(1)}, u32[]{:S(2)}, u32[]{:S(2)}) collective-permute-start(bf16[512,896]{1,0:T(8,128)(2,1)S(1)} %copy-done.2), channel_id=1, source_target_pairs={{0,4},{4,0},{8,12},{12,8},{16,20},{20,16},{24,28},{28,24},{1,5},{5... | collective-permute-start | bytes 2752520 | tf_op jit(solution)/shard_map/ppermute | solution.py:15
  44.9 39.9 %collective-permute-start.6 = (bf16[896,512]{1,0:T(8,128)(2,1)S(1)}, bf16[896,512]{1,0:T(8,128)(2,1)}, u32[]{:S(2)}, u32[]{:S(2)}) collective-permute-start(bf16[896,512]{1,0:T(8,128)(2,1)S(1)} %copy-done.1), channel_id=1, source_target_pairs={{0,4},{4,0},{8,12},{12,8},{16,20},{20,16},{24,28},{28,24},{1,5},{5... | collective-permute-start | bytes 2752520 | tf_op jit(solution)/shard_map/ppermute | solution.py:15
  45.5 66.1 %collective-permute-start.26 = (bf16[2,128,256]{2,1,0:T(8,128)(2,1)S(1)}, bf16[2,128,256]{2,1,0:T(8,128)(2,1)S(1)}, u32[]{:S(2)}, u32[]{:S(2)}) collective-permute-start(bf16[2,128,256]{2,1,0:T(8,128)(2,1)S(1)} %fusion.117), channel_id=1, source_target_pairs={{0,2},{1,3},{4,6},{5,7},{8,10},{9,11},{12,14},{13,15},{16,18},{17,... | collective-permute-start | bytes 393224 | tf_op jit(solution)/shard_map/ppermute | solution.py:35
  86.5 16.0 %collective-permute-start.7 = (bf16[2,128,896]{2,1,0:T(8,128)(2,1)S(1)}, bf16[2,128,896]{2,1,0:T(8,128)(2,1)S(1)}, u32[]{:S(2)}, u32[]{:S(2)}) collective-permute-start(bf16[2,128,896]{2,1,0:T(8,128)(2,1)S(1)} %bitcast.212), channel_id=1, source_target_pairs={{0,8},{4,12},{8,0},{12,4},{16,24},{20,28},{24,16},{28,20},{1,9},{5... | collective-permute-start | bytes 1376264 | tf_op jit(solution)/shard_map/ppermute | solution.py:15
  87.6 23.8 %collective-permute-start.16 = (bf16[2,128,896]{2,1,0:T(8,128)(2,1)S(1)}, bf16[2,128,896]{2,1,0:T(8,128)(2,1)S(1)}, u32[]{:S(2)}, u32[]{:S(2)}) collective-permute-start(bf16[2,128,896]{2,1,0:T(8,128)(2,1)S(1)} %bitcast.213), channel_id=1, source_target_pairs={{0,8},{4,12},{8,0},{12,4},{16,24},{20,28},{24,16},{28,20},{1,9},{5... | collective-permute-start | bytes 1376264 | tf_op jit(solution)/shard_map/ppermute | solution.py:15
  102.6 16.8 %collective-permute-start.8 = (bf16[1,128,896]{2,1,0:T(8,128)(2,1)S(1)}, bf16[1,128,896]{2,1,0:T(8,128)(2,1)S(1)}, u32[]{:S(2)}, u32[]{:S(2)}) collective-permute-start(bf16[1,128,896]{2,1,0:T(8,128)(2,1)S(1)} %slice.257), channel_id=1, source_target_pairs={{0,16},{4,20},{8,24},{12,28},{16,0},{20,4},{24,8},{28,12},{1,17},{... | collective-permute-start | bytes 688136 | tf_op jit(solution)/shard_map/ppermute | solution.py:15
  111.5 12.1 %collective-permute-start.17 = (bf16[1,128,896]{2,1,0:T(8,128)(2,1)S(1)}, bf16[1,128,896]{2,1,0:T(8,128)(2,1)S(1)}, u32[]{:S(2)}, u32[]{:S(2)}) collective-permute-start(bf16[1,128,896]{2,1,0:T(8,128)(2,1)S(1)} %slice.256), channel_id=1, source_target_pairs={{0,16},{4,20},{8,24},{12,28},{16,0},{20,4},{24,8},{28,12},{1,17},{... | collective-permute-start | bytes 688136 | tf_op jit(solution)/shard_map/ppermute | solution.py:15
  111.7 12.2 %copy-start.5 = (f32[1,256,896]{2,1,0:T(8,128)S(1)}, f32[1,256,896]{2,1,0:T(8,128)}, u32[]{:S(2)}) copy-start(f32[1,256,896]{2,1,0:T(8,128)} %param.15) | copy-start | bytes 2752516
  125.1 1.3 collective-permute-start.27
  126.4 4.8 %collective-permute-start.28 = (f32[256,32]{0,1:T(8,128)S(1)}, f32[256,32]{0,1:T(8,128)S(1)}, u32[]{:S(2)}, u32[]{:S(2)}) collective-permute-start(f32[256,32]{0,1:T(8,128)S(1)} %add.165), channel_id=1, source_target_pairs={{0,2},{1,3},{2,0},{3,1},{4,6},{5,7},{6,4},{7,5},{8,10},{9,11},{10,... | collective-permute-start | bytes 98312 | tf_op jit(solution)/shard_map/ppermute | solution.py:15
  129.3 25.8 %collective-permute-start.18 = (bf16[1,128,896]{2,1,0:T(8,128)(2,1)S(1)}, bf16[1,128,896]{2,1,0:T(8,128)(2,1)}, u32[]{:S(2)}, u32[]{:S(2)}) collective-permute-start(bf16[1,128,896]{2,1,0:T(8,128)(2,1)S(1)} %multiply_convert_fusion.1), channel_id=1, source_target_pairs={{0,16},{4,20},{8,24},{12,28},{16,0},{20,4},{24,8},{28,12},{1,17},{... | collective-permute-start | bytes 688136 | tf_op jit(solution)/shard_map/ppermute | solution.py:15
  131.2 4.0 %collective-permute-start.29 = (f32[256,32]{0,1:T(8,128)S(1)}, f32[256,32]{0,1:T(8,128)S(1)}, u32[]{:S(2)}, u32[]{:S(2)}) collective-permute-start(f32[256,32]{0,1:T(8,128)S(1)} %add.166), channel_id=1, source_target_pairs={{0,4},{4,0},{8,12},{12,8},{16,20},{20,16},{24,28},{28,24},{1,5},{5... | collective-permute-start | bytes 98312 | tf_op jit(solution)/shard_map/ppermute | solution.py:15
  135.1 5.6 %collective-permute-start.30 = (f32[256,32]{0,1:T(8,128)S(1)}, f32[256,32]{0,1:T(8,128)S(1)}, u32[]{:S(2)}, u32[]{:S(2)}) collective-permute-start(f32[256,32]{0,1:T(8,128)S(1)} %add.167), channel_id=1, source_target_pairs={{0,8},{4,12},{8,0},{12,4},{16,24},{20,28},{24,16},{28,20},{1,9},{5... | collective-permute-start | bytes 98312 | tf_op jit(solution)/shard_map/ppermute | solution.py:15
  136.4 5.6 %collective-permute-start.35 = (f32[896,32]{0,1:T(8,128)S(1)}, f32[896,32]{0,1:T(8,128)S(1)}, u32[]{:S(2)}, u32[]{:S(2)}) collective-permute-start(f32[896,32]{0,1:T(8,128)S(1)} %fusion.83), channel_id=1, source_target_pairs={{0,4},{4,0},{8,12},{12,8},{16,20},{20,16},{24,28},{28,24},{1,5},{5... | collective-permute-start | bytes 344072 | tf_op jit(solution)/shard_map/ppermute | solution.py:15
  140.7 4.8 %collective-permute-start.31 = (f32[256,32]{0,1:T(8,128)S(1)}, f32[256,32]{0,1:T(8,128)S(1)}, u32[]{:S(2)}, u32[]{:S(2)}) collective-permute-start(f32[256,32]{0,1:T(8,128)S(1)} %add.168), channel_id=1, source_target_pairs={{0,16},{4,20},{8,24},{12,28},{16,0},{20,4},{24,8},{28,12},{1,17},{... | collective-permute-start | bytes 98312 | tf_op jit(solution)/shard_map/ppermute | solution.py:15
  142.0 12.7 %collective-permute-start.36 = (f32[896,32]{0,1:T(8,128)S(1)}, f32[896,32]{0,1:T(8,128)S(1)}, u32[]{:S(2)}, u32[]{:S(2)}) collective-permute-start(f32[896,32]{0,1:T(8,128)S(1)} %add.174), channel_id=1, source_target_pairs={{0,8},{4,12},{8,0},{12,4},{16,24},{20,28},{24,16},{28,20},{1,9},{5... | collective-permute-start | bytes 344072 | tf_op jit(solution)/shard_map/ppermute | solution.py:15
  153.1 9.4 %collective-permute-start.32 = (f32[896,32]{0,1:T(8,128)S(1)}, f32[896,32]{0,1:T(8,128)S(1)}, u32[]{:S(2)}, u32[]{:S(2)}) collective-permute-start(f32[896,32]{0,1:T(8,128)S(1)} %fusion.82), channel_id=1, source_target_pairs={{0,4},{4,0},{8,12},{12,8},{16,20},{20,16},{24,28},{28,24},{1,5},{5... | collective-permute-start | bytes 344072 | tf_op jit(solution)/shard_map/ppermute | solution.py:15
  154.7 6.7 %collective-permute-start.37 = (f32[896,32]{0,1:T(8,128)S(1)}, f32[896,32]{0,1:T(8,128)S(1)}, u32[]{:S(2)}, u32[]{:S(2)}) collective-permute-start(f32[896,32]{0,1:T(8,128)S(1)} %add.175), channel_id=1, source_target_pairs={{0,16},{4,20},{8,24},{12,28},{16,0},{20,4},{24,8},{28,12},{1,17},{... | collective-permute-start | bytes 344072 | tf_op jit(solution)/shard_map/ppermute | solution.py:15
  156.8 16.5 %collective-permute-start.19 = (bf16[2,128,896]{2,1,0:T(8,128)(2,1)}, bf16[2,128,896]{2,1,0:T(8,128)(2,1)}, u32[]{:S(2)}, u32[]{:S(2)}) collective-permute-start(bf16[2,128,896]{2,1,0:T(8,128)(2,1)} %pad_maximum_fusion.5), channel_id=1, source_target_pairs={{0,8},{4,12},{8,0},{12,4},{16,24},{20,28},{24,16},{28,20},{1,9},{5... | collective-permute-start | bytes 1376264 | tf_op jit(solution)/shard_map/ppermute | solution.py:15
  162.2 1.3 collective-permute-start.38
  162.6 7.5 %collective-permute-start.33 = (f32[896,32]{0,1:T(8,128)S(1)}, f32[896,32]{0,1:T(8,128)S(1)}, u32[]{:S(2)}, u32[]{:S(2)}) collective-permute-start(f32[896,32]{0,1:T(8,128)S(1)} %add.170), channel_id=1, source_target_pairs={{0,8},{4,12},{8,0},{12,4},{16,24},{20,28},{24,16},{28,20},{1,9},{5... | collective-permute-start | bytes 344072 | tf_op jit(solution)/shard_map/ppermute | solution.py:15
  163.6 8.3 %collective-permute-start.39 = (f32[288,32]{0,1:T(8,128)S(1)}, f32[288,32]{0,1:T(8,128)S(1)}, u32[]{:S(2)}, u32[]{:S(2)}) collective-permute-start(f32[288,32]{0,1:T(8,128)S(1)} %fusion.78), channel_id=1, source_target_pairs={{0,2},{1,3},{2,0},{3,1},{4,6},{5,7},{6,4},{7,5},{8,10},{9,11},{10,... | collective-permute-start | bytes 110600 | tf_op jit(solution)/shard_map/ppermute | solution.py:15
  166.0 52.0 %copy-start.17 = (f32[256,32]{0,1:T(8,128)}, f32[256,32]{0,1:T(8,128)S(1)}, u32[]{:S(2)}) copy-start(f32[256,32]{0,1:T(8,128)S(1)} %fusion.81) | copy-start | bytes 98308
  170.1 32.5 %collective-permute-start.34 = (f32[896,32]{0,1:T(8,128)S(1)}, f32[896,32]{0,1:T(8,128)S(1)}, u32[]{:S(2)}, u32[]{:S(2)}) collective-permute-start(f32[896,32]{0,1:T(8,128)S(1)} %add.171), channel_id=1, source_target_pairs={{0,16},{4,20},{8,24},{12,28},{16,0},{20,4},{24,8},{28,12},{1,17},{... | collective-permute-start | bytes 344072 | tf_op jit(solution)/shard_map/ppermute | solution.py:15
  177.1 10.5 %collective-permute-start.20 = (bf16[512,512]{1,0:T(8,128)(2,1)}, bf16[512,512]{1,0:T(8,128)(2,1)}, u32[]{:S(2)}, u32[]{:S(2)}) collective-permute-start(bf16[512,512]{1,0:T(8,128)(2,1)} %convolution_convert_fusion), channel_id=1, source_target_pairs={{0,1},{1,0},{2,3},{3,2},{4,5},{5,4},{6,7},{7,6},{8,9},{9,8},{10,11... | collective-permute-start | bytes 1572872 | tf_op jit(solution)/shard_map/ppermute | solution.py:15
  187.1 4.2 %collective-permute-start.40 = (f32[256,32]{0,1:T(8,128)}, f32[256,32]{0,1:T(8,128)S(1)}, u32[]{:S(2)}, u32[]{:S(2)}) collective-permute-start(f32[256,32]{0,1:T(8,128)} %slice.196), channel_id=1, source_target_pairs={{0,4},{4,0},{8,12},{12,8},{16,20},{20,16},{24,28},{28,24},{1,5},{5... | collective-permute-start | bytes 98312 | tf_op jit(solution)/shard_map/ppermute | solution.py:15
  189.8 9.1 %collective-permute-start.21 = (bf16[2,1,128,512]{3,2,0,1:T(8,128)(2,1)S(1)}, bf16[2,1,128,512]{3,2,0,1:T(8,128)(2,1)S(1)}, u32[]{:S(2)}, u32[]{:S(2)}) collective-permute-start(bf16[2,1,128,512]{3,2,0,1:T(8,128)(2,1)S(1)} %get-tuple-element.20), channel_id=1, source_target_pairs={{0,8},{4,12},{8,0},{12,4},{16,24},{20,28},{24,16},{28,20},{1,9},{5... | collective-permute-start | bytes 786440 | tf_op jit(solution)/shard_map/ppermute | solution.py:15
  191.2 9.6 %collective-permute-start.41 = (f32[256,32]{0,1:T(8,128)S(1)}, f32[256,32]{0,1:T(8,128)S(1)}, u32[]{:S(2)}, u32[]{:S(2)}) collective-permute-start(f32[256,32]{0,1:T(8,128)S(1)} %slice_add_fusion.3), channel_id=1, source_target_pairs={{0,8},{4,12},{8,0},{12,4},{16,24},{20,28},{24,16},{28,20},{1,9},{5... | collective-permute-start | bytes 98312 | tf_op jit(solution)/shard_map/ppermute | solution.py:15
  199.1 14.9 %collective-permute-start.22 = (bf16[1,2,128,512]{3,2,1,0:T(8,128)(2,1)S(1)}, bf16[1,2,128,512]{3,2,1,0:T(8,128)(2,1)S(1)}, u32[]{:S(2)}, u32[]{:S(2)}) collective-permute-start(bf16[1,2,128,512]{3,2,1,0:T(8,128)(2,1)S(1)} %get-tuple-element.17), channel_id=1, source_target_pairs={{0,16},{4,20},{8,24},{12,28},{16,0},{20,4},{24,8},{28,12},{1,17},{... | collective-permute-start | bytes 786440 | tf_op jit(solution)/shard_map/ppermute | solution.py:15
  200.8 22.5 %copy-start.11 = (f32[896,32]{0,1:T(8,128)}, f32[896,32]{0,1:T(8,128)S(1)}, u32[]{:S(2)}) copy-start(f32[896,32]{0,1:T(8,128)S(1)} %fusion.86) | copy-start | bytes 344068
  200.9 19.0 %collective-permute-start.42 = (f32[256,32]{0,1:T(8,128)S(1)}, f32[256,32]{0,1:T(8,128)S(1)}, u32[]{:S(2)}, u32[]{:S(2)}) collective-permute-start(f32[256,32]{0,1:T(8,128)S(1)} %add.180), channel_id=1, source_target_pairs={{0,16},{4,20},{8,24},{12,28},{16,0},{20,4},{24,8},{28,12},{1,17},{... | collective-permute-start | bytes 98312 | tf_op jit(solution)/shard_map/ppermute | solution.py:15
  202.8 17.1 %copy-start.12 = (f32[896,32]{0,1:T(8,128)}, f32[896,32]{0,1:T(8,128)S(1)}, u32[]{:S(2)}) copy-start(f32[896,32]{0,1:T(8,128)S(1)} %convolution_multiply_fusion.2) | copy-start | bytes 344068
  214.2 9.0 %collective-permute-start.23 = (bf16[2,128,512]{2,1,0:T(8,128)(2,1)S(1)}, bf16[2,128,512]{2,1,0:T(8,128)(2,1)S(1)}, u32[]{:S(2)}, u32[]{:S(2)}) collective-permute-start(bf16[2,128,512]{2,1,0:T(8,128)(2,1)S(1)} %pad_maximum_fusion.8), channel_id=1, source_target_pairs={{0,2},{1,3},{2,0},{3,1},{4,6},{5,7},{6,4},{7,5},{8,10},{9,11},{10,... | collective-permute-start | bytes 786440 | tf_op jit(solution)/shard_map/ppermute | solution.py:15
  223.3 1.9 collective-permute-start.24
  (15 other events, 83.0 us)

commit v2 on v1

v2 whole, which is shorter than its diff:
```python
import math

import jax
import jax.numpy as jnp
from jax import lax
from jax.sharding import PartitionSpec as P

BF = jnp.bfloat16
F32 = jnp.float32
HIGHEST = lax.Precision.HIGHEST


def flip(arr, axis, mask):
    size = lax.axis_size(axis)
    return lax.ppermute(arr, axis, [(i, i ^ mask) for i in range(size)])


def bits_of(size):
    return [1 << b for b in range(size.bit_length() - 1)]


def dot(a, b, dims=((1,), (0,)), precision=None):
    return lax.dot_general(a, b, (dims, ((), ())), preferred_element_type=F32, precision=precision)


def allsum(arr, axis, masks):
    for mask in masks:
        arr = arr + flip(arr, axis, mask)
    return arr


def broadcast_first(arr, axis):
    arr = jnp.where(lax.axis_index(axis) == 0, arr, jnp.zeros_like(arr))
    for mask in bits_of(lax.axis_size(axis)):
        arr = arr + lax.ppermute(arr, axis, [(i, i + mask) for i in range(mask)])
    return arr


def inverse_factor(gram):
    lower = jnp.linalg.cholesky(gram)
    return lax.linalg.triangular_solve(
        lower, jnp.eye(gram.shape[0], dtype=F32), left_side=False, lower=True, transpose_a=True
    )


def tie(*arrs):
    return lax.optimization_barrier(arrs)


def first_half(count):
    return (count // 2 + 127) // 128 * 128


def exchange_tensor(arr, half, tbits):
    width = arr.shape[1] // 2
    lo, hi = arr[:, :width], arr[:, width:]
    mine = jnp.where(half == 0, lo, hi)
    other = jnp.where(half == 0, hi, lo)
    blocks = [mine, flip(other, "tensor", 1)]
    for mask in tbits[1:]:
        got = flip(jnp.stack(blocks), "tensor", mask)
        blocks = blocks + [got[n] for n in range(len(blocks))]
    return jnp.stack(blocks)


def exchange_z(blocks, zrel):
    kept = []
    for k in range(blocks.shape[0]):
        piece = lax.dynamic_index_in_dim(blocks, zrel ^ k, 0, keepdims=False)
        kept.append(piece if k == 0 else flip(piece, "dp", 2 * k))
    return kept


def shards(tokens, out_grad, up_weight, down_weight, up_accum, down_accum, up_q, down_q):
    replicas, columns = lax.axis_size("dp"), lax.axis_size("tensor")
    dp_i, t_i = lax.axis_index("dp"), lax.axis_index("tensor")
    x_i, z_i = dp_i % 2, dp_i // 2
    core = t_i % 2
    zcount = replicas // 2
    zbits, tbits, dbits = bits_of(zcount), bits_of(columns), bits_of(replicas)
    rows, width = tokens.shape
    window = up_accum.shape[1]
    scale = 1.0 / math.sqrt(rows)
    half = core ^ x_i
    zrel = z_i ^ t_i

    ucut, dcut = first_half(up_weight.shape[0]), first_half(down_weight.shape[0])
    up_a = flip(up_weight[:ucut], "dp", 1)
    tok_blocks = exchange_tensor(tokens, half, tbits)
    grad_blocks = exchange_tensor(out_grad, half, tbits)
    tok_blocks, up_a = tie(tok_blocks, up_a)
    up_b_in, up_a = tie(up_weight[ucut:], up_a)
    up_b = flip(up_b_in, "dp", 1)
    tok_keep = exchange_z(tok_blocks, zrel)
    windows = broadcast_first(jnp.stack([tokens[:, :window], out_grad[:, :window]]), "tensor")
    grad_keep = exchange_z(grad_blocks, zrel)
    tok_keep[1], up_b = tie(tok_keep[1], up_b)
    tok_other = [flip(piece, "tensor", 1) for piece in tok_keep]
    down_a_in, up_b = tie(down_weight[:dcut], up_b)
    down_a = flip(down_a_in, "dp", 1)
    grad_other = [flip(piece, "tensor", 1) for piece in grad_keep]
    up_other = jnp.concatenate([up_a, up_b])
    tok_win, grad_win = windows[0], windows[1]

    def partial(kept, other, own_w, par_w, dims):
        def part_of(ks):
            a = jnp.concatenate([jnp.where(core == 0, kept[k], other[k]) for k in ks])
            b = jnp.concatenate([jnp.where(core == 0, other[k], kept[k]) for k in ks])
            return (dot(a, own_w, dims) + dot(b, par_w, dims)).reshape(len(ks), rows, -1)

        return part_of

    def first_stage(part_of):
        send = [k for k in range(zcount) if k & 1]
        keep = [k for k in range(zcount) if not k & 1]
        got = flip(part_of(send).astype(BF), "dp", 2)
        return part_of(keep) + got.astype(F32)

    def later_stages(acc):
        ks = [k for k in range(zcount) if not k & 1]
        for bit in zbits[1:]:
            sel = [n for n, k in enumerate(ks) if k & bit]
            stay = [n for n, k in enumerate(ks) if not k & bit]
            send = jnp.stack([acc[n] for n in sel]).astype(BF)
            acc = jnp.stack([acc[n] for n in stay]) + flip(send, "dp", 2 * bit).astype(F32)
            ks = [ks[n] for n in stay]
        return acc[0]

    pre_acc = first_stage(partial(tok_keep, tok_other, up_weight, up_other, ((1,), (0,))))
    pre_acc, down_a = tie(pre_acc, down_a)
    down_b_in, down_a = tie(down_weight[dcut:], down_a)
    down_b = flip(down_b_in, "dp", 1)
    preact = later_stages(pre_acc)
    down_other = jnp.concatenate([down_a, down_b])
    back_acc = first_stage(partial(grad_keep, grad_other, down_weight, down_other, ((1,), (1,))))
    back_act = later_stages(back_acc)

    squash = jax.nn.sigmoid(preact)
    act_out = (preact * squash).astype(BF)
    slope = squash * (1.0 + preact * (1.0 - squash))
    down_matrix = down_accum[0] + dot(act_out, grad_win, ((0,), (0,))) * scale
    down_sum = allsum(dot(down_matrix, down_q, precision=HIGHEST), "dp", dbits)
    down_gram = dot(down_sum, down_sum, ((0,), (0,)), HIGHEST)
    down_term = dot(down_matrix, down_sum, ((0,), (0,)), HIGHEST)
    back_act, down_gram, down_term = tie(back_act, down_gram, down_term)
    hidden = (back_act * slope).astype(BF)

    w_dims = ((1,), (1,))
    hid = {0: hidden}
    returned = {}

    def send_back(ks):
        lhs = jnp.concatenate([hid[k] for k in ks])
        own = dot(lhs, up_weight, w_dims).astype(BF)
        par = dot(lhs, up_other, w_dims).astype(BF)
        got = flip(jnp.where(core == 0, par, own), "tensor", 1)
        mine = (jnp.where(core == 0, own, par).astype(F32) + got.astype(F32)).astype(BF)
        mine = mine.reshape(len(ks), rows, -1)
        for n, k in enumerate(ks):
            returned[k] = mine[n] if k == 0 else flip(mine[n], "dp", 2 * k)

    def settle(ks):
        blocks = [returned[k] for k in ks]
        stack = jnp.stack(blocks)
        order = [
            lax.dynamic_index_in_dim(stack, (zrel >> 1) ^ q, 0, keepdims=False) for q in range(len(ks))
        ]
        for mask in reversed(tbits[1:]):
            n = len(order) // 2
            got = flip(jnp.stack(order[n:]), "tensor", mask)
            order = [(order[i].astype(F32) + got[i].astype(F32)).astype(BF) for i in range(n)]
        return order[0]

    for bit in reversed(zbits[1:]):
        ks = sorted(hid)
        got = flip(jnp.stack([hid[k] for k in ks]), "dp", 2 * bit)
        for n, k in enumerate(ks):
            hid[k | bit] = got[n]
    even = sorted(hid)
    got = flip(jnp.stack([hid[k] for k in even]), "dp", 2)
    send_back(even)
    for n, k in enumerate(even):
        hid[k | 1] = got[n]
    send_back([k | 1 for k in even])
    sum_a = settle(even)
    sum_b = settle([k | 1 for k in even])
    low = zrel & 1
    got = flip(jnp.where(low == 0, sum_b, sum_a), "tensor", 1)
    own = jnp.where(low == 0, sum_a, sum_b)
    input_grad = jnp.concatenate(
        [jnp.where(half == 0, own, got), jnp.where(half == 0, got, own)], axis=1
    )

    up_matrix = up_accum[0] + dot(tok_win, hidden, ((0,), (0,))) * scale
    both = jnp.concatenate([dot(up_matrix, up_q, precision=HIGHEST), down_term, down_gram])
    both = allsum(allsum(both, "tensor", tbits), "dp", dbits)
    up_sum, down_term, down_gram = both[:window], both[window : 2 * window], both[2 * window :]
    up_term = allsum(dot(up_matrix, up_sum, ((0,), (0,)), HIGHEST), "dp", dbits)
    up_inv = inverse_factor(dot(up_sum, up_sum, ((0,), (0,)), HIGHEST))
    up_left = dot(up_sum, up_inv, precision=HIGHEST)
    up_right = dot(up_term, up_inv, precision=HIGHEST) / replicas
    up_error = up_matrix - dot(up_left, up_right, ((1,), (1,)), HIGHEST)
    down_inv = inverse_factor(down_gram / replicas)
    down_left = dot(down_sum, down_inv, precision=HIGHEST)
    down_right = dot(down_term, down_inv, precision=HIGHEST) / replicas
    down_error = down_matrix - dot(down_left, down_right, ((1,), (1,)), HIGHEST)
    return (input_grad, up_error[None], up_left, up_right, down_error[None], down_left, down_right)


def solution(mesh):
    return jax.shard_map(
        shards,
        mesh=mesh,
        in_specs=(
            P("dp", "tensor"),
            P("dp", "tensor"),
            P("dp", "tensor"),
            P("tensor", "dp"),
            P("dp", None, "tensor"),
            P("dp", "tensor", None),
            P("tensor", None),
            P(),
        ),
        out_specs=(
            P("dp", "tensor"),
            P("dp", None, "tensor"),
            P(),
            P("tensor", None),
            P("dp", "tensor", None),
            P("tensor", None),
            P(),
        ),
        check_vma=False,
    )
```

time: 227 us -> 189 us (0.83)
  waiting for transfers between devices: 116 us -> 82 us
  other arithmetic: 26.5 us -> 23.4 us
  local copies, waits for them, and re-layouts: 5.62 us -> 8.21 us
  matrix products: 19.8 us -> 17.4 us
    ppermute x41 -> x47, waiting for transfers between devices: 116 us -> 80.4 us  [flip(): return lax.ppermute(arr, axis, [(i, i ^ mask) for i in range(size)])]
    unnamed x40, local copies, waits for them, and re-layouts: 0.29 us -> 3.75 us
    ppermute x41 -> x47, starting transfers between devices: 52.3 us -> 49.9 us  [flip(): return lax.ppermute(arr, axis, [(i, i ^ mask) for i in range(size)])]
    dot_general x24 -> x26, matrix products: 19.4 us -> 17 us  [dot(): lax.dot_general(a, b, (dims, ((), ())), preferred_element_type=F32, preci...]
    another operation x8 -> x9, other arithmetic: 5.58 us -> 3.72 us  [the longest x4 1.81 us: exchange_tensor(): return jnp.stack(blocks)]
  transfers between devices with their start and end apart: 43 -> 49, of which waited for: 20 -> 23; matrix products, arithmetic and copies ran while one was open for 21% -> 22% of each run, Pallas kernels for 0% -> 0%
where the time goes in v2:
time: 189 us; the launch traced here: 187 us
  waiting for transfers between devices  82 us (43%)
  starting transfers between devices  54.2 us (29%)
  other arithmetic  23.4 us (12%)
  matrix products  17.4 us (9%)
  local copies, waits for them, and re-layouts  8.21 us (4%)
    ppermute x47, waiting for transfers between devices, flip(): return lax.ppermute(arr, axis, [(i, i ^ mask) for i in range(size)])  80.4 us
    ppermute x47, starting transfers between devices, flip(): return lax.ppermute(arr, axis, [(i, i ^ mask) for i in range(size)])  49.9 us
    dot_general x26, matrix products, dot(): lax.dot_general(a, b, (dims, ((), ())), preferred_element_type=F32, preci...  17 us
    another operation x6, other arithmetic, inverse_factor(): lower = jnp.linalg.cholesky(gram)  7.19 us
    another operation x4, other arithmetic, inverse_factor(): lax.linalg.triangular_solve(lower, jnp.eye(gram.shape[0], dtype=F32), lef...  6.17 us
    ppermute x2, starting transfers between devices, broadcast_first(): arr = arr + lax.ppermute(arr, axis, [(i, i + mask) for i in range(mask)])  4.3 us
  transfers between devices with their start and end apart: 49, of which 23 were waited for; matrix products, arithmetic and copies ran while one was open for 22% of the time, Pallas kernels for 0%

profile of v2, /device:TPU:0, one launch (start us, length us, event | category | flops | bytes accessed | tf_op | source)
XLA Modules:
  0.0 186.8 jit_solution(17986492613459518431)
XLA Ops:
  3.5 2.6 %collective-permute-start.7 = (bf16[256,896]{1,0:T(8,128)(2,1)S(1)}, bf16[256,896]{1,0:T(8,128)(2,1)}, u32[]{:S(2)}, u32[]{:S(2)}) collective-permute-start(bf16[256,896]{1,0:T(8,128)(2,1)S(1)} %get-tuple-element.42), channel_id=1, source_target_pairs={{0,4},{4,0},{8,12},{12,8},{16,20},{20,16},{24,28},{28,24},{1,5},{5... | collective-permute-start | bytes 1376264 | tf_op jit(solution)/shard_map/ppermute | solution.py:15
  7.6 2.1 %collective-permute-start.26 = (bf16[2,128,256]{2,1,0:T(8,128)(2,1)}, bf16[2,128,256]{2,1,0:T(8,128)(2,1)S(1)}, u32[]{:S(2)}, u32[]{:S(2)}) collective-permute-start(bf16[2,128,256]{2,1,0:T(8,128)(2,1)} %maximum_select_fusion), channel_id=1, source_target_pairs={{0,1},{4,5},{8,9},{12,13},{16,17},{20,21},{24,25},{28,29}} | collective-permute-start | bytes 393224 | tf_op jit(solution)/shard_map/ppermute | solution.py:35
  11.3 2.2 %collective-permute-start.27 = (bf16[2,128,256]{2,1,0:T(8,128)(2,1)S(1)}, bf16[2,128,256]{2,1,0:T(8,128)(2,1)S(1)}, u32[]{:S(2)}, u32[]{:S(2)}) collective-permute-start(bf16[2,128,256]{2,1,0:T(8,128)(2,1)S(1)} %fusion.116), channel_id=1, source_target_pairs={{0,2},{1,3},{4,6},{5,7},{8,10},{9,11},{12,14},{13,15},{16,18},{17,... | collective-permute-start | bytes 393224 | tf_op jit(solution)/shard_map/ppermute | solution.py:35
  13.6 2.1 %collective-permute-start.6 = (bf16[2,128,512]{2,1,0:T(8,128)(2,1)S(1)}, bf16[2,128,512]{2,1,0:T(8,128)(2,1)S(1)}, u32[]{:S(2)}, u32[]{:S(2)}) collective-permute-start(bf16[2,128,512]{2,1,0:T(8,128)(2,1)S(1)} %pad_maximum_fusion.10), channel_id=1, source_target_pairs={{0,2},{1,3},{2,0},{3,1},{4,6},{5,7},{6,4},{7,5},{8,10},{9,11},{10,... | collective-permute-start | bytes 786440 | tf_op jit(solution)/shard_map/ppermute | solution.py:15
  15.7 1.6 collective-permute-done.27
  17.3 5.6 %collective-permute-done.1 = bf16[2,128,512]{2,1,0:T(8,128)(2,1)S(1)} collective-permute-done((bf16[2,128,512]{2,1,0:T(8,128)(2,1)S(1)}, bf16[2,128,512]{2,1,0:T(8,128)(2,1)S(1)}, u32[]{:S(2)}, u32[]{:S(2)}) %collective-permute-start.1) | collective-permute-done | bytes 262176 | tf_op jit(solution)/shard_map/ppermute | solution.py:15
  23.0 2.7 %collective-permute-start.3 = (bf16[128,512]{1,0:T(8,128)(2,1)S(1)}, bf16[128,512]{1,0:T(8,128)(2,1)S(1)}, u32[]{:S(2)}, u32[]{:S(2)}) collective-permute-start(bf16[128,512]{1,0:T(8,128)(2,1)S(1)} %get-tuple-element.46), channel_id=1, source_target_pairs={{0,16},{4,20},{8,24},{12,28},{16,0},{20,4},{24,8},{28,12},{1,17},{... | collective-permute-start | bytes 393224 | tf_op jit(solution)/shard_map/ppermute | solution.py:15
  27.9 1.6 collective-permute-start.19
  31.3 3.5 %collective-permute-done.3 = bf16[128,512]{1,0:T(8,128)(2,1)S(1)} collective-permute-done((bf16[128,512]{1,0:T(8,128)(2,1)S(1)}, bf16[128,512]{1,0:T(8,128)(2,1)S(1)}, u32[]{:S(2)}, u32[]{:S(2)}) %collective-permute-start.3) | collective-permute-done | bytes 131104 | tf_op jit(solution)/shard_map/ppermute | solution.py:15
  34.9 3.5 %collective-permute-start.14 = (bf16[128,512]{1,0:T(8,128)(2,1)S(1)}, bf16[128,512]{1,0:T(8,128)(2,1)S(1)}, u32[]{:S(2)}, u32[]{:S(2)}) collective-permute-start(bf16[128,512]{1,0:T(8,128)(2,1)S(1)} %get-tuple-element.48), channel_id=1, source_target_pairs={{0,24},{4,28},{8,16},{12,20},{16,8},{20,12},{24,0},{28,4},{1,25},{... | collective-permute-start | bytes 393224 | tf_op jit(solution)/shard_map/ppermute | solution.py:15
  39.2 8.0 %collective-permute-done.9 = bf16[128,512]{1,0:T(8,128)(2,1)S(1)} collective-permute-done((bf16[128,512]{1,0:T(8,128)(2,1)S(1)}, bf16[128,512]{1,0:T(8,128)(2,1)S(1)}, u32[]{:S(2)}, u32[]{:S(2)}) %collective-permute-start.9) | collective-permute-done | bytes 131104 | tf_op jit(solution)/shard_map/ppermute | solution.py:15
  48.8 2.6 %collective-permute-done.12 = bf16[256,896]{1,0:T(8,128)(2,1)S(1)} collective-permute-done((bf16[256,896]{1,0:T(8,128)(2,1)S(1)}, bf16[256,896]{1,0:T(8,128)(2,1)S(1)}, u32[]{:S(2)}, u32[]{:S(2)}) %collective-permute-start.12) | collective-permute-done | bytes 458784 | tf_op jit(solution)/shard_map/ppermute | solution.py:15
  54.4 1.9 collective-permute-start.16
  57.2 9.9 %collective-permute-done.16 = bf16[2,128,896]{2,1,0:T(8,128)(2,1)S(1)} collective-permute-done((bf16[2,128,896]{2,1,0:T(8,128)(2,1)S(1)}, bf16[2,128,896]{2,1,0:T(8,128)(2,1)S(1)}, u32[]{:S(2)}, u32[]{:S(2)}) %collective-permute-start.16) | collective-permute-done | bytes 458784 | tf_op jit(solution)/shard_map/ppermute | solution.py:15
  67.3 2.0 %collective-permute-start.25 = (bf16[1,128,896]{2,1,0:T(8,128)(2,1)S(1)}, bf16[1,128,896]{2,1,0:T(8,128)(2,1)S(1)}, u32[]{:S(2)}, u32[]{:S(2)}) collective-permute-start(bf16[1,128,896]{2,1,0:T(8,128)(2,1)S(1)} %slice.176), channel_id=1, source_target_pairs={{0,16},{4,20},{8,24},{12,28},{16,0},{20,4},{24,8},{28,12},{1,17},{... | collective-permute-start | bytes 688136 | tf_op jit(solution)/shard_map/ppermute | solution.py:15
  70.6 9.4 %collective-permute-done.25 = bf16[1,128,896]{2,1,0:T(8,128)(2,1)S(1)} collective-permute-done((bf16[1,128,896]{2,1,0:T(8,128)(2,1)S(1)}, bf16[1,128,896]{2,1,0:T(8,128)(2,1)S(1)}, u32[]{:S(2)}, u32[]{:S(2)}) %collective-permute-start.25) | collective-permute-done | bytes 229408 | tf_op jit(solution)/shard_map/ppermute | solution.py:15
  81.6 1.4 collective-permute-start.28
  83.1 3.4 %collective-permute-done.28 = f32[896,32]{0,1:T(8,128)S(1)} collective-permute-done((f32[896,32]{0,1:T(8,128)S(1)}, f32[896,32]{0,1:T(8,128)S(1)}, u32[]{:S(2)}, u32[]{:S(2)}) %collective-permute-start.28) | collective-permute-done | bytes 114720 | tf_op jit(solution)/shard_map/ppermute | solution.py:15
  87.6 2.1 %collective-permute-start.23 = (bf16[2,128,896]{2,1,0:T(8,128)(2,1)S(1)}, bf16[2,128,896]{2,1,0:T(8,128)(2,1)S(1)}, u32[]{:S(2)}, u32[]{:S(2)}) collective-permute-start(bf16[2,128,896]{2,1,0:T(8,128)(2,1)S(1)} %bitcast.151), channel_id=1, source_target_pairs={{0,8},{4,12},{8,0},{12,4},{16,24},{20,28},{24,16},{28,20},{1,9},{5... | collective-permute-start | bytes 1376264 | tf_op jit(solution)/shard_map/ppermute | solution.py:15
  90.1 3.8 %collective-permute-done.29 = f32[896,32]{0,1:T(8,128)S(1)} collective-permute-done((f32[896,32]{0,1:T(8,128)S(1)}, f32[896,32]{0,1:T(8,128)S(1)}, u32[]{:S(2)}, u32[]{:S(2)}) %collective-permute-start.29) | collective-permute-done | bytes 114720 | tf_op jit(solution)/shard_map/ppermute | solution.py:15
  94.5 6.2 %collective-permute-done.30 = f32[896,32]{0,1:T(8,128)S(1)} collective-permute-done((f32[896,32]{0,1:T(8,128)S(1)}, f32[896,32]{0,1:T(8,128)S(1)}, u32[]{:S(2)}, u32[]{:S(2)}) %collective-permute-start.30) | collective-permute-done | bytes 114720 | tf_op jit(solution)/shard_map/ppermute | solution.py:15
  101.7 3.2 %collective-permute-start.24 = (bf16[1,128,896]{2,1,0:T(8,128)(2,1)S(1)}, bf16[1,128,896]{2,1,0:T(8,128)(2,1)S(1)}, u32[]{:S(2)}, u32[]{:S(2)}) collective-permute-start(bf16[1,128,896]{2,1,0:T(8,128)(2,1)S(1)} %slice.177), channel_id=1, source_target_pairs={{0,16},{4,20},{8,24},{12,28},{16,0},{20,4},{24,8},{28,12},{1,17},{... | collective-permute-start | bytes 688136 | tf_op jit(solution)/shard_map/ppermute | solution.py:15
  105.1 8.1 %collective-permute-done.24 = bf16[1,128,896]{2,1,0:T(8,128)(2,1)S(1)} collective-permute-done((bf16[1,128,896]{2,1,0:T(8,128)(2,1)S(1)}, bf16[1,128,896]{2,1,0:T(8,128)(2,1)S(1)}, u32[]{:S(2)}, u32[]{:S(2)}) %collective-permute-start.24) | collective-permute-done | bytes 229408 | tf_op jit(solution)/shard_map/ppermute | solution.py:15
  118.1 2.5 %collective-permute-start.42 = (f32[544,32]{0,1:T(8,128)S(1)}, f32[544,32]{0,1:T(8,128)S(1)}, u32[]{:S(2)}, u32[]{:S(2)}) collective-permute-start(f32[544,32]{0,1:T(8,128)S(1)} %fusion.76), channel_id=1, source_target_pairs={{0,2},{1,3},{2,0},{3,1},{4,6},{5,7},{6,4},{7,5},{8,10},{9,11},{10,... | collective-permute-start | bytes 208904 | tf_op jit(solution)/shard_map/ppermute | solution.py:15
  120.7 2.8 %collective-permute-done.42 = f32[544,32]{0,1:T(8,128)S(1)} collective-permute-done((f32[544,32]{0,1:T(8,128)S(1)}, f32[544,32]{0,1:T(8,128)S(1)}, u32[]{:S(2)}, u32[]{:S(2)}) %collective-permute-start.42) | collective-permute-done | bytes 69664 | tf_op jit(solution)/shard_map/ppermute | solution.py:15
  123.5 1.4 collective-permute-start.43
  124.9 3.1 %collective-permute-done.43 = f32[544,32]{0,1:T(8,128)S(1)} collective-permute-done((f32[544,32]{0,1:T(8,128)S(1)}, f32[544,32]{0,1:T(8,128)S(1)}, u32[]{:S(2)}, u32[]{:S(2)}) %collective-permute-start.43) | collective-permute-done | bytes 69664 | tf_op jit(solution)/shard_map/ppermute | solution.py:15
  128.0 1.8 collective-permute-start.44
  130.5 1.5 convolution_convert_fusion.3
  132.0 2.2 %broadcast_select_fusion.1 = (bf16[256,512]{1,0:T(8,128)(2,1)}, bf16[256,512]{1,0:T(8,128)(2,1)}) fusion(bf16[256,512]{1,0:T(8,128)(2,1)S(1)} %convolution_convert_fusion.3, pred[]{:T(512)S(6)} %eq.17, bf16[512,896]{1,0:T(8,128)(2,1)S(1)} %copy-done.4, bf16[128,896]{1,0:T(8,128)(2,1)} %bitcast.24, bf16[128,896]{1,0:T(8,128)(2,1)S(1)} %fusion.13), kind=kOutput, calls=%fused_computation.88 | convolution fusion | flops 236060672 | bytes 2162689 | tf_op jit(solution)/shard_map/dot_general | solution.py:23
  134.7 1.8 pad_maximum_fusion.3
  136.5 1.7 collective-permute-start.35
  138.1 2.8 %collective-permute-done.45 = f32[544,32]{0,1:T(8,128)S(1)} collective-permute-done((f32[544,32]{0,1:T(8,128)S(1)}, f32[544,32]{0,1:T(8,128)S(1)}, u32[]{:S(2)}, u32[]{:S(2)}) %collective-permute-start.45) | collective-permute-done | bytes 69664 | tf_op jit(solution)/shard_map/ppermute | solution.py:15
  141.8 2.9 %cholesky.44 = f32[32,32]{1,0:T(8,128)S(1)} custom-call(f32[32,32]{1,0:T(8,128)S(1)} %fusion.62), custom_call_target="Cholesky" | custom-call | tf_op jit(solution)/shard_map/jit(cholesky)/cholesky | solution.py:40
  146.1 2.4 %custom-call.6 = f32[1,32,32]{1,2,0:T(8,128)S(1)} custom-call(f32[1,32,32]{2,1,0:T(8,128)S(1)} %fusion.57), custom_call_target="InvertDiagBlocksLowerTriangular" | custom-call | tf_op jit(solution)/shard_map/triangular_solve/custom-call.0 | solution.py:41
  148.7 1.4 collective-permute-start.46
  150.2 2.9 %cholesky.55 = f32[32,32]{1,0:T(8,128)S(1)} custom-call(f32[32,32]{1,0:T(8,128)S(1)} %fusion.60), custom_call_target="Cholesky" | custom-call | tf_op jit(solution)/shard_map/jit(cholesky)/cholesky | solution.py:40
  154.4 2.4 %custom-call.7 = f32[1,32,32]{1,2,0:T(8,128)S(1)} custom-call(f32[1,32,32]{2,1,0:T(8,128)S(1)} %fusion.58), custom_call_target="InvertDiagBlocksLowerTriangular" | custom-call | tf_op jit(solution)/shard_map/triangular_solve/custom-call.0 | solution.py:41
  163.2 2.9 %collective-permute-start.33 = (bf16[128,512]{1,0:T(8,128)(2,1)S(1)}, bf16[128,512]{1,0:T(8,128)(2,1)S(1)}, u32[]{:S(2)}, u32[]{:S(2)}) collective-permute-start(bf16[128,512]{1,0:T(8,128)(2,1)S(1)} %get-tuple-element.58), channel_id=1, source_target_pairs={{0,16},{4,20},{8,24},{12,28},{16,0},{20,4},{24,8},{28,12},{1,17},{... | collective-permute-start | bytes 393224 | tf_op jit(solution)/shard_map/ppermute | solution.py:15
  166.4 1.6 collective-permute-start.38
  167.9 1.8 fusion
  169.8 2.0 %collective-permute-start.48 = (f32[896,32]{0,1:T(8,128)S(1)}, f32[896,32]{0,1:T(8,128)S(1)}, u32[]{:S(2)}, u32[]{:S(2)}) collective-permute-start(f32[896,32]{0,1:T(8,128)S(1)} %add.170), channel_id=1, source_target_pairs={{0,16},{4,20},{8,24},{12,28},{16,0},{20,4},{24,8},{28,12},{1,17},{... | collective-permute-start | bytes 344072 | tf_op jit(solution)/shard_map/ppermute | solution.py:15
  171.8 1.7 collective-permute-done.33
  173.5 2.5 %collective-permute-start.34 = (bf16[1,128,512]{2,1,0:T(8,128)(2,1)S(1)}, bf16[1,128,512]{2,1,0:T(8,128)(2,1)S(1)}, u32[]{:S(2)}, u32[]{:S(2)}) collective-permute-start(bf16[1,128,512]{2,1,0:T(8,128)(2,1)S(1)} %fusion.45), channel_id=1, source_target_pairs={{0,2},{1,3},{2,0},{3,1},{4,6},{5,7},{6,4},{7,5},{8,10},{9,11},{10,... | collective-permute-start | bytes 393224 | tf_op jit(solution)/shard_map/ppermute | solution.py:15
  176.0 1.7 collective-permute-done.38
  177.8 2.5 %collective-permute-start.39 = (bf16[1,128,512]{2,1,0:T(8,128)(2,1)S(1)}, bf16[1,128,512]{2,1,0:T(8,128)(2,1)S(1)}, u32[]{:S(2)}, u32[]{:S(2)}) collective-permute-start(bf16[1,128,512]{2,1,0:T(8,128)(2,1)S(1)} %fusion.43), channel_id=1, source_target_pairs={{0,2},{1,3},{2,0},{3,1},{4,6},{5,7},{6,4},{7,5},{8,10},{9,11},{10,... | collective-permute-start | bytes 393224 | tf_op jit(solution)/shard_map/ppermute | solution.py:15
  180.3 3.0 %collective-permute-done.48 = f32[896,32]{0,1:T(8,128)S(1)} collective-permute-done((f32[896,32]{0,1:T(8,128)S(1)}, f32[896,32]{0,1:T(8,128)S(1)}, u32[]{:S(2)}, u32[]{:S(2)}) %collective-permute-start.48) | collective-permute-done | bytes 114720 | tf_op jit(solution)/shard_map/ppermute | solution.py:15
  184.2 1.9 fusion.1
  (188 shorter events, 40.9 us)
Async XLA Ops:
  1.7 11.9 %collective-permute-start.5 = (bf16[128,512]{1,0:T(8,128)(2,1)S(1)}, bf16[128,512]{1,0:T(8,128)(2,1)S(1)}, u32[]{:S(2)}, u32[]{:S(2)}) collective-permute-start(bf16[128,512]{1,0:T(8,128)(2,1)S(1)} %get-tuple-element.79), channel_id=1, source_target_pairs={{0,1},{1,0},{2,3},{3,2},{4,5},{5,4},{6,7},{7,6},{8,9},{9,8},{10,11... | collective-permute-start | bytes 393224 | tf_op jit(solution)/shard_map/ppermute | solution.py:15
  3.5 26.1 %collective-permute-start.7 = (bf16[256,896]{1,0:T(8,128)(2,1)S(1)}, bf16[256,896]{1,0:T(8,128)(2,1)}, u32[]{:S(2)}, u32[]{:S(2)}) collective-permute-start(bf16[256,896]{1,0:T(8,128)(2,1)S(1)} %get-tuple-element.42), channel_id=1, source_target_pairs={{0,4},{4,0},{8,12},{12,8},{16,20},{20,16},{24,28},{28,24},{1,5},{5... | collective-permute-start | bytes 1376264 | tf_op jit(solution)/shard_map/ppermute | solution.py:15
  7.6 3.7 %collective-permute-start.26 = (bf16[2,128,256]{2,1,0:T(8,128)(2,1)}, bf16[2,128,256]{2,1,0:T(8,128)(2,1)S(1)}, u32[]{:S(2)}, u32[]{:S(2)}) collective-permute-start(bf16[2,128,256]{2,1,0:T(8,128)(2,1)} %maximum_select_fusion), channel_id=1, source_target_pairs={{0,1},{4,5},{8,9},{12,13},{16,17},{20,21},{24,25},{28,29}} | collective-permute-start | bytes 393224 | tf_op jit(solution)/shard_map/ppermute | solution.py:35
  10.4 3.1 %collective-permute-start = (bf16[128,512]{1,0:T(8,128)(2,1)}, bf16[128,512]{1,0:T(8,128)(2,1)S(1)}, u32[]{:S(2)}, u32[]{:S(2)}) collective-permute-start(bf16[128,512]{1,0:T(8,128)(2,1)} %get-tuple-element.69), channel_id=1, source_target_pairs={{0,1},{1,0},{2,3},{3,2},{4,5},{5,4},{6,7},{7,6},{8,9},{9,8},{10,11... | collective-permute-start | bytes 393224 | tf_op jit(solution)/shard_map/ppermute | solution.py:15
  11.3 6.0 %collective-permute-start.27 = (bf16[2,128,256]{2,1,0:T(8,128)(2,1)S(1)}, bf16[2,128,256]{2,1,0:T(8,128)(2,1)S(1)}, u32[]{:S(2)}, u32[]{:S(2)}) collective-permute-start(bf16[2,128,256]{2,1,0:T(8,128)(2,1)S(1)} %fusion.116), channel_id=1, source_target_pairs={{0,2},{1,3},{4,6},{5,7},{8,10},{9,11},{12,14},{13,15},{16,18},{17,... | collective-permute-start | bytes 393224 | tf_op jit(solution)/shard_map/ppermute | solution.py:35
  13.5 9.4 %collective-permute-start.1 = (bf16[2,128,512]{2,1,0:T(8,128)(2,1)S(1)}, bf16[2,128,512]{2,1,0:T(8,128)(2,1)S(1)}, u32[]{:S(2)}, u32[]{:S(2)}) collective-permute-start(bf16[2,128,512]{2,1,0:T(8,128)(2,1)S(1)} %pad_maximum_fusion.9), channel_id=1, source_target_pairs={{0,2},{1,3},{2,0},{3,1},{4,6},{5,7},{6,4},{7,5},{8,10},{9,11},{10,... | collective-permute-start | bytes 786440 | tf_op jit(solution)/shard_map/ppermute | solution.py:15
  13.6 14.3 %collective-permute-start.6 = (bf16[2,128,512]{2,1,0:T(8,128)(2,1)S(1)}, bf16[2,128,512]{2,1,0:T(8,128)(2,1)S(1)}, u32[]{:S(2)}, u32[]{:S(2)}) collective-permute-start(bf16[2,128,512]{2,1,0:T(8,128)(2,1)S(1)} %pad_maximum_fusion.10), channel_id=1, source_target_pairs={{0,2},{1,3},{2,0},{3,1},{4,6},{5,7},{6,4},{7,5},{8,10},{9,11},{10,... | collective-permute-start | bytes 786440 | tf_op jit(solution)/shard_map/ppermute | solution.py:15
  23.0 11.8 %collective-permute-start.3 = (bf16[128,512]{1,0:T(8,128)(2,1)S(1)}, bf16[128,512]{1,0:T(8,128)(2,1)S(1)}, u32[]{:S(2)}, u32[]{:S(2)}) collective-permute-start(bf16[128,512]{1,0:T(8,128)(2,1)S(1)} %get-tuple-element.46), channel_id=1, source_target_pairs={{0,16},{4,20},{8,24},{12,28},{16,0},{20,4},{24,8},{28,12},{1,17},{... | collective-permute-start | bytes 393224 | tf_op jit(solution)/shard_map/ppermute | solution.py:15
  25.7 5.5 %collective-permute-start.2 = (bf16[128,512]{1,0:T(8,128)(2,1)S(1)}, bf16[128,512]{1,0:T(8,128)(2,1)S(1)}, u32[]{:S(2)}, u32[]{:S(2)}) collective-permute-start(bf16[128,512]{1,0:T(8,128)(2,1)S(1)} %get-tuple-element.47), channel_id=1, source_target_pairs={{0,1},{1,0},{2,3},{3,2},{4,5},{5,4},{6,7},{7,6},{8,9},{9,8},{10,11... | collective-permute-start | bytes 393224 | tf_op jit(solution)/shard_map/ppermute | solution.py:15
  25.7 9.2 %collective-permute-start.21 = (bf16[128,512]{1,0:T(8,128)(2,1)S(1)}, bf16[128,512]{1,0:T(8,128)(2,1)S(1)}, u32[]{:S(2)}, u32[]{:S(2)}) collective-permute-start(bf16[128,512]{1,0:T(8,128)(2,1)S(1)} %get-tuple-element.45), channel_id=1, source_target_pairs={{0,24},{4,28},{8,16},{12,20},{16,8},{20,12},{24,0},{28,4},{1,25},{... | collective-permute-start | bytes 393224 | tf_op jit(solution)/shard_map/ppermute | solution.py:15
  27.9 10.7 %collective-permute-start.19 = (bf16[128,512]{1,0:T(8,128)(2,1)S(1)}, bf16[128,512]{1,0:T(8,128)(2,1)S(1)}, u32[]{:S(2)}, u32[]{:S(2)}) collective-permute-start(bf16[128,512]{1,0:T(8,128)(2,1)S(1)} %get-tuple-element.44), channel_id=1, source_target_pairs={{0,8},{4,12},{8,0},{12,4},{16,24},{20,28},{24,16},{28,20},{1,9},{5... | collective-permute-start | bytes 393224 | tf_op jit(solution)/shard_map/ppermute | solution.py:15
  29.6 19.2 %collective-permute-start.11 = (bf16[128,512]{1,0:T(8,128)(2,1)S(1)}, bf16[128,512]{1,0:T(8,128)(2,1)S(1)}, u32[]{:S(2)}, u32[]{:S(2)}) collective-permute-start(bf16[128,512]{1,0:T(8,128)(2,1)S(1)} %get-tuple-element.49), channel_id=1, source_target_pairs={{0,8},{4,12},{8,0},{12,4},{16,24},{20,28},{24,16},{28,20},{1,9},{5... | collective-permute-start | bytes 393224 | tf_op jit(solution)/shard_map/ppermute | solution.py:15
  31.2 3.6 %collective-permute-start.8 = (bf16[128,512]{1,0:T(8,128)(2,1)S(1)}, bf16[128,512]{1,0:T(8,128)(2,1)S(1)}, u32[]{:S(2)}, u32[]{:S(2)}) collective-permute-start(bf16[128,512]{1,0:T(8,128)(2,1)S(1)} %get-tuple-element.51), channel_id=1, source_target_pairs={{0,1},{1,0},{2,3},{3,2},{4,5},{5,4},{6,7},{7,6},{8,9},{9,8},{10,11... | collective-permute-start | bytes 393224 | tf_op jit(solution)/shard_map/ppermute | solution.py:15
  34.8 12.4 %collective-permute-start.9 = (bf16[128,512]{1,0:T(8,128)(2,1)S(1)}, bf16[128,512]{1,0:T(8,128)(2,1)S(1)}, u32[]{:S(2)}, u32[]{:S(2)}) collective-permute-start(bf16[128,512]{1,0:T(8,128)(2,1)S(1)} %get-tuple-element.50), channel_id=1, source_target_pairs={{0,16},{4,20},{8,24},{12,28},{16,0},{20,4},{24,8},{28,12},{1,17},{... | collective-permute-start | bytes 393224 | tf_op jit(solution)/shard_map/ppermute | solution.py:15
  34.8 3.6 %collective-permute-start.4 = (bf16[128,512]{1,0:T(8,128)(2,1)S(1)}, bf16[128,512]{1,0:T(8,128)(2,1)S(1)}, u32[]{:S(2)}, u32[]{:S(2)}) collective-permute-start(bf16[128,512]{1,0:T(8,128)(2,1)S(1)} %collective-permute-done.3), channel_id=1, source_target_pairs={{0,1},{1,0},{2,3},{3,2},{4,5},{5,4},{6,7},{7,6},{8,9},{9,8},{10,11... | collective-permute-start | bytes 393224 | tf_op jit(solution)/shard_map/ppermute | solution.py:15
  34.9 12.3 %collective-permute-start.14 = (bf16[128,512]{1,0:T(8,128)(2,1)S(1)}, bf16[128,512]{1,0:T(8,128)(2,1)S(1)}, u32[]{:S(2)}, u32[]{:S(2)}) collective-permute-start(bf16[128,512]{1,0:T(8,128)(2,1)S(1)} %get-tuple-element.48), channel_id=1, source_target_pairs={{0,24},{4,28},{8,16},{12,20},{16,8},{20,12},{24,0},{28,4},{1,25},{... | collective-permute-start | bytes 393224 | tf_op jit(solution)/shard_map/ppermute | solution.py:15
  38.4 9.3 %collective-permute-start.22 = (bf16[128,512]{1,0:T(8,128)(2,1)S(1)}, bf16[128,512]{1,0:T(8,128)(2,1)S(1)}, u32[]{:S(2)}, u32[]{:S(2)}) collective-permute-start(bf16[128,512]{1,0:T(8,128)(2,1)S(1)} %collective-permute-done.21), channel_id=1, source_target_pairs={{0,1},{1,0},{2,3},{3,2},{4,5},{5,4},{6,7},{7,6},{8,9},{9,8},{10,11... | collective-permute-start | bytes 393224 | tf_op jit(solution)/shard_map/ppermute | solution.py:15
  38.6 12.8 %collective-permute-start.12 = (bf16[256,896]{1,0:T(8,128)(2,1)S(1)}, bf16[256,896]{1,0:T(8,128)(2,1)S(1)}, u32[]{:S(2)}, u32[]{:S(2)}) collective-permute-start(bf16[256,896]{1,0:T(8,128)(2,1)S(1)} %get-tuple-element.27), channel_id=1, source_target_pairs={{0,4},{4,0},{8,12},{12,8},{16,20},{20,16},{24,28},{28,24},{1,5},{5... | collective-permute-start | bytes 1376264 | tf_op jit(solution)/shard_map/ppermute | solution.py:15
  47.2 22.1 %collective-permute-start.20 = (bf16[128,512]{1,0:T(8,128)(2,1)S(1)}, bf16[128,512]{1,0:T(8,128)(2,1)S(1)}, u32[]{:S(2)}, u32[]{:S(2)}) collective-permute-start(bf16[128,512]{1,0:T(8,128)(2,1)S(1)} %collective-permute-done.19), channel_id=1, source_target_pairs={{0,1},{1,0},{2,3},{3,2},{4,5},{5,4},{6,7},{7,6},{8,9},{9,8},{10,11... | collective-permute-start | bytes 393224 | tf_op jit(solution)/shard_map/ppermute | solution.py:15
  47.2 1.5 collective-permute-start.10
  47.7 3.7 %collective-permute-start.15 = (bf16[128,512]{1,0:T(8,128)(2,1)S(1)}, bf16[128,512]{1,0:T(8,128)(2,1)S(1)}, u32[]{:S(2)}, u32[]{:S(2)}) collective-permute-start(bf16[128,512]{1,0:T(8,128)(2,1)S(1)} %collective-permute-done.14), channel_id=1, source_target_pairs={{0,1},{1,0},{2,3},{3,2},{4,5},{5,4},{6,7},{7,6},{8,9},{9,8},{10,11... | collective-permute-start | bytes 393224 | tf_op jit(solution)/shard_map/ppermute | solution.py:15
  51.4 1.3 collective-permute-start.13
  51.5 15.8 %collective-permute-start.17 = (bf16[512,512]{1,0:T(8,128)(2,1)S(1)}, bf16[512,512]{1,0:T(8,128)(2,1)S(1)}, u32[]{:S(2)}, u32[]{:S(2)}) collective-permute-start(bf16[512,512]{1,0:T(8,128)(2,1)S(1)} %slice.102), channel_id=1, source_target_pairs={{0,4},{4,0},{8,12},{12,8},{16,20},{20,16},{24,28},{28,24},{1,5},{5... | collective-permute-start | bytes 1572872 | tf_op jit(solution)/shard_map/ppermute | solution.py:15
  54.4 12.7 %collective-permute-start.16 = (bf16[2,128,896]{2,1,0:T(8,128)(2,1)S(1)}, bf16[2,128,896]{2,1,0:T(8,128)(2,1)S(1)}, u32[]{:S(2)}, u32[]{:S(2)}) collective-permute-start(bf16[2,128,896]{2,1,0:T(8,128)(2,1)S(1)} %bitcast.152), channel_id=1, source_target_pairs={{0,8},{4,12},{8,0},{12,4},{16,24},{20,28},{24,16},{28,20},{1,9},{5... | collective-permute-start | bytes 1376264 | tf_op jit(solution)/shard_map/ppermute | solution.py:15
  67.3 12.8 %collective-permute-start.25 = (bf16[1,128,896]{2,1,0:T(8,128)(2,1)S(1)}, bf16[1,128,896]{2,1,0:T(8,128)(2,1)S(1)}, u32[]{:S(2)}, u32[]{:S(2)}) collective-permute-start(bf16[1,128,896]{2,1,0:T(8,128)(2,1)S(1)} %slice.176), channel_id=1, source_target_pairs={{0,16},{4,20},{8,24},{12,28},{16,0},{20,4},{24,8},{28,12},{1,17},{... | collective-permute-start | bytes 688136 | tf_op jit(solution)/shard_map/ppermute | solution.py:15
  69.3 17.3 %collective-permute-start.18 = (bf16[384,512]{1,0:T(8,128)(2,1)S(1)}, bf16[384,512]{1,0:T(8,128)(2,1)S(1)}, u32[]{:S(2)}, u32[]{:S(2)}) collective-permute-start(bf16[384,512]{1,0:T(8,128)(2,1)S(1)} %copy-done.12), channel_id=1, source_target_pairs={{0,4},{4,0},{8,12},{12,8},{16,20},{20,16},{24,28},{28,24},{1,5},{5... | collective-permute-start | bytes 1179656 | tf_op jit(solution)/shard_map/ppermute | solution.py:15
  81.6 4.9 %collective-permute-start.28 = (f32[896,32]{0,1:T(8,128)S(1)}, f32[896,32]{0,1:T(8,128)S(1)}, u32[]{:S(2)}, u32[]{:S(2)}) collective-permute-start(f32[896,32]{0,1:T(8,128)S(1)} %fusion.80), channel_id=1, source_target_pairs={{0,4},{4,0},{8,12},{12,8},{16,20},{20,16},{24,28},{28,24},{1,5},{5... | collective-permute-start | bytes 344072 | tf_op jit(solution)/shard_map/ppermute | solution.py:15
  86.5 7.4 %collective-permute-start.29 = (f32[896,32]{0,1:T(8,128)S(1)}, f32[896,32]{0,1:T(8,128)S(1)}, u32[]{:S(2)}, u32[]{:S(2)}) collective-permute-start(f32[896,32]{0,1:T(8,128)S(1)} %add.152), channel_id=1, source_target_pairs={{0,8},{4,12},{8,0},{12,4},{16,24},{20,28},{24,16},{28,20},{1,9},{5... | collective-permute-start | bytes 344072 | tf_op jit(solution)/shard_map/ppermute | solution.py:15
  87.6 14.0 %collective-permute-start.23 = (bf16[2,128,896]{2,1,0:T(8,128)(2,1)S(1)}, bf16[2,128,896]{2,1,0:T(8,128)(2,1)S(1)}, u32[]{:S(2)}, u32[]{:S(2)}) collective-permute-start(bf16[2,128,896]{2,1,0:T(8,128)(2,1)S(1)} %bitcast.151), channel_id=1, source_target_pairs={{0,8},{4,12},{8,0},{12,4},{16,24},{20,28},{24,16},{28,20},{1,9},{5... | collective-permute-start | bytes 1376264 | tf_op jit(solution)/shard_map/ppermute | solution.py:15
  93.9 6.8 %collective-permute-start.30 = (f32[896,32]{0,1:T(8,128)S(1)}, f32[896,32]{0,1:T(8,128)S(1)}, u32[]{:S(2)}, u32[]{:S(2)}) collective-permute-start(f32[896,32]{0,1:T(8,128)S(1)} %add.153), channel_id=1, source_target_pairs={{0,16},{4,20},{8,24},{12,28},{16,0},{20,4},{24,8},{28,12},{1,17},{... | collective-permute-start | bytes 344072 | tf_op jit(solution)/shard_map/ppermute | solution.py:15
  101.7 11.5 %collective-permute-start.24 = (bf16[1,128,896]{2,1,0:T(8,128)(2,1)S(1)}, bf16[1,128,896]{2,1,0:T(8,128)(2,1)S(1)}, u32[]{:S(2)}, u32[]{:S(2)}) collective-permute-start(bf16[1,128,896]{2,1,0:T(8,128)(2,1)S(1)} %slice.177), channel_id=1, source_target_pairs={{0,16},{4,20},{8,24},{12,28},{16,0},{20,4},{24,8},{28,12},{1,17},{... | collective-permute-start | bytes 688136 | tf_op jit(solution)/shard_map/ppermute | solution.py:15
  116.9 13.7 %collective-permute-start.31 = (bf16[1,128,896]{2,1,0:T(8,128)(2,1)S(1)}, bf16[1,128,896]{2,1,0:T(8,128)(2,1)}, u32[]{:S(2)}, u32[]{:S(2)}) collective-permute-start(bf16[1,128,896]{2,1,0:T(8,128)(2,1)S(1)} %bitcast.139), channel_id=1, source_target_pairs={{0,16},{4,20},{8,24},{12,28},{16,0},{20,4},{24,8},{28,12},{1,17},{... | collective-permute-start | bytes 688136 | tf_op jit(solution)/shard_map/ppermute | solution.py:15
  118.1 5.3 %collective-permute-start.42 = (f32[544,32]{0,1:T(8,128)S(1)}, f32[544,32]{0,1:T(8,128)S(1)}, u32[]{:S(2)}, u32[]{:S(2)}) collective-permute-start(f32[544,32]{0,1:T(8,128)S(1)} %fusion.76), channel_id=1, source_target_pairs={{0,2},{1,3},{2,0},{3,1},{4,6},{5,7},{6,4},{7,5},{8,10},{9,11},{10,... | collective-permute-start | bytes 208904 | tf_op jit(solution)/shard_map/ppermute | solution.py:15
  123.5 4.5 %collective-permute-start.43 = (f32[544,32]{0,1:T(8,128)S(1)}, f32[544,32]{0,1:T(8,128)S(1)}, u32[]{:S(2)}, u32[]{:S(2)}) collective-permute-start(f32[544,32]{0,1:T(8,128)S(1)} %add.165), channel_id=1, source_target_pairs={{0,4},{4,0},{8,12},{12,8},{16,20},{20,16},{24,28},{28,24},{1,5},{5... | collective-permute-start | bytes 208904 | tf_op jit(solution)/shard_map/ppermute | solution.py:15
  128.0 6.2 %collective-permute-start.44 = (f32[544,32]{0,1:T(8,128)S(1)}, f32[544,32]{0,1:T(8,128)S(1)}, u32[]{:S(2)}, u32[]{:S(2)}) collective-permute-start(f32[544,32]{0,1:T(8,128)S(1)} %add.166), channel_id=1, source_target_pairs={{0,8},{4,12},{8,0},{12,4},{16,24},{20,28},{24,16},{28,20},{1,9},{5... | collective-permute-start | bytes 208904 | tf_op jit(solution)/shard_map/ppermute | solution.py:15
  134.2 27.5 %collective-permute-start.32 = (bf16[256,512]{1,0:T(8,128)(2,1)}, bf16[256,512]{1,0:T(8,128)(2,1)}, u32[]{:S(2)}, u32[]{:S(2)}) collective-permute-start(bf16[256,512]{1,0:T(8,128)(2,1)} %get-tuple-element.80), channel_id=1, source_target_pairs={{0,1},{1,0},{2,3},{3,2},{4,5},{5,4},{6,7},{7,6},{8,9},{9,8},{10,11... | collective-permute-start | bytes 786440 | tf_op jit(solution)/shard_map/ppermute | solution.py:15
  134.3 6.7 %collective-permute-start.45 = (f32[544,32]{0,1:T(8,128)S(1)}, f32[544,32]{0,1:T(8,128)S(1)}, u32[]{:S(2)}, u32[]{:S(2)}) collective-permute-start(f32[544,32]{0,1:T(8,128)S(1)} %add.167), channel_id=1, source_target_pairs={{0,16},{4,20},{8,24},{12,28},{16,0},{20,4},{24,8},{28,12},{1,17},{... | collective-permute-start | bytes 208904 | tf_op jit(solution)/shard_map/ppermute | solution.py:15
  136.5 22.4 %collective-permute-start.35 = (bf16[2,128,896]{2,1,0:T(8,128)(2,1)}, bf16[2,128,896]{2,1,0:T(8,128)(2,1)}, u32[]{:S(2)}, u32[]{:S(2)}) collective-permute-start(bf16[2,128,896]{2,1,0:T(8,128)(2,1)} %pad_maximum_fusion.3), channel_id=1, source_target_pairs={{0,8},{4,12},{8,0},{12,4},{16,24},{20,28},{24,16},{28,20},{1,9},{5... | collective-permute-start | bytes 1376264 | tf_op jit(solution)/shard_map/ppermute | solution.py:15
  148.7 9.2 %collective-permute-start.46 = (f32[896,32]{0,1:T(8,128)S(1)}, f32[896,32]{0,1:T(8,128)}, u32[]{:S(2)}, u32[]{:S(2)}) collective-permute-start(f32[896,32]{0,1:T(8,128)S(1)} %fusion.49), channel_id=1, source_target_pairs={{0,4},{4,0},{8,12},{12,8},{16,20},{20,16},{24,28},{28,24},{1,5},{5... | collective-permute-start | bytes 344072 | tf_op jit(solution)/shard_map/ppermute | solution.py:15
  158.8 11.0 %collective-permute-start.47 = (f32[896,32]{0,1:T(8,128)S(1)}, f32[896,32]{0,1:T(8,128)S(1)}, u32[]{:S(2)}, u32[]{:S(2)}) collective-permute-start(f32[896,32]{0,1:T(8,128)S(1)} %add.169), channel_id=1, source_target_pairs={{0,8},{4,12},{8,0},{12,4},{16,24},{20,28},{24,16},{28,20},{1,9},{5... | collective-permute-start | bytes 344072 | tf_op jit(solution)/shard_map/ppermute | solution.py:15
  161.7 4.5 %collective-permute-start.36 = (bf16[256,512]{1,0:T(8,128)(2,1)S(1)}, bf16[256,512]{1,0:T(8,128)(2,1)S(1)}, u32[]{:S(2)}, u32[]{:S(2)}) collective-permute-start(bf16[256,512]{1,0:T(8,128)(2,1)S(1)} %get-tuple-element.82), channel_id=1, source_target_pairs={{0,1},{1,0},{2,3},{3,2},{4,5},{5,4},{6,7},{7,6},{8,9},{9,8},{10,11... | collective-permute-start | bytes 786440 | tf_op jit(solution)/shard_map/ppermute | solution.py:15
  163.2 10.2 %collective-permute-start.33 = (bf16[128,512]{1,0:T(8,128)(2,1)S(1)}, bf16[128,512]{1,0:T(8,128)(2,1)S(1)}, u32[]{:S(2)}, u32[]{:S(2)}) collective-permute-start(bf16[128,512]{1,0:T(8,128)(2,1)S(1)} %get-tuple-element.58), channel_id=1, source_target_pairs={{0,16},{4,20},{8,24},{12,28},{16,0},{20,4},{24,8},{28,12},{1,17},{... | collective-permute-start | bytes 393224 | tf_op jit(solution)/shard_map/ppermute | solution.py:15
  166.3 9.7 %collective-permute-start.37 = (bf16[128,512]{1,0:T(8,128)(2,1)S(1)}, bf16[128,512]{1,0:T(8,128)(2,1)S(1)}, u32[]{:S(2)}, u32[]{:S(2)}) collective-permute-start(bf16[128,512]{1,0:T(8,128)(2,1)S(1)} %get-tuple-element.57), channel_id=1, source_target_pairs={{0,8},{4,12},{8,0},{12,4},{16,24},{20,28},{24,16},{28,20},{1,9},{5... | collective-permute-start | bytes 393224 | tf_op jit(solution)/shard_map/ppermute | solution.py:15
  166.4 11.4 %collective-permute-start.38 = (bf16[128,512]{1,0:T(8,128)(2,1)S(1)}, bf16[128,512]{1,0:T(8,128)(2,1)S(1)}, u32[]{:S(2)}, u32[]{:S(2)}) collective-permute-start(bf16[128,512]{1,0:T(8,128)(2,1)S(1)} %get-tuple-element.56), channel_id=1, source_target_pairs={{0,24},{4,28},{8,16},{12,20},{16,8},{20,12},{24,0},{28,4},{1,25},{... | collective-permute-start | bytes 393224 | tf_op jit(solution)/shard_map/ppermute | solution.py:15
  169.8 13.5 %collective-permute-start.48 = (f32[896,32]{0,1:T(8,128)S(1)}, f32[896,32]{0,1:T(8,128)S(1)}, u32[]{:S(2)}, u32[]{:S(2)}) collective-permute-start(f32[896,32]{0,1:T(8,128)S(1)} %add.170), channel_id=1, source_target_pairs={{0,16},{4,20},{8,24},{12,28},{16,0},{20,4},{24,8},{28,12},{1,17},{... | collective-permute-start | bytes 344072 | tf_op jit(solution)/shard_map/ppermute | solution.py:15
  173.5 10.0 %collective-permute-start.34 = (bf16[1,128,512]{2,1,0:T(8,128)(2,1)S(1)}, bf16[1,128,512]{2,1,0:T(8,128)(2,1)S(1)}, u32[]{:S(2)}, u32[]{:S(2)}) collective-permute-start(bf16[1,128,512]{2,1,0:T(8,128)(2,1)S(1)} %fusion.45), channel_id=1, source_target_pairs={{0,2},{1,3},{2,0},{3,1},{4,6},{5,7},{6,4},{7,5},{8,10},{9,11},{10,... | collective-permute-start | bytes 393224 | tf_op jit(solution)/shard_map/ppermute | solution.py:15
  177.8 5.7 %collective-permute-start.39 = (bf16[1,128,512]{2,1,0:T(8,128)(2,1)S(1)}, bf16[1,128,512]{2,1,0:T(8,128)(2,1)S(1)}, u32[]{:S(2)}, u32[]{:S(2)}) collective-permute-start(bf16[1,128,512]{2,1,0:T(8,128)(2,1)S(1)} %fusion.43), channel_id=1, source_target_pairs={{0,2},{1,3},{2,0},{3,1},{4,6},{5,7},{6,4},{7,5},{8,10},{9,11},{10,... | collective-permute-start | bytes 393224 | tf_op jit(solution)/shard_map/ppermute | solution.py:15
  183.7 2.3 %collective-permute-start.40 = (bf16[128,512]{1,0:T(8,128)(2,1)S(1)}, bf16[128,512]{1,0:T(8,128)(2,1)S(1)}, u32[]{:S(2)}, u32[]{:S(2)}) collective-permute-start(bf16[128,512]{1,0:T(8,128)(2,1)S(1)} %get-tuple-element.39), channel_id=1, source_target_pairs={{0,1},{1,0},{2,3},{3,2},{4,5},{5,4},{6,7},{7,6},{8,9},{9,8},{10,11... | collective-permute-start | bytes 393224 | tf_op jit(solution)/shard_map/ppermute | solution.py:15
  (20 other events, 239.1 us)

commit v3 on v2

v3 whole, which is shorter than its diff:
```python
import math

import jax
import jax.numpy as jnp
from jax import lax
from jax.experimental import pallas as pl
from jax.experimental.pallas import tpu as pltpu
from jax.sharding import PartitionSpec as P

BF = jnp.bfloat16
F32 = jnp.float32
HIGHEST = lax.Precision.HIGHEST


def flip(arr, axis, mask):
    size = lax.axis_size(axis)
    return lax.ppermute(arr, axis, [(i, i ^ mask) for i in range(size)])


def bits_of(size):
    return [1 << b for b in range(size.bit_length() - 1)]


def dot(a, b, dims=((1,), (0,)), precision=None):
    return lax.dot_general(a, b, (dims, ((), ())), preferred_element_type=F32, precision=precision)


def factor_kernel(up_ref, down_ref, up_out, down_out):
    rank = up_ref.shape[0]
    row_id = lax.broadcasted_iota(jnp.int32, (rank, 2 * rank), 0)
    col_id = lax.broadcasted_iota(jnp.int32, (rank, 2 * rank), 1)
    eye = (row_id + rank == col_id).astype(F32)
    state = [
        eye + jnp.concatenate([ref[...], jnp.zeros((rank, rank), F32)], axis=1)
        for ref in (up_ref, down_ref)
    ]
    for j in range(rank):
        for n in range(2):
            aug = state[n]
            root = lax.rsqrt(aug[j : j + 1, j : j + 1])
            row = aug[j : j + 1, :] * root
            col = aug[:, j : j + 1] * root
            state[n] = jnp.where(row_id > j, aug - col * row, jnp.where(row_id == j, row, aug))
    up_out[...] = state[0][:, rank:]
    down_out[...] = state[1][:, rank:]


def inverse_factors(up_gram, down_gram):
    shape = jax.ShapeDtypeStruct(up_gram.shape, F32)
    return pl.pallas_call(
        factor_kernel,
        out_shape=(shape, shape),
        name="inverse_factors",
        cost_estimate=pl.CostEstimate(flops=10**6, bytes_accessed=20000, transcendentals=64),
    )(up_gram, down_gram)


class Order:
    def __init__(self):
        self.last = None

    def __call__(self, arr):
        if self.last is not None:
            arr, self.last = lax.optimization_barrier((arr, self.last))
        self.last = arr
        return arr


def tie(*arrs):
    return lax.optimization_barrier(arrs)


def split_half(arr, half):
    width = arr.shape[1] // 2
    lo, hi = arr[:, :width], arr[:, width:]
    return jnp.where(half == 0, lo, hi), jnp.where(half == 0, hi, lo)


def shards(tokens, out_grad, up_weight, down_weight, up_accum, down_accum, up_q, down_q):
    replicas, columns = lax.axis_size("dp"), lax.axis_size("tensor")
    dp_i, t_i = lax.axis_index("dp"), lax.axis_index("tensor")
    x_i, z_i = dp_i % 2, dp_i // 2
    core = t_i % 2
    zcount = replicas // 2
    zbits, tbits, dbits = bits_of(zcount), bits_of(columns), bits_of(replicas)
    rows = tokens.shape[0]
    window = up_accum.shape[1]
    scale = 1.0 / math.sqrt(rows)
    half = core ^ x_i
    zrel = z_i ^ t_i
    wait = Order()

    def send_z(blocks):
        kept = []
        for k in range(blocks.shape[0]):
            piece = lax.dynamic_index_in_dim(blocks, zrel ^ k, 0, keepdims=False)
            kept.append(piece if k == 0 else flip(piece, "dp", 2 * k))
        return kept

    ucut = (up_weight.shape[0] * 3 // 8 + 63) // 64 * 64
    dcut = (down_weight.shape[0] // 2 + 127) // 128 * 128
    up_a = flip(up_weight[:ucut], "dp", 1)
    mine, swap = split_half(tokens, half)
    tok_blocks = [mine, wait(flip(swap, "tensor", 1))]
    got = flip(jnp.stack(tok_blocks), "tensor", tbits[1])
    grad_in, tok_win, grad_win, wait.last = tie(
        out_grad, tokens[:, :window], out_grad[:, :window], wait.last
    )
    mine, swap = split_half(grad_in, half)
    swap = flip(swap, "tensor", 1)
    windows = jnp.stack([tok_win, grad_win])
    windows = jnp.where(t_i == 0, windows, jnp.zeros_like(windows))
    win_got = lax.ppermute(windows, "tensor", [(0, 1)])
    grad_blocks = [mine, wait(swap)]
    for mask in tbits[1:]:
        if mask > tbits[1]:
            got = flip(jnp.stack(tok_blocks), "tensor", mask)
        got = wait(got)
        tok_blocks = tok_blocks + [got[n] for n in range(len(tok_blocks))]
    tok_keep = send_z(jnp.stack(tok_blocks))
    up_a = wait(up_a)
    up_b_in, up_a = tie(up_weight[ucut:], up_a)
    up_b = flip(up_b_in, "dp", 1)
    windows = windows + wait(win_got)
    grad_got = flip(jnp.stack(grad_blocks), "tensor", tbits[1])
    win_got = lax.ppermute(windows, "tensor", [(0, 2), (1, 3)])
    tok_keep = [tok_keep[0]] + [wait(piece) for piece in tok_keep[1:]]
    for mask in tbits[1:]:
        if mask > tbits[1]:
            grad_got = flip(jnp.stack(grad_blocks), "tensor", mask)
        grad_got = wait(grad_got)
        grad_blocks = grad_blocks + [grad_got[n] for n in range(len(grad_blocks))]
    grad_keep = send_z(jnp.stack(grad_blocks))
    windows = windows + wait(win_got)
    for mask in tbits[2:]:
        windows = windows + wait(
            lax.ppermute(windows, "tensor", [(i, i + mask) for i in range(mask)])
        )
    tok_win, grad_win = windows[0], windows[1]
    up_b = wait(up_b)
    down_a_in, up_b = tie(down_weight[:dcut], up_b)
    down_a = flip(down_a_in, "dp", 1)
    up_other = jnp.concatenate([up_a, up_b])

    def other_halves(kept):
        got = [flip(piece, "tensor", 1) for piece in kept]
        return [wait(piece) for piece in got]

    def partial(kept, other, own_w, par_w, dims):
        def part_of(ks):
            a = jnp.concatenate([jnp.where(core == 0, kept[k], other[k]) for k in ks])
            b = jnp.concatenate([jnp.where(core == 0, other[k], kept[k]) for k in ks])
            return (dot(a, own_w, dims) + dot(b, par_w, dims)).reshape(len(ks), rows, -1)

        return part_of

    odd = [k for k in range(zcount) if k & 1]
    even = [k for k in range(zcount) if not k & 1]

    def later_stages(acc):
        ks = even
        for bit in zbits[1:]:
            sel = [n for n, k in enumerate(ks) if k & bit]
            stay = [n for n, k in enumerate(ks) if not k & bit]
            send = jnp.stack([acc[n] for n in sel]).astype(BF)
            acc = jnp.stack([acc[n] for n in stay]) + wait(flip(send, "dp", 2 * bit)).astype(F32)
            ks = [ks[n] for n in stay]
        return acc[0]

    tok_other = other_halves(tok_keep)
    part_of = partial(tok_keep, tok_other, up_weight, up_other, ((1,), (0,)))
    pre_got = flip(part_of(odd).astype(BF), "dp", 2)
    pre_acc = part_of(even)
    down_a = wait(down_a)
    down_b_in, down_a = tie(down_weight[dcut:], down_a)
    down_b = flip(down_b_in, "dp", 1)
    grad_keep = [grad_keep[0]] + [wait(piece) for piece in grad_keep[1:]]
    pre_acc = pre_acc + wait(pre_got).astype(F32)
    grad_other = other_halves(grad_keep)
    down_b = wait(down_b)
    down_other = jnp.concatenate([down_a, down_b])
    part_of = partial(grad_keep, grad_other, down_weight, down_other, ((1,), (1,)))
    back_got = flip(part_of(odd).astype(BF), "dp", 2)
    back_acc = part_of(even)
    preact = later_stages(pre_acc)

    squash = jax.nn.sigmoid(preact)
    act_out = (preact * squash).astype(BF)
    slope = squash * (1.0 + preact * (1.0 - squash))
    down_matrix = down_accum[0] + dot(act_out, grad_win, ((0,), (0,))) * scale
    down_sum = dot(down_q, down_matrix, ((0,), (1,)), HIGHEST)
    down_sum = down_sum + wait(flip(down_sum, "dp", 1))
    back_acc = back_acc + wait(back_got).astype(F32)
    for mask in dbits[1:-1]:
        down_sum = down_sum + wait(flip(down_sum, "dp", mask))
    down_got = flip(down_sum, "dp", dbits[-1])
    back_act = later_stages(back_acc)
    hidden = wait((back_act * slope).astype(BF))

    w_dims = ((1,), (1,))
    hid = {0: hidden}
    returned = {}

    def level_after(level):
        return sorted({k | bit for k in level for bit in zbits if bit < (k & -k or zcount)})

    def forward(level):
        return {k: flip(hid[k ^ (k & -k)], "dp", 2 * (k & -k)) for k in level}

    def products(ks):
        lhs = jnp.concatenate([hid[k] for k in ks])
        own = dot(lhs, up_weight, w_dims).astype(BF)
        par = dot(lhs, up_other, w_dims).astype(BF)
        return jnp.where(core == 0, own, par), jnp.where(core == 0, par, own)

    def send_back(ks, mine, got):
        mine = (mine.astype(F32) + got.astype(F32)).astype(BF).reshape(len(ks), rows, -1)
        for n, k in enumerate(ks):
            returned[k] = mine[n] if k == 0 else flip(mine[n], "dp", 2 * k)

    def settle(ks):
        stack = jnp.stack([returned[k] for k in ks])
        order = [
            lax.dynamic_index_in_dim(stack, (zrel >> 1) ^ q, 0, keepdims=False) for q in range(len(ks))
        ]
        for mask in reversed(tbits[1:]):
            n = len(order) // 2
            got = flip(jnp.stack(order[n:]), "tensor", mask)
            order = [(order[i], got[i]) for i in range(n)]
            if mask != tbits[1]:
                order = [(a.astype(F32) + wait(b).astype(F32)).astype(BF) for a, b in order]
        return order[0]

    def add_pair(pair):
        return (pair[0].astype(F32) + wait(pair[1]).astype(F32)).astype(BF)

    first = level_after([0])
    coming = forward(first)
    up_matrix = up_accum[0] + dot(tok_win, hidden, ((0,), (0,))) * scale
    both = dot(up_q, up_matrix, ((0,), (1,)), HIGHEST)
    down_sum = down_sum + wait(down_got)
    down_gram = dot(down_sum, down_sum, ((1,), (1,)), HIGHEST)
    down_term = dot(down_sum, down_matrix, ((1,), (0,)), HIGHEST)
    both = jnp.concatenate([both, down_term, down_gram], axis=1)
    for mask in tbits:
        both = both + wait(flip(both, "tensor", mask))
    both = both + wait(flip(both, "dp", 1))
    for k in reversed(first):
        hid[k] = wait(coming[k])
    group = [0] + first
    level = level_after(first)
    coming = forward(level)
    mine, send = products(group)
    send_got = flip(send, "tensor", 1)
    both_got = flip(both, "dp", dbits[1])
    send_back(group, mine, wait(send_got))
    both = both + wait(both_got)
    for mask in dbits[2:-1]:
        both = both + wait(flip(both, "dp", mask))
    both_got = flip(both, "dp", dbits[-1])
    while level:
        for k in level:
            hid[k] = wait(coming[k])
        mine, send = products(level)
        send_got = flip(send, "tensor", 1)
        after = level_after(level)
        coming = forward(after)
        send_back(level, mine, wait(send_got))
        level = after
    both = both + wait(both_got)
    up_sum, down_term, down_gram = both[:, :window], both[:, window : 2 * window], both[:, 2 * window :]
    up_inv, down_inv = inverse_factors(
        dot(up_sum, up_sum, ((1,), (1,)), HIGHEST), down_gram / replicas
    )

    def scaled(inv, arr):
        return dot(inv, arr, precision=HIGHEST)

    outer = ((0,), (0,))
    up_left = scaled(up_inv, up_sum)
    up_right = dot(up_left, up_matrix, ((1,), (0,)), HIGHEST).astype(BF)
    right_got = flip(up_right, "dp", 1)
    returned.update({k: wait(returned[k]) for k in even[1:]})
    pair_a = settle(even)
    up_right = up_right.astype(F32) + wait(right_got).astype(F32)
    for n, mask in enumerate(dbits[1:]):
        up_right = up_right.astype(BF)
        right_got = flip(up_right, "dp", mask)
        if n == 0:
            returned.update({k: wait(returned[k]) for k in odd})
            pair_b = settle(odd)
        if n == 1:
            sum_a, sum_b = add_pair(pair_a), add_pair(pair_b)
            low = zrel & 1
            got = flip(jnp.where(low == 0, sum_b, sum_a), "tensor", 1)
        up_right = up_right.astype(F32) + wait(right_got).astype(F32)
    own = jnp.where(low == 0, sum_a, sum_b)
    got = wait(got)
    input_grad = jnp.concatenate(
        [jnp.where(half == 0, own, got), jnp.where(half == 0, got, own)], axis=1
    )
    up_right = up_right / replicas
    up_error = up_matrix - dot(up_left, up_right, outer, HIGHEST)
    down_left = scaled(down_inv, down_sum)
    down_right = scaled(down_inv, down_term) / replicas
    down_error = down_matrix - dot(down_left, down_right, outer, HIGHEST)
    up_left, up_right, down_left, down_right = up_left.T, up_right.T, down_left.T, down_right.T
    return (input_grad, up_error[None], up_left, up_right, down_error[None], down_left, down_right)


def solution(mesh):
    return jax.shard_map(
        shards,
        mesh=mesh,
        in_specs=(
            P("dp", "tensor"),
            P("dp", "tensor"),
            P("dp", "tensor"),
            P("tensor", "dp"),
            P("dp", None, "tensor"),
            P("dp", "tensor", None),
            P("tensor", None),
            P(),
        ),
        out_specs=(
            P("dp", "tensor"),
            P("dp", None, "tensor"),
            P(),
            P("tensor", None),
            P("dp", "tensor", None),
            P("tensor", None),
            P(),
        ),
        check_vma=False,
    )
```

time: 189 us -> 169 us (0.89)
  other arithmetic: 23.4 us -> 10.5 us
  Pallas kernels: 0 us -> 4.04 us
  starting transfers between devices: 54.2 us -> 50.8 us
  waiting for transfers between devices: 82 us -> 79.5 us
  local copies, waits for them, and re-layouts: 8.21 us -> 6.04 us
    another operation x19 -> x8, other arithmetic: 17.1 us -> 3.04 us  [the longest x2 1.14 us: shards(): tok_keep = send_z(jnp.stack(tok_blocks))]
    ppermute x47 -> x48, starting transfers between devices: 49.9 us -> 45.2 us  [flip(): return lax.ppermute(arr, axis, [(i, i ^ mask) for i in range(size)])]
    pallas_call x0 -> x1, Pallas kernels: none -> 4.04 us  [inverse_factors(): pl.pallas_call(factor_kernel, out_shape=(shape, shape), name='inverse_fac...]
    ppermute x47 -> x48, waiting for transfers between devices: 80.4 us -> 79.5 us  [flip(): return lax.ppermute(arr, axis, [(i, i ^ mask) for i in range(size)])]
    dot_general x26 -> x25, matrix products: 17 us -> 16.3 us  [dot(): lax.dot_general(a, b, (dims, ((), ())), preferred_element_type=F32, preci...]
  transfers between devices with their start and end apart: 49 -> 50, of which waited for: 23 -> 24; matrix products, arithmetic and copies ran while one was open for 22% -> 15% of each run, Pallas kernels for 0% -> 2%
where the time goes in v3:
time: 169 us
  waiting for transfers between devices  79.5 us (47%)
  starting transfers between devices  50.8 us (30%)
  matrix products  16.3 us (10%)
  other arithmetic  10.5 us (6%)
  local copies, waits for them, and re-layouts  6.04 us (4%)
  Pallas kernels  4.04 us (2%)
    ppermute x48, waiting for transfers between devices, flip(): return lax.ppermute(arr, axis, [(i, i ^ mask) for i in range(size)])  79.5 us
    ppermute x48, starting transfers between devices, flip(): return lax.ppermute(arr, axis, [(i, i ^ mask) for i in range(size)])  45.2 us
    dot_general x25, matrix products, dot(): lax.dot_general(a, b, (dims, ((), ())), preferred_element_type=F32, preci...  16.3 us
    pallas_call x1, Pallas kernels, inverse_factors(): pl.pallas_call(factor_kernel, out_shape=(shape, shape), name='inverse_fac...  4.04 us
    ppermute x1, starting transfers between devices, shards(): win_got = lax.ppermute(windows, 'tensor', [(0, 2), (1, 3)])  3.45 us
  transfers between devices with their start and end apart: 50, of which 24 were waited for; matrix products, arithmetic and copies ran while one was open for 15% of the time, Pallas kernels for 2%

profile of v3, /device:TPU:0, one launch (start us, length us, event | category | flops | bytes accessed | tf_op | source)
XLA Modules:
  0.0 168.5 jit_solution(7609498154822299605)
XLA Ops:
  3.3 2.9 %collective-permute-start.3 = (bf16[2,128,512]{2,1,0:T(8,128)(2,1)S(1)}, bf16[2,128,512]{2,1,0:T(8,128)(2,1)S(1)}, u32[]{:S(2)}, u32[]{:S(2)}) collective-permute-start(bf16[2,128,512]{2,1,0:T(8,128)(2,1)S(1)} %pad_maximum_fusion.3), channel_id=1, source_target_pairs={{0,2},{1,3},{2,0},{3,1},{4,6},{5,7},{6,4},{7,5},{8,10},{9,11},{10,... | collective-permute-start | bytes 786440 | tf_op jit(solution)/shard_map/ppermute | solution.py:17
  7.1 1.5 collective-permute-start.8
  8.6 2.1 %collective-permute-start.7 = (bf16[2,128,256]{2,1,0:T(8,128)(2,1)S(1)}, bf16[2,128,256]{2,1,0:T(8,128)(2,1)S(1)}, u32[]{:S(2)}, u32[]{:S(2)}) collective-permute-start(bf16[2,128,256]{2,1,0:T(8,128)(2,1)S(1)} %maximum_select_fusion), channel_id=1, source_target_pairs={{0,1},{4,5},{8,9},{12,13},{16,17},{20,21},{24,25},{28,29}} | collective-permute-start | bytes 393224 | tf_op jit(solution)/shard_map/ppermute | solution.py:113
  11.5 1.4 collective-permute-done.3
  13.7 3.8 %collective-permute-start.4 = (bf16[128,512]{1,0:T(8,128)(2,1)}, bf16[128,512]{1,0:T(8,128)(2,1)}, u32[]{:S(2)}, u32[]{:S(2)}) collective-permute-start(bf16[128,512]{1,0:T(8,128)(2,1)} %get-tuple-element.137), channel_id=1, source_target_pairs={{0,24},{4,28},{8,16},{12,20},{16,8},{20,12},{24,0},{28,4},{1,25},{... | collective-permute-start | bytes 393224 | tf_op jit(solution)/shard_map/ppermute | solution.py:17
  17.9 1.6 collective-permute-start.6
  20.2 3.5 %collective-permute-start.13 = (bf16[2,128,256]{2,1,0:T(8,128)(2,1)}, bf16[2,128,256]{2,1,0:T(8,128)(2,1)}, u32[]{:S(2)}, u32[]{:S(2)}) collective-permute-start(bf16[2,128,256]{2,1,0:T(8,128)(2,1)} %fusion.109), channel_id=1, source_target_pairs={{0,2},{1,3},{4,6},{5,7},{8,10},{9,11},{12,14},{13,15},{16,18},{17,... | collective-permute-start | bytes 393224 | tf_op jit(solution)/shard_map/ppermute | solution.py:126
  24.5 1.2 collective-permute-done.6
  26.4 1.5 collective-permute-start.12
  32.0 8.0 %collective-permute-done.12 = bf16[320,896]{1,0:T(8,128)(2,1)S(1)} collective-permute-done((bf16[320,896]{1,0:T(8,128)(2,1)}, bf16[320,896]{1,0:T(8,128)(2,1)S(1)}, u32[]{:S(2)}, u32[]{:S(2)}) %collective-permute-start.12) | collective-permute-done | bytes 573472 | tf_op jit(solution)/shard_map/ppermute | solution.py:17
  40.0 1.8 %collective-permute-start.18 = (bf16[128,512]{1,0:T(8,128)(2,1)S(1)}, bf16[128,512]{1,0:T(8,128)(2,1)S(1)}, u32[]{:S(2)}, u32[]{:S(2)}) collective-permute-start(bf16[128,512]{1,0:T(8,128)(2,1)S(1)} %get-tuple-element.132), channel_id=1, source_target_pairs={{0,16},{4,20},{8,24},{12,28},{16,0},{20,4},{24,8},{28,12},{1,17},{... | collective-permute-start | bytes 393224 | tf_op jit(solution)/shard_map/ppermute | solution.py:17
  41.8 2.1 %collective-permute-start.19 = (bf16[128,512]{1,0:T(8,128)(2,1)S(1)}, bf16[128,512]{1,0:T(8,128)(2,1)S(1)}, u32[]{:S(2)}, u32[]{:S(2)}) collective-permute-start(bf16[128,512]{1,0:T(8,128)(2,1)S(1)} %get-tuple-element.131), channel_id=1, source_target_pairs={{0,8},{4,12},{8,0},{12,4},{16,24},{20,28},{24,16},{28,20},{1,9},{5... | collective-permute-start | bytes 393224 | tf_op jit(solution)/shard_map/ppermute | solution.py:17
  44.0 1.8 %collective-permute-start.20 = (bf16[512,512]{1,0:T(8,128)(2,1)S(1)}, bf16[512,512]{1,0:T(8,128)(2,1)S(1)}, u32[]{:S(2)}, u32[]{:S(2)}) collective-permute-start(bf16[512,512]{1,0:T(8,128)(2,1)S(1)} %slice.87), channel_id=1, source_target_pairs={{0,4},{4,0},{8,12},{12,8},{16,20},{20,16},{24,28},{28,24},{1,5},{5... | collective-permute-start | bytes 1572872 | tf_op jit(solution)/shard_map/ppermute | solution.py:17
  49.2 9.1 %collective-permute-done.20 = bf16[512,512]{1,0:T(8,128)(2,1)S(1)} collective-permute-done((bf16[512,512]{1,0:T(8,128)(2,1)S(1)}, bf16[512,512]{1,0:T(8,128)(2,1)S(1)}, u32[]{:S(2)}, u32[]{:S(2)}) %collective-permute-start.20) | collective-permute-done | bytes 524320 | tf_op jit(solution)/shard_map/ppermute | solution.py:17
  58.3 1.1 collective-permute-start.17
  60.4 4.8 %collective-permute-done.17 = bf16[128,512]{1,0:T(8,128)(2,1)S(1)} collective-permute-done((bf16[128,512]{1,0:T(8,128)(2,1)S(1)}, bf16[128,512]{1,0:T(8,128)(2,1)S(1)}, u32[]{:S(2)}, u32[]{:S(2)}) %collective-permute-start.17) | collective-permute-done | bytes 131104 | tf_op jit(solution)/shard_map/ppermute | solution.py:17
  65.3 1.8 %collective-permute-start.23 = (bf16[384,512]{1,0:T(8,128)(2,1)S(1)}, bf16[384,512]{1,0:T(8,128)(2,1)S(1)}, u32[]{:S(2)}, u32[]{:S(2)}) collective-permute-start(bf16[384,512]{1,0:T(8,128)(2,1)S(1)} %slice.88), channel_id=1, source_target_pairs={{0,4},{4,0},{8,12},{12,8},{16,20},{20,16},{24,28},{28,24},{1,5},{5... | collective-permute-start | bytes 1179656 | tf_op jit(solution)/shard_map/ppermute | solution.py:17
  67.2 2.0 %collective-permute-start.26 = (bf16[1,128,896]{2,1,0:T(8,128)(2,1)S(1)}, bf16[1,128,896]{2,1,0:T(8,128)(2,1)S(1)}, u32[]{:S(2)}, u32[]{:S(2)}) collective-permute-start(bf16[1,128,896]{2,1,0:T(8,128)(2,1)S(1)} %slice.152), channel_id=1, source_target_pairs={{0,16},{4,20},{8,24},{12,28},{16,0},{20,4},{24,8},{28,12},{1,17},{... | collective-permute-start | bytes 688136 | tf_op jit(solution)/shard_map/ppermute | solution.py:17
  70.3 6.5 %collective-permute-done.23 = bf16[384,512]{1,0:T(8,128)(2,1)S(1)} collective-permute-done((bf16[384,512]{1,0:T(8,128)(2,1)S(1)}, bf16[384,512]{1,0:T(8,128)(2,1)S(1)}, u32[]{:S(2)}, u32[]{:S(2)}) %collective-permute-start.23) | collective-permute-done | bytes 393248 | tf_op jit(solution)/shard_map/ppermute | solution.py:17
  77.3 1.4 collective-permute-start.25
  78.7 2.2 %collective-permute-done.26 = bf16[1,128,896]{2,1,0:T(8,128)(2,1)S(1)} collective-permute-done((bf16[1,128,896]{2,1,0:T(8,128)(2,1)S(1)}, bf16[1,128,896]{2,1,0:T(8,128)(2,1)S(1)}, u32[]{:S(2)}, u32[]{:S(2)}) %collective-permute-start.26) | collective-permute-done | bytes 229408 | tf_op jit(solution)/shard_map/ppermute | solution.py:17
  82.9 4.1 %collective-permute-done.27 = f32[32,896]{1,0:T(8,128)S(1)} collective-permute-done((f32[32,896]{1,0:T(8,128)S(1)}, f32[32,896]{1,0:T(8,128)S(1)}, u32[]{:S(2)}, u32[]{:S(2)}) %collective-permute-start.27) | collective-permute-done | bytes 114720 | tf_op jit(solution)/shard_map/ppermute | solution.py:17
  87.0 3.6 %collective-permute-done.25 = bf16[2,128,896]{2,1,0:T(8,128)(2,1)S(1)} collective-permute-done((bf16[2,128,896]{2,1,0:T(8,128)(2,1)S(1)}, bf16[2,128,896]{2,1,0:T(8,128)(2,1)S(1)}, u32[]{:S(2)}, u32[]{:S(2)}) %collective-permute-start.25) | collective-permute-done | bytes 458784 | tf_op jit(solution)/shard_map/ppermute | solution.py:17
  90.7 1.4 collective-permute-start.28
  92.5 6.0 %collective-permute-done.29 = f32[32,896]{1,0:T(8,128)S(1)} collective-permute-done((f32[32,896]{1,0:T(8,128)S(1)}, f32[32,896]{1,0:T(8,128)S(1)}, u32[]{:S(2)}, u32[]{:S(2)}) %collective-permute-start.29) | collective-permute-done | bytes 114720 | tf_op jit(solution)/shard_map/ppermute | solution.py:17
  98.5 2.7 %collective-permute-start.32 = (f32[32,896]{1,0:T(8,128)S(1)}, f32[32,896]{1,0:T(8,128)S(1)}, u32[]{:S(2)}, u32[]{:S(2)}) collective-permute-start(f32[32,896]{1,0:T(8,128)S(1)} %add.146), channel_id=1, source_target_pairs={{0,16},{4,20},{8,24},{12,28},{16,0},{20,4},{24,8},{28,12},{1,17},{... | collective-permute-start | bytes 344072 | tf_op jit(solution)/shard_map/ppermute | solution.py:17
  101.2 3.1 %collective-permute-done.28 = bf16[1,128,896]{2,1,0:T(8,128)(2,1)S(1)} collective-permute-done((bf16[1,128,896]{2,1,0:T(8,128)(2,1)S(1)}, bf16[1,128,896]{2,1,0:T(8,128)(2,1)S(1)}, u32[]{:S(2)}, u32[]{:S(2)}) %collective-permute-start.28) | collective-permute-done | bytes 229408 | tf_op jit(solution)/shard_map/ppermute | solution.py:17
  104.5 3.4 %collective-permute-done.32 = f32[32,896]{1,0:T(8,128)S(1)} collective-permute-done((f32[32,896]{1,0:T(8,128)S(1)}, f32[32,896]{1,0:T(8,128)S(1)}, u32[]{:S(2)}, u32[]{:S(2)}) %collective-permute-start.32) | collective-permute-done | bytes 114720 | tf_op jit(solution)/shard_map/ppermute | solution.py:17
  110.1 1.8 %collective-permute-start.31 = (bf16[128,896]{1,0:T(8,128)(2,1)S(1)}, bf16[128,896]{1,0:T(8,128)(2,1)S(1)}, u32[]{:S(2)}, u32[]{:S(2)}) collective-permute-start(bf16[128,896]{1,0:T(8,128)(2,1)S(1)} %fusion.8), channel_id=1, source_target_pairs={{0,16},{4,20},{8,24},{12,28},{16,0},{20,4},{24,8},{28,12},{1,17},{... | collective-permute-start | bytes 688136 | tf_op jit(solution)/shard_map/ppermute | solution.py:17
  113.0 3.5 %collective-permute-done.34 = f32[32,544]{1,0:T(8,128)S(1)} collective-permute-done((f32[32,544]{1,0:T(8,128)S(1)}, f32[32,544]{1,0:T(8,128)S(1)}, u32[]{:S(2)}, u32[]{:S(2)}) %collective-permute-start.34) | collective-permute-done | bytes 69664 | tf_op jit(solution)/shard_map/ppermute | solution.py:17
  116.5 1.3 collective-permute-start.35
  117.8 3.2 %collective-permute-done.35 = f32[32,544]{1,0:T(8,128)S(1)} collective-permute-done((f32[32,544]{1,0:T(8,128)S(1)}, f32[32,544]{1,0:T(8,128)S(1)}, u32[]{:S(2)}, u32[]{:S(2)}) %collective-permute-start.35) | collective-permute-done | bytes 69664 | tf_op jit(solution)/shard_map/ppermute | solution.py:17
  121.0 2.9 %collective-permute-done.31 = bf16[128,896]{1,0:T(8,128)(2,1)S(1)} collective-permute-done((bf16[128,896]{1,0:T(8,128)(2,1)S(1)}, bf16[128,896]{1,0:T(8,128)(2,1)S(1)}, u32[]{:S(2)}, u32[]{:S(2)}) %collective-permute-start.31) | collective-permute-done | bytes 229408 | tf_op jit(solution)/shard_map/ppermute | solution.py:17
  125.2 1.5 broadcast_select_fusion
  126.8 2.0 %collective-permute-start.40 = (bf16[128,896]{1,0:T(8,128)(2,1)}, bf16[128,896]{1,0:T(8,128)(2,1)S(1)}, u32[]{:S(2)}, u32[]{:S(2)}) collective-permute-start(bf16[128,896]{1,0:T(8,128)(2,1)} %copy-done.9), channel_id=1, source_target_pairs={{0,8},{4,12},{8,0},{12,4},{16,24},{20,28},{24,16},{28,20},{1,9},{5... | collective-permute-start | bytes 688136 | tf_op jit(solution)/shard_map/ppermute | solution.py:17
  128.8 3.2 %collective-permute-done.38 = f32[32,544]{1,0:T(8,128)S(1)} collective-permute-done((f32[32,544]{1,0:T(8,128)S(1)}, f32[32,544]{1,0:T(8,128)S(1)}, u32[]{:S(2)}, u32[]{:S(2)}) %collective-permute-start.38) | collective-permute-done | bytes 69664 | tf_op jit(solution)/shard_map/ppermute | solution.py:17
  132.2 1.1 add_convert_fusion
  133.3 4.4 %collective-permute-done.40 = bf16[128,896]{1,0:T(8,128)(2,1)S(1)} collective-permute-done((bf16[128,896]{1,0:T(8,128)(2,1)}, bf16[128,896]{1,0:T(8,128)(2,1)S(1)}, u32[]{:S(2)}, u32[]{:S(2)}) %collective-permute-start.40) | collective-permute-done | bytes 229408 | tf_op jit(solution)/shard_map/ppermute | solution.py:17
  138.8 2.4 %collective-permute-start.46 = (bf16[128,512]{1,0:T(8,128)(2,1)S(1)}, bf16[128,512]{1,0:T(8,128)(2,1)S(1)}, u32[]{:S(2)}, u32[]{:S(2)}) collective-permute-start(bf16[128,512]{1,0:T(8,128)(2,1)S(1)} %get-tuple-element.140), channel_id=1, source_target_pairs={{0,8},{4,12},{8,0},{12,4},{16,24},{20,28},{24,16},{28,20},{1,9},{5... | collective-permute-start | bytes 393224 | tf_op jit(solution)/shard_map/ppermute | solution.py:17
  142.6 4.0 %inverse_factors.1 = (f32[32,32]{1,0:T(8,128)}, f32[32,32]{1,0:T(8,128)}) custom-call(f32[32,32]{1,0:T(8,128)} %fusion.56.up_ref, f32[32,32]{1,0:T(8,128)} %slice_multiply_fusion.down_ref), custom_call_target="tpu_custom_call" | custom-call | flops 1000000 | bytes 20000 | tf_op jit(solution)/shard_map/inverse_factors/pallas_call | solution.py:50
  149.6 1.2 collective-permute-start.43
  150.8 2.0 %collective-permute-start.45 = (bf16[128,512]{1,0:T(8,128)(2,1)S(1)}, bf16[128,512]{1,0:T(8,128)(2,1)S(1)}, u32[]{:S(2)}, u32[]{:S(2)}) collective-permute-start(bf16[128,512]{1,0:T(8,128)(2,1)S(1)} %add_convert_fusion.1), channel_id=1, source_target_pairs={{0,24},{4,28},{8,16},{12,20},{16,8},{20,12},{24,0},{28,4},{1,25},{... | collective-permute-start | bytes 393224 | tf_op jit(solution)/shard_map/ppermute | solution.py:17
  153.9 1.9 %fusion = f32[1,896,256]{2,1,0:T(8,128)} fusion(f32[896,256]{1,0:T(8,128)S(1)} %copy-done.4, f32[32,896]{1,0:T(8,128)S(1)} %fusion.74, f32[32,256]{1,0:T(8,128)S(1)} %convolution_multiply_fusion.2), kind=kOutput, calls=%fused_computation.1 | convolution fusion | flops 88309760 | bytes 1982464 | tf_op jit(solution)/shard_map/dot_general | solution.py:25
  155.8 2.4 %collective-permute-done.45 = bf16[128,512]{1,0:T(8,128)(2,1)S(1)} collective-permute-done((bf16[128,512]{1,0:T(8,128)(2,1)S(1)}, bf16[128,512]{1,0:T(8,128)(2,1)S(1)}, u32[]{:S(2)}, u32[]{:S(2)}) %collective-permute-start.45) | collective-permute-done | bytes 131104 | tf_op jit(solution)/shard_map/ppermute | solution.py:17
  158.8 1.1 collective-permute-start.47
  160.6 3.3 %collective-permute-done.47 = bf16[1,128,512]{2,1,0:T(8,128)(2,1)S(1)} collective-permute-done((bf16[1,128,512]{2,1,0:T(8,128)(2,1)S(1)}, bf16[1,128,512]{2,1,0:T(8,128)(2,1)S(1)}, u32[]{:S(2)}, u32[]{:S(2)}) %collective-permute-start.47) | collective-permute-done | bytes 131104 | tf_op jit(solution)/shard_map/ppermute | solution.py:17
  164.1 1.1 collective-permute-done.49
  165.9 1.8 %fusion.1 = f32[1,256,896]{2,1,0:T(8,128)} fusion(f32[256,896]{1,0:T(8,128)S(1)} %fusion.2, f32[32,256]{1,0:T(8,128)S(1)} %fusion.54, bf16[32,896]{1,0:T(8,128)(2,1)S(1)} %collective-permute-done.49, bf16[32,896]{1,0:T(8,128)(2,1)S(1)} %add_convert_fusion.2), kind=kOutput, calls=%fused_computation.3 | convolution fusion | flops 88424448 | bytes 1982464 | tf_op jit(solution)/shard_map/dot_general | solution.py:25
  (167 shorter events, 34.6 us)
Async XLA Ops:
  3.3 9.6 %collective-permute-start.3 = (bf16[2,128,512]{2,1,0:T(8,128)(2,1)S(1)}, bf16[2,128,512]{2,1,0:T(8,128)(2,1)S(1)}, u32[]{:S(2)}, u32[]{:S(2)}) collective-permute-start(bf16[2,128,512]{2,1,0:T(8,128)(2,1)S(1)} %pad_maximum_fusion.3), channel_id=1, source_target_pairs={{0,2},{1,3},{2,0},{3,1},{4,6},{5,7},{6,4},{7,5},{8,10},{9,11},{10,... | collective-permute-start | bytes 786440 | tf_op jit(solution)/shard_map/ppermute | solution.py:17
  6.3 4.5 %collective-permute-start.1 = (bf16[128,512]{1,0:T(8,128)(2,1)S(1)}, bf16[128,512]{1,0:T(8,128)(2,1)S(1)}, u32[]{:S(2)}, u32[]{:S(2)}) collective-permute-start(bf16[128,512]{1,0:T(8,128)(2,1)S(1)} %get-tuple-element.162), channel_id=1, source_target_pairs={{0,1},{1,0},{2,3},{3,2},{4,5},{5,4},{6,7},{7,6},{8,9},{9,8},{10,11... | collective-permute-start | bytes 393224 | tf_op jit(solution)/shard_map/ppermute | solution.py:17
  7.1 10.8 %collective-permute-start.8 = (bf16[192,896]{1,0:T(8,128)(2,1)}, bf16[192,896]{1,0:T(8,128)(2,1)}, u32[]{:S(2)}, u32[]{:S(2)}) collective-permute-start(bf16[192,896]{1,0:T(8,128)(2,1)} %slice.85), channel_id=1, source_target_pairs={{0,4},{4,0},{8,12},{12,8},{16,20},{20,16},{24,28},{28,24},{1,5},{5... | collective-permute-start | bytes 1032200 | tf_op jit(solution)/shard_map/ppermute | solution.py:17
  8.6 10.8 %collective-permute-start.7 = (bf16[2,128,256]{2,1,0:T(8,128)(2,1)S(1)}, bf16[2,128,256]{2,1,0:T(8,128)(2,1)S(1)}, u32[]{:S(2)}, u32[]{:S(2)}) collective-permute-start(bf16[2,128,256]{2,1,0:T(8,128)(2,1)S(1)} %maximum_select_fusion), channel_id=1, source_target_pairs={{0,1},{4,5},{8,9},{12,13},{16,17},{20,21},{24,25},{28,29}} | collective-permute-start | bytes 393224 | tf_op jit(solution)/shard_map/ppermute | solution.py:113
  11.5 18.0 %collective-permute-start.2 = (bf16[2,128,512]{2,1,0:T(8,128)(2,1)}, bf16[2,128,512]{2,1,0:T(8,128)(2,1)}, u32[]{:S(2)}, u32[]{:S(2)}) collective-permute-start(bf16[2,128,512]{2,1,0:T(8,128)(2,1)} %pad_maximum_fusion.2), channel_id=1, source_target_pairs={{0,2},{1,3},{2,0},{3,1},{4,6},{5,7},{6,4},{7,5},{8,10},{9,11},{10,... | collective-permute-start | bytes 786440 | tf_op jit(solution)/shard_map/ppermute | solution.py:17
  13.7 15.3 %collective-permute-start.4 = (bf16[128,512]{1,0:T(8,128)(2,1)}, bf16[128,512]{1,0:T(8,128)(2,1)}, u32[]{:S(2)}, u32[]{:S(2)}) collective-permute-start(bf16[128,512]{1,0:T(8,128)(2,1)} %get-tuple-element.137), channel_id=1, source_target_pairs={{0,24},{4,28},{8,16},{12,20},{16,8},{20,12},{24,0},{28,4},{1,25},{... | collective-permute-start | bytes 393224 | tf_op jit(solution)/shard_map/ppermute | solution.py:17
  17.5 11.4 %collective-permute-start.5 = (bf16[128,512]{1,0:T(8,128)(2,1)}, bf16[128,512]{1,0:T(8,128)(2,1)}, u32[]{:S(2)}, u32[]{:S(2)}) collective-permute-start(bf16[128,512]{1,0:T(8,128)(2,1)} %get-tuple-element.136), channel_id=1, source_target_pairs={{0,16},{4,20},{8,24},{12,28},{16,0},{20,4},{24,8},{28,12},{1,17},{... | collective-permute-start | bytes 393224 | tf_op jit(solution)/shard_map/ppermute | solution.py:17
  17.9 7.8 %collective-permute-start.6 = (bf16[128,512]{1,0:T(8,128)(2,1)S(1)}, bf16[128,512]{1,0:T(8,128)(2,1)S(1)}, u32[]{:S(2)}, u32[]{:S(2)}) collective-permute-start(bf16[128,512]{1,0:T(8,128)(2,1)S(1)} %get-tuple-element.135), channel_id=1, source_target_pairs={{0,8},{4,12},{8,0},{12,4},{16,24},{20,28},{24,16},{28,20},{1,9},{5... | collective-permute-start | bytes 393224 | tf_op jit(solution)/shard_map/ppermute | solution.py:17
  20.2 9.4 %collective-permute-start.13 = (bf16[2,128,256]{2,1,0:T(8,128)(2,1)}, bf16[2,128,256]{2,1,0:T(8,128)(2,1)}, u32[]{:S(2)}, u32[]{:S(2)}) collective-permute-start(bf16[2,128,256]{2,1,0:T(8,128)(2,1)} %fusion.109), channel_id=1, source_target_pairs={{0,2},{1,3},{4,6},{5,7},{8,10},{9,11},{12,14},{13,15},{16,18},{17,... | collective-permute-start | bytes 393224 | tf_op jit(solution)/shard_map/ppermute | solution.py:126
  26.4 13.6 %collective-permute-start.12 = (bf16[320,896]{1,0:T(8,128)(2,1)}, bf16[320,896]{1,0:T(8,128)(2,1)S(1)}, u32[]{:S(2)}, u32[]{:S(2)}) collective-permute-start(bf16[320,896]{1,0:T(8,128)(2,1)} %slice.86), channel_id=1, source_target_pairs={{0,4},{4,0},{8,12},{12,8},{16,20},{20,16},{24,28},{28,24},{1,5},{5... | collective-permute-start | bytes 1720328 | tf_op jit(solution)/shard_map/ppermute | solution.py:17
  28.9 12.9 %collective-permute-start.11 = (bf16[128,512]{1,0:T(8,128)(2,1)S(1)}, bf16[128,512]{1,0:T(8,128)(2,1)S(1)}, u32[]{:S(2)}, u32[]{:S(2)}) collective-permute-start(bf16[128,512]{1,0:T(8,128)(2,1)S(1)} %get-tuple-element.134), channel_id=1, source_target_pairs={{0,1},{1,0},{2,3},{3,2},{4,5},{5,4},{6,7},{7,6},{8,9},{9,8},{10,11... | collective-permute-start | bytes 393224 | tf_op jit(solution)/shard_map/ppermute | solution.py:17
  29.0 14.9 %collective-permute-start.15 = (bf16[128,512]{1,0:T(8,128)(2,1)}, bf16[128,512]{1,0:T(8,128)(2,1)S(1)}, u32[]{:S(2)}, u32[]{:S(2)}) collective-permute-start(bf16[128,512]{1,0:T(8,128)(2,1)} %collective-permute-done.5), channel_id=1, source_target_pairs={{0,1},{1,0},{2,3},{3,2},{4,5},{5,4},{6,7},{7,6},{8,9},{9,8},{10,11... | collective-permute-start | bytes 393224 | tf_op jit(solution)/shard_map/ppermute | solution.py:17
  29.5 16.3 %collective-permute-start.14 = (bf16[128,512]{1,0:T(8,128)(2,1)}, bf16[128,512]{1,0:T(8,128)(2,1)S(1)}, u32[]{:S(2)}, u32[]{:S(2)}) collective-permute-start(bf16[128,512]{1,0:T(8,128)(2,1)} %collective-permute-done.4), channel_id=1, source_target_pairs={{0,1},{1,0},{2,3},{3,2},{4,5},{5,4},{6,7},{7,6},{8,9},{9,8},{10,11... | collective-permute-start | bytes 393224 | tf_op jit(solution)/shard_map/ppermute | solution.py:17
  29.6 14.4 %collective-permute-start.10 = (bf16[128,512]{1,0:T(8,128)(2,1)S(1)}, bf16[128,512]{1,0:T(8,128)(2,1)S(1)}, u32[]{:S(2)}, u32[]{:S(2)}) collective-permute-start(bf16[128,512]{1,0:T(8,128)(2,1)S(1)} %copy-done.12), channel_id=1, source_target_pairs={{0,1},{1,0},{2,3},{3,2},{4,5},{5,4},{6,7},{7,6},{8,9},{9,8},{10,11... | collective-permute-start | bytes 393224 | tf_op jit(solution)/shard_map/ppermute | solution.py:17
  40.0 19.9 %collective-permute-start.18 = (bf16[128,512]{1,0:T(8,128)(2,1)S(1)}, bf16[128,512]{1,0:T(8,128)(2,1)S(1)}, u32[]{:S(2)}, u32[]{:S(2)}) collective-permute-start(bf16[128,512]{1,0:T(8,128)(2,1)S(1)} %get-tuple-element.132), channel_id=1, source_target_pairs={{0,16},{4,20},{8,24},{12,28},{16,0},{20,4},{24,8},{28,12},{1,17},{... | collective-permute-start | bytes 393224 | tf_op jit(solution)/shard_map/ppermute | solution.py:17
  41.8 18.0 %collective-permute-start.19 = (bf16[128,512]{1,0:T(8,128)(2,1)S(1)}, bf16[128,512]{1,0:T(8,128)(2,1)S(1)}, u32[]{:S(2)}, u32[]{:S(2)}) collective-permute-start(bf16[128,512]{1,0:T(8,128)(2,1)S(1)} %get-tuple-element.131), channel_id=1, source_target_pairs={{0,8},{4,12},{8,0},{12,4},{16,24},{20,28},{24,16},{28,20},{1,9},{5... | collective-permute-start | bytes 393224 | tf_op jit(solution)/shard_map/ppermute | solution.py:17
  44.0 21.3 %collective-permute-start.9 = (bf16[128,512]{1,0:T(8,128)(2,1)S(1)}, bf16[128,512]{1,0:T(8,128)(2,1)S(1)}, u32[]{:S(2)}, u32[]{:S(2)}) collective-permute-start(bf16[128,512]{1,0:T(8,128)(2,1)S(1)} %get-tuple-element.133), channel_id=1, source_target_pairs={{0,1},{1,0},{2,3},{3,2},{4,5},{5,4},{6,7},{7,6},{8,9},{9,8},{10,11... | collective-permute-start | bytes 393224 | tf_op jit(solution)/shard_map/ppermute | solution.py:17
  44.0 14.3 %collective-permute-start.20 = (bf16[512,512]{1,0:T(8,128)(2,1)S(1)}, bf16[512,512]{1,0:T(8,128)(2,1)S(1)}, u32[]{:S(2)}, u32[]{:S(2)}) collective-permute-start(bf16[512,512]{1,0:T(8,128)(2,1)S(1)} %slice.87), channel_id=1, source_target_pairs={{0,4},{4,0},{8,12},{12,8},{16,20},{20,16},{24,28},{28,24},{1,5},{5... | collective-permute-start | bytes 1572872 | tf_op jit(solution)/shard_map/ppermute | solution.py:17
  47.7 17.6 %collective-permute-start.16 = (bf16[2,128,896]{2,1,0:T(8,128)(2,1)S(1)}, bf16[2,128,896]{2,1,0:T(8,128)(2,1)S(1)}, u32[]{:S(2)}, u32[]{:S(2)}) collective-permute-start(bf16[2,128,896]{2,1,0:T(8,128)(2,1)S(1)} %bitcast.148), channel_id=1, source_target_pairs={{0,8},{4,12},{8,0},{12,4},{16,24},{20,28},{24,16},{28,20},{1,9},{5... | collective-permute-start | bytes 1376264 | tf_op jit(solution)/shard_map/ppermute | solution.py:17
  58.3 7.0 %collective-permute-start.17 = (bf16[128,512]{1,0:T(8,128)(2,1)S(1)}, bf16[128,512]{1,0:T(8,128)(2,1)S(1)}, u32[]{:S(2)}, u32[]{:S(2)}) collective-permute-start(bf16[128,512]{1,0:T(8,128)(2,1)S(1)} %get-tuple-element.130), channel_id=1, source_target_pairs={{0,24},{4,28},{8,16},{12,20},{16,8},{20,12},{24,0},{28,4},{1,25},{... | collective-permute-start | bytes 393224 | tf_op jit(solution)/shard_map/ppermute | solution.py:17
  59.9 9.4 %collective-permute-start.22 = (bf16[128,512]{1,0:T(8,128)(2,1)S(1)}, bf16[128,512]{1,0:T(8,128)(2,1)S(1)}, u32[]{:S(2)}, u32[]{:S(2)}) collective-permute-start(bf16[128,512]{1,0:T(8,128)(2,1)S(1)} %collective-permute-done.19), channel_id=1, source_target_pairs={{0,1},{1,0},{2,3},{3,2},{4,5},{5,4},{6,7},{7,6},{8,9},{9,8},{10,11... | collective-permute-start | bytes 393224 | tf_op jit(solution)/shard_map/ppermute | solution.py:17
  59.9 9.3 %collective-permute-start.21 = (bf16[128,512]{1,0:T(8,128)(2,1)S(1)}, bf16[128,512]{1,0:T(8,128)(2,1)S(1)}, u32[]{:S(2)}, u32[]{:S(2)}) collective-permute-start(bf16[128,512]{1,0:T(8,128)(2,1)S(1)} %collective-permute-done.18), channel_id=1, source_target_pairs={{0,1},{1,0},{2,3},{3,2},{4,5},{5,4},{6,7},{7,6},{8,9},{9,8},{10,11... | collective-permute-start | bytes 393224 | tf_op jit(solution)/shard_map/ppermute | solution.py:17
  65.3 4.1 %collective-permute-start.24 = (bf16[128,512]{1,0:T(8,128)(2,1)S(1)}, bf16[128,512]{1,0:T(8,128)(2,1)S(1)}, u32[]{:S(2)}, u32[]{:S(2)}) collective-permute-start(bf16[128,512]{1,0:T(8,128)(2,1)S(1)} %collective-permute-done.17), channel_id=1, source_target_pairs={{0,1},{1,0},{2,3},{3,2},{4,5},{5,4},{6,7},{7,6},{8,9},{9,8},{10,11... | collective-permute-start | bytes 393224 | tf_op jit(solution)/shard_map/ppermute | solution.py:17
  65.3 11.5 %collective-permute-start.23 = (bf16[384,512]{1,0:T(8,128)(2,1)S(1)}, bf16[384,512]{1,0:T(8,128)(2,1)S(1)}, u32[]{:S(2)}, u32[]{:S(2)}) collective-permute-start(bf16[384,512]{1,0:T(8,128)(2,1)S(1)} %slice.88), channel_id=1, source_target_pairs={{0,4},{4,0},{8,12},{12,8},{16,20},{20,16},{24,28},{28,24},{1,5},{5... | collective-permute-start | bytes 1179656 | tf_op jit(solution)/shard_map/ppermute | solution.py:17
  67.2 13.7 %collective-permute-start.26 = (bf16[1,128,896]{2,1,0:T(8,128)(2,1)S(1)}, bf16[1,128,896]{2,1,0:T(8,128)(2,1)S(1)}, u32[]{:S(2)}, u32[]{:S(2)}) collective-permute-start(bf16[1,128,896]{2,1,0:T(8,128)(2,1)S(1)} %slice.152), channel_id=1, source_target_pairs={{0,16},{4,20},{8,24},{12,28},{16,0},{20,4},{24,8},{28,12},{1,17},{... | collective-permute-start | bytes 688136 | tf_op jit(solution)/shard_map/ppermute | solution.py:17
  77.3 13.3 %collective-permute-start.25 = (bf16[2,128,896]{2,1,0:T(8,128)(2,1)S(1)}, bf16[2,128,896]{2,1,0:T(8,128)(2,1)S(1)}, u32[]{:S(2)}, u32[]{:S(2)}) collective-permute-start(bf16[2,128,896]{2,1,0:T(8,128)(2,1)S(1)} %bitcast.149), channel_id=1, source_target_pairs={{0,8},{4,12},{8,0},{12,4},{16,24},{20,28},{24,16},{28,20},{1,9},{5... | collective-permute-start | bytes 1376264 | tf_op jit(solution)/shard_map/ppermute | solution.py:17
  82.2 4.9 %collective-permute-start.27 = (f32[32,896]{1,0:T(8,128)S(1)}, f32[32,896]{1,0:T(8,128)S(1)}, u32[]{:S(2)}, u32[]{:S(2)}) collective-permute-start(f32[32,896]{1,0:T(8,128)S(1)} %convolution_bitcast_fusion), channel_id=1, source_target_pairs={{0,4},{4,0},{8,12},{12,8},{16,20},{20,16},{24,28},{28,24},{1,5},{5... | collective-permute-start | bytes 344072 | tf_op jit(solution)/shard_map/ppermute | solution.py:17
  90.7 13.6 %collective-permute-start.28 = (bf16[1,128,896]{2,1,0:T(8,128)(2,1)S(1)}, bf16[1,128,896]{2,1,0:T(8,128)(2,1)S(1)}, u32[]{:S(2)}, u32[]{:S(2)}) collective-permute-start(bf16[1,128,896]{2,1,0:T(8,128)(2,1)S(1)} %slice.151), channel_id=1, source_target_pairs={{0,16},{4,20},{8,24},{12,28},{16,0},{20,4},{24,8},{28,12},{1,17},{... | collective-permute-start | bytes 688136 | tf_op jit(solution)/shard_map/ppermute | solution.py:17
  92.1 6.3 %collective-permute-start.29 = (f32[32,896]{1,0:T(8,128)S(1)}, f32[32,896]{1,0:T(8,128)S(1)}, u32[]{:S(2)}, u32[]{:S(2)}) collective-permute-start(f32[32,896]{1,0:T(8,128)S(1)} %add.141), channel_id=1, source_target_pairs={{0,8},{4,12},{8,0},{12,4},{16,24},{20,28},{24,16},{28,20},{1,9},{5... | collective-permute-start | bytes 344072 | tf_op jit(solution)/shard_map/ppermute | solution.py:17
  98.5 9.4 %collective-permute-start.32 = (f32[32,896]{1,0:T(8,128)S(1)}, f32[32,896]{1,0:T(8,128)S(1)}, u32[]{:S(2)}, u32[]{:S(2)}) collective-permute-start(f32[32,896]{1,0:T(8,128)S(1)} %add.146), channel_id=1, source_target_pairs={{0,16},{4,20},{8,24},{12,28},{16,0},{20,4},{24,8},{28,12},{1,17},{... | collective-permute-start | bytes 344072 | tf_op jit(solution)/shard_map/ppermute | solution.py:17
  110.0 13.9 %collective-permute-start.30 = (bf16[128,896]{1,0:T(8,128)(2,1)S(1)}, bf16[128,896]{1,0:T(8,128)(2,1)S(1)}, u32[]{:S(2)}, u32[]{:S(2)}) collective-permute-start(bf16[128,896]{1,0:T(8,128)(2,1)S(1)} %fusion.8), channel_id=1, source_target_pairs={{0,8},{4,12},{8,0},{12,4},{16,24},{20,28},{24,16},{28,20},{1,9},{5... | collective-permute-start | bytes 688136 | tf_op jit(solution)/shard_map/ppermute | solution.py:17
  110.1 13.8 %collective-permute-start.31 = (bf16[128,896]{1,0:T(8,128)(2,1)S(1)}, bf16[128,896]{1,0:T(8,128)(2,1)S(1)}, u32[]{:S(2)}, u32[]{:S(2)}) collective-permute-start(bf16[128,896]{1,0:T(8,128)(2,1)S(1)} %fusion.8), channel_id=1, source_target_pairs={{0,16},{4,20},{8,24},{12,28},{16,0},{20,4},{24,8},{28,12},{1,17},{... | collective-permute-start | bytes 688136 | tf_op jit(solution)/shard_map/ppermute | solution.py:17
  111.9 4.5 %collective-permute-start.34 = (f32[32,544]{1,0:T(8,128)S(1)}, f32[32,544]{1,0:T(8,128)S(1)}, u32[]{:S(2)}, u32[]{:S(2)}) collective-permute-start(f32[32,544]{1,0:T(8,128)S(1)} %fusion.68), channel_id=1, source_target_pairs={{0,2},{1,3},{2,0},{3,1},{4,6},{5,7},{6,4},{7,5},{8,10},{9,11},{10,... | collective-permute-start | bytes 208904 | tf_op jit(solution)/shard_map/ppermute | solution.py:17
  116.5 4.5 %collective-permute-start.35 = (f32[32,544]{1,0:T(8,128)S(1)}, f32[32,544]{1,0:T(8,128)S(1)}, u32[]{:S(2)}, u32[]{:S(2)}) collective-permute-start(f32[32,544]{1,0:T(8,128)S(1)} %add.149), channel_id=1, source_target_pairs={{0,4},{4,0},{8,12},{12,8},{16,20},{20,16},{24,28},{28,24},{1,5},{5... | collective-permute-start | bytes 208904 | tf_op jit(solution)/shard_map/ppermute | solution.py:17
  126.7 2.1 %collective-permute-start.36 = (bf16[384,512]{1,0:T(8,128)(2,1)}, bf16[384,512]{1,0:T(8,128)(2,1)}, u32[]{:S(2)}, u32[]{:S(2)}) collective-permute-start(bf16[384,512]{1,0:T(8,128)(2,1)} %get-tuple-element.163), channel_id=1, source_target_pairs={{0,1},{1,0},{2,3},{3,2},{4,5},{5,4},{6,7},{7,6},{8,9},{9,8},{10,11... | collective-permute-start | bytes 1179656 | tf_op jit(solution)/shard_map/ppermute | solution.py:17
  126.7 5.3 %collective-permute-start.38 = (f32[32,544]{1,0:T(8,128)S(1)}, f32[32,544]{1,0:T(8,128)S(1)}, u32[]{:S(2)}, u32[]{:S(2)}) collective-permute-start(f32[32,544]{1,0:T(8,128)S(1)} %add.151), channel_id=1, source_target_pairs={{0,8},{4,12},{8,0},{12,4},{16,24},{20,28},{24,16},{28,20},{1,9},{5... | collective-permute-start | bytes 208904 | tf_op jit(solution)/shard_map/ppermute | solution.py:17
  126.8 10.9 %collective-permute-start.40 = (bf16[128,896]{1,0:T(8,128)(2,1)}, bf16[128,896]{1,0:T(8,128)(2,1)S(1)}, u32[]{:S(2)}, u32[]{:S(2)}) collective-permute-start(bf16[128,896]{1,0:T(8,128)(2,1)} %copy-done.9), channel_id=1, source_target_pairs={{0,8},{4,12},{8,0},{12,4},{16,24},{20,28},{24,16},{28,20},{1,9},{5... | collective-permute-start | bytes 688136 | tf_op jit(solution)/shard_map/ppermute | solution.py:17
  132.0 9.2 %collective-permute-start.39 = (f32[32,544]{1,0:T(8,128)S(1)}, f32[32,544]{1,0:T(8,128)S(1)}, u32[]{:S(2)}, u32[]{:S(2)}) collective-permute-start(f32[32,544]{1,0:T(8,128)S(1)} %add.152), channel_id=1, source_target_pairs={{0,16},{4,20},{8,24},{12,28},{16,0},{20,4},{24,8},{28,12},{1,17},{... | collective-permute-start | bytes 208904 | tf_op jit(solution)/shard_map/ppermute | solution.py:17
  138.6 2.6 %collective-permute-start.41 = (bf16[128,512]{1,0:T(8,128)(2,1)S(1)}, bf16[128,512]{1,0:T(8,128)(2,1)S(1)}, u32[]{:S(2)}, u32[]{:S(2)}) collective-permute-start(bf16[128,512]{1,0:T(8,128)(2,1)S(1)} %get-tuple-element.165), channel_id=1, source_target_pairs={{0,1},{1,0},{2,3},{3,2},{4,5},{5,4},{6,7},{7,6},{8,9},{9,8},{10,11... | collective-permute-start | bytes 393224 | tf_op jit(solution)/shard_map/ppermute | solution.py:17
  138.7 9.2 %collective-permute-start.37 = (bf16[128,512]{1,0:T(8,128)(2,1)S(1)}, bf16[128,512]{1,0:T(8,128)(2,1)S(1)}, u32[]{:S(2)}, u32[]{:S(2)}) collective-permute-start(bf16[128,512]{1,0:T(8,128)(2,1)S(1)} %get-tuple-element.141), channel_id=1, source_target_pairs={{0,16},{4,20},{8,24},{12,28},{16,0},{20,4},{24,8},{28,12},{1,17},{... | collective-permute-start | bytes 393224 | tf_op jit(solution)/shard_map/ppermute | solution.py:17
  138.8 17.0 %collective-permute-start.46 = (bf16[128,512]{1,0:T(8,128)(2,1)S(1)}, bf16[128,512]{1,0:T(8,128)(2,1)S(1)}, u32[]{:S(2)}, u32[]{:S(2)}) collective-permute-start(bf16[128,512]{1,0:T(8,128)(2,1)S(1)} %get-tuple-element.140), channel_id=1, source_target_pairs={{0,8},{4,12},{8,0},{12,4},{16,24},{20,28},{24,16},{28,20},{1,9},{5... | collective-permute-start | bytes 393224 | tf_op jit(solution)/shard_map/ppermute | solution.py:17
  148.0 10.7 %collective-permute-start.42 = (bf16[1,128,512]{2,1,0:T(8,128)(2,1)S(1)}, bf16[1,128,512]{2,1,0:T(8,128)(2,1)S(1)}, u32[]{:S(2)}, u32[]{:S(2)}) collective-permute-start(bf16[1,128,512]{2,1,0:T(8,128)(2,1)S(1)} %fusion.48), channel_id=1, source_target_pairs={{0,2},{1,3},{2,0},{3,1},{4,6},{5,7},{6,4},{7,5},{8,10},{9,11},{10,... | collective-permute-start | bytes 393224 | tf_op jit(solution)/shard_map/ppermute | solution.py:17
  149.6 4.2 %collective-permute-start.43 = (bf16[32,896]{1,0:T(8,128)(2,1)S(1)}, bf16[32,896]{1,0:T(8,128)(2,1)S(1)}, u32[]{:S(2)}, u32[]{:S(2)}) collective-permute-start(bf16[32,896]{1,0:T(8,128)(2,1)S(1)} %convolution_convert_fusion.4), channel_id=1, source_target_pairs={{0,4},{4,0},{8,12},{12,8},{16,20},{20,16},{24,28},{28,24},{1,5},{5... | collective-permute-start | bytes 172040 | tf_op jit(solution)/shard_map/ppermute | solution.py:17
  150.8 7.4 %collective-permute-start.45 = (bf16[128,512]{1,0:T(8,128)(2,1)S(1)}, bf16[128,512]{1,0:T(8,128)(2,1)S(1)}, u32[]{:S(2)}, u32[]{:S(2)}) collective-permute-start(bf16[128,512]{1,0:T(8,128)(2,1)S(1)} %add_convert_fusion.1), channel_id=1, source_target_pairs={{0,24},{4,28},{8,16},{12,20},{16,8},{20,12},{24,0},{28,4},{1,25},{... | collective-permute-start | bytes 393224 | tf_op jit(solution)/shard_map/ppermute | solution.py:17
  153.8 4.9 %collective-permute-start.44 = (bf16[32,896]{1,0:T(8,128)(2,1)S(1)}, bf16[32,896]{1,0:T(8,128)(2,1)S(1)}, u32[]{:S(2)}, u32[]{:S(2)}) collective-permute-start(bf16[32,896]{1,0:T(8,128)(2,1)S(1)} %add_convert_fusion.3), channel_id=1, source_target_pairs={{0,8},{4,12},{8,0},{12,4},{16,24},{20,28},{24,16},{28,20},{1,9},{5... | collective-permute-start | bytes 172040 | tf_op jit(solution)/shard_map/ppermute | solution.py:17
  158.8 5.0 %collective-permute-start.47 = (bf16[1,128,512]{2,1,0:T(8,128)(2,1)S(1)}, bf16[1,128,512]{2,1,0:T(8,128)(2,1)S(1)}, u32[]{:S(2)}, u32[]{:S(2)}) collective-permute-start(bf16[1,128,512]{2,1,0:T(8,128)(2,1)S(1)} %fusion.45), channel_id=1, source_target_pairs={{0,2},{1,3},{2,0},{3,1},{4,6},{5,7},{6,4},{7,5},{8,10},{9,11},{10,... | collective-permute-start | bytes 393224 | tf_op jit(solution)/shard_map/ppermute | solution.py:17
  160.0 5.2 %collective-permute-start.49 = (bf16[32,896]{1,0:T(8,128)(2,1)S(1)}, bf16[32,896]{1,0:T(8,128)(2,1)S(1)}, u32[]{:S(2)}, u32[]{:S(2)}) collective-permute-start(bf16[32,896]{1,0:T(8,128)(2,1)S(1)} %add_convert_fusion.2), channel_id=1, source_target_pairs={{0,16},{4,20},{8,24},{12,28},{16,0},{20,4},{24,8},{28,12},{1,17},{... | collective-permute-start | bytes 172040 | tf_op jit(solution)/shard_map/ppermute | solution.py:17
  164.0 3.7 %collective-permute-start.48 = (bf16[128,512]{1,0:T(8,128)(2,1)S(1)}, bf16[128,512]{1,0:T(8,128)(2,1)S(1)}, u32[]{:S(2)}, u32[]{:S(2)}) collective-permute-start(bf16[128,512]{1,0:T(8,128)(2,1)S(1)} %get-tuple-element.127), channel_id=1, source_target_pairs={{0,1},{1,0},{2,3},{3,2},{4,5},{5,4},{6,7},{7,6},{8,9},{9,8},{10,11... | collective-permute-start | bytes 393224 | tf_op jit(solution)/shard_map/ppermute | solution.py:17
  (19 other events, 209.9 us)

commit v4 on v3

--- a/solution.py
+++ b/solution.py
@@ -10,6 +10,7 @@
 BF = jnp.bfloat16
 F32 = jnp.float32
 HIGHEST = lax.Precision.HIGHEST
+HIGH = lax.Precision.HIGH
 
 
 def flip(arr, axis, mask):
@@ -97,7 +98,7 @@
             kept.append(piece if k == 0 else flip(piece, "dp", 2 * k))
         return kept
 
-    ucut = (up_weight.shape[0] * 3 // 8 + 63) // 64 * 64
+    ucut = (up_weight.shape[0] * 7 // 16 + 31) // 32 * 32
     dcut = (down_weight.shape[0] // 2 + 127) // 128 * 128
     up_a = flip(up_weight[:ucut], "dp", 1)
     mine, swap = split_half(tokens, half)
@@ -121,25 +122,19 @@
     up_a = wait(up_a)
     up_b_in, up_a = tie(up_weight[ucut:], up_a)
     up_b = flip(up_b_in, "dp", 1)
-    windows = windows + wait(win_got)
     grad_got = flip(jnp.stack(grad_blocks), "tensor", tbits[1])
-    win_got = lax.ppermute(windows, "tensor", [(0, 2), (1, 3)])
-    tok_keep = [tok_keep[0]] + [wait(piece) for piece in tok_keep[1:]]
+    tok_keep = [tok_keep[0]] + [wait(piece) for piece in tok_keep[1:-1]] + tok_keep[-1:]
+    up_b = wait(up_b)
+    down_a_in, up_b = tie(down_weight[:dcut], up_b)
+    down_a = flip(down_a_in, "dp", 1)
+    tok_keep[-1] = wait(tok_keep[-1])
     for mask in tbits[1:]:
         if mask > tbits[1]:
             grad_got = flip(jnp.stack(grad_blocks), "tensor", mask)
         grad_got = wait(grad_got)
         grad_blocks = grad_blocks + [grad_got[n] for n in range(len(grad_blocks))]
     grad_keep = send_z(jnp.stack(grad_blocks))
-    windows = windows + wait(win_got)
-    for mask in tbits[2:]:
-        windows = windows + wait(
-            lax.ppermute(windows, "tensor", [(i, i + mask) for i in range(mask)])
-        )
-    tok_win, grad_win = windows[0], windows[1]
-    up_b = wait(up_b)
-    down_a_in, up_b = tie(down_weight[:dcut], up_b)
-    down_a = flip(down_a_in, "dp", 1)
+    tok_other = [wait(flip(piece, "tensor", 1)) for piece in tok_keep]
     up_other = jnp.concatenate([up_a, up_b])
 
     def other_halves(kept):
@@ -167,16 +162,21 @@
             ks = [ks[n] for n in stay]
         return acc[0]
 
-    tok_other = other_halves(tok_keep)
     part_of = partial(tok_keep, tok_other, up_weight, up_other, ((1,), (0,)))
     pre_got = flip(part_of(odd).astype(BF), "dp", 2)
     pre_acc = part_of(even)
+    grad_keep = [grad_keep[0]] + [wait(piece) for piece in grad_keep[1:]]
+    pre_acc = pre_acc + wait(pre_got).astype(F32)
     down_a = wait(down_a)
     down_b_in, down_a = tie(down_weight[dcut:], down_a)
     down_b = flip(down_b_in, "dp", 1)
-    grad_keep = [grad_keep[0]] + [wait(piece) for piece in grad_keep[1:]]
-    pre_acc = pre_acc + wait(pre_got).astype(F32)
-    grad_other = other_halves(grad_keep)
+    windows = windows + wait(win_got)
+    for n, mask in enumerate(tbits[1:]):
+        win_got = lax.ppermute(windows, "tensor", [(i, i + mask) for i in range(mask)])
+        if n == 0:
+            grad_other = other_halves(grad_keep)
+        windows = windows + wait(win_got)
+    tok_win, grad_win = windows[0], windows[1]
     down_b = wait(down_b)
     down_other = jnp.concatenate([down_a, down_b])
     part_of = partial(grad_keep, grad_other, down_weight, down_other, ((1,), (1,)))
@@ -188,9 +188,10 @@
     act_out = (preact * squash).astype(BF)
     slope = squash * (1.0 + preact * (1.0 - squash))
     down_matrix = down_accum[0] + dot(act_out, grad_win, ((0,), (0,))) * scale
-    down_sum = dot(down_q, down_matrix, ((0,), (1,)), HIGHEST)
-    down_sum = down_sum + wait(flip(down_sum, "dp", 1))
+    down_sum = dot(down_q, down_matrix, ((0,), (1,)), HIGH)
+    down_got = flip(down_sum, "dp", 1)
     back_acc = back_acc + wait(back_got).astype(F32)
+    down_sum = down_sum + wait(down_got)
     for mask in dbits[1:-1]:
         down_sum = down_sum + wait(flip(down_sum, "dp", mask))
     down_got = flip(down_sum, "dp", dbits[-1])
@@ -207,16 +208,14 @@
     def forward(level):
         return {k: flip(hid[k ^ (k & -k)], "dp", 2 * (k & -k)) for k in level}
 
-    def products(ks):
-        lhs = jnp.concatenate([hid[k] for k in ks])
-        own = dot(lhs, up_weight, w_dims).astype(BF)
-        par = dot(lhs, up_other, w_dims).astype(BF)
-        return jnp.where(core == 0, own, par), jnp.where(core == 0, par, own)
-
-    def send_back(ks, mine, got):
-        mine = (mine.astype(F32) + got.astype(F32)).astype(BF).reshape(len(ks), rows, -1)
-        for n, k in enumerate(ks):
-            returned[k] = mine[n] if k == 0 else flip(mine[n], "dp", 2 * k)
+    def start_back(k):
+        own = dot(hid[k], up_weight, w_dims).astype(BF)
+        par = dot(hid[k], up_other, w_dims).astype(BF)
+        return jnp.where(core == 0, own, par), flip(jnp.where(core == 0, par, own), "tensor", 1)
+
+    def send_back(k, mine, got):
+        mine = (mine.astype(F32) + got.astype(F32)).astype(BF)
+        returned[k] = mine if k == 0 else flip(mine, "dp", 2 * k)
 
     def settle(ks):
         stack = jnp.stack([returned[k] for k in ks])
@@ -237,36 +236,40 @@
     first = level_after([0])
     coming = forward(first)
     up_matrix = up_accum[0] + dot(tok_win, hidden, ((0,), (0,))) * scale
-    both = dot(up_q, up_matrix, ((0,), (1,)), HIGHEST)
+    both = dot(up_q, up_matrix, ((0,), (1,)), HIGH)
     down_sum = down_sum + wait(down_got)
     down_gram = dot(down_sum, down_sum, ((1,), (1,)), HIGHEST)
-    down_term = dot(down_sum, down_matrix, ((1,), (0,)), HIGHEST)
+    down_term = dot(down_sum, down_matrix, ((1,), (0,)), HIGH)
     both = jnp.concatenate([both, down_term, down_gram], axis=1)
-    for mask in tbits:
-        both = both + wait(flip(both, "tensor", mask))
-    both = both + wait(flip(both, "dp", 1))
+    both = both + wait(flip(both, "tensor", 1))
+    both_got = flip(both, "tensor", tbits[1])
+    mine, got = start_back(0)
+    send_back(0, mine, wait(got))
     for k in reversed(first):
         hid[k] = wait(coming[k])
-    group = [0] + first
     level = level_after(first)
     coming = forward(level)
-    mine, send = products(group)
-    send_got = flip(send, "tensor", 1)
+    both = both + wait(both_got)
+    for mask in tbits[2:]:
+        both = both + wait(flip(both, "tensor", mask))
+    both_got = flip(both, "dp", 1)
+    pending = {k: start_back(k) for k in first}
+    both = both + wait(both_got)
     both_got = flip(both, "dp", dbits[1])
-    send_back(group, mine, wait(send_got))
-    both = both + wait(both_got)
-    for mask in dbits[2:-1]:
-        both = both + wait(flip(both, "dp", mask))
-    both_got = flip(both, "dp", dbits[-1])
-    while level:
-        for k in level:
-            hid[k] = wait(coming[k])
-        mine, send = products(level)
-        send_got = flip(send, "tensor", 1)
-        after = level_after(level)
-        coming = forward(after)
-        send_back(level, mine, wait(send_got))
-        level = after
+    for k in first:
+        mine, got = pending[k]
+        send_back(k, mine, wait(got))
+    for k in level:
+        hid[k] = wait(coming[k])
+    pending = {k: start_back(k) for k in level}
+    after = level_after(level)
+    coming = forward(after)
+    for mask in dbits[2:]:
+        both = both + wait(both_got)
+        both_got = flip(both, "dp", mask)
+    for k in level:
+        mine, got = pending[k]
+        send_back(k, mine, wait(got))
     both = both + wait(both_got)
     up_sum, down_term, down_gram = both[:, :window], both[:, window : 2 * window], both[:, 2 * window :]
     up_inv, down_inv = inverse_factors(
@@ -278,32 +281,42 @@
 
     outer = ((0,), (0,))
     up_left = scaled(up_inv, up_sum)
-    up_right = dot(up_left, up_matrix, ((1,), (0,)), HIGHEST).astype(BF)
+    up_right = dot(up_left, up_matrix, ((1,), (0,)), HIGH).astype(BF)
     right_got = flip(up_right, "dp", 1)
+    level = after
+    while level:
+        for k in level:
+            hid[k] = wait(coming[k])
+        after = level_after(level)
+        coming = forward(after)
+        for k in level:
+            mine, got = start_back(k)
+            send_back(k, mine, wait(got))
+        level = after
     returned.update({k: wait(returned[k]) for k in even[1:]})
     pair_a = settle(even)
+    returned.update({k: wait(returned[k]) for k in odd})
+    pair_b = settle(odd)
     up_right = up_right.astype(F32) + wait(right_got).astype(F32)
     for n, mask in enumerate(dbits[1:]):
         up_right = up_right.astype(BF)
         right_got = flip(up_right, "dp", mask)
         if n == 0:
-            returned.update({k: wait(returned[k]) for k in odd})
-            pair_b = settle(odd)
-        if n == 1:
             sum_a, sum_b = add_pair(pair_a), add_pair(pair_b)
             low = zrel & 1
             got = flip(jnp.where(low == 0, sum_b, sum_a), "tensor", 1)
+        if n == 1:
+            got = wait(got)
         up_right = up_right.astype(F32) + wait(right_got).astype(F32)
     own = jnp.where(low == 0, sum_a, sum_b)
-    got = wait(got)
     input_grad = jnp.concatenate(
         [jnp.where(half == 0, own, got), jnp.where(half == 0, got, own)], axis=1
     )
     up_right = up_right / replicas
-    up_error = up_matrix - dot(up_left, up_right, outer, HIGHEST)
+    up_error = up_matrix - dot(up_left, up_right, outer, HIGH)
     down_left = scaled(down_inv, down_sum)
     down_right = scaled(down_inv, down_term) / replicas
-    down_error = down_matrix - dot(down_left, down_right, outer, HIGHEST)
+    down_error = down_matrix - dot(down_left, down_right, outer, HIGH)
     up_left, up_right, down_left, down_right = up_left.T, up_right.T, down_left.T, down_right.T
     return (input_grad, up_error[None], up_left, up_right, down_error[None], down_left, down_right)
 

time: 169 us -> 164 us (0.970)
  other arithmetic: 10.5 us -> 5.53 us
  starting transfers between devices: 50.8 us -> 46.1 us
  waiting for transfers between devices: 79.5 us -> 82.8 us
  local copies, waits for them, and re-layouts: 6.04 us -> 9.02 us
    ppermute x48 -> x50, starting transfers between devices: 45.2 us -> 42.3 us  [flip(): return lax.ppermute(arr, axis, [(i, i ^ mask) for i in range(size)])]
    ppermute x48 -> x50, waiting for transfers between devices: 79.5 us -> 81.9 us  [flip(): return lax.ppermute(arr, axis, [(i, i ^ mask) for i in range(size)])]
    select_n x5, other arithmetic: 1.98 us -> 0.17 us  [part_of(): b = jnp.concatenate([jnp.where(core == 0, other[k], kept[k]) for k in ks])]
    dot_general x25 -> x29, matrix products: 16.3 us -> 14.7 us  [dot(): lax.dot_general(a, b, (dims, ((), ())), preferred_element_type=F32, preci...]
  transfers between devices with their start and end apart: 50 -> 52, of which waited for: 24 -> 26; matrix products, arithmetic and copies ran while one was open for 15% -> 14% of each run, Pallas kernels for 2% -> 2%
where the time goes in v4:
time: 164 us
  waiting for transfers between devices  82.8 us (50%)
  starting transfers between devices  46.1 us (28%)
  matrix products  14.7 us (9%)
  local copies, waits for them, and re-layouts  9.02 us (6%)
  other arithmetic  5.53 us (3%)
  Pallas kernels  4.05 us (2%)
    ppermute x50, waiting for transfers between devices, flip(): return lax.ppermute(arr, axis, [(i, i ^ mask) for i in range(size)])  81.9 us
    ppermute x50, starting transfers between devices, flip(): return lax.ppermute(arr, axis, [(i, i ^ mask) for i in range(size)])  42.3 us
    dot_general x29, matrix products, dot(): lax.dot_general(a, b, (dims, ((), ())), preferred_element_type=F32, preci...  14.7 us
    pallas_call x1, Pallas kernels, inverse_factors(): pl.pallas_call(factor_kernel, out_shape=(shape, shape), name='inverse_fac...  4.05 us
  transfers between devices with their start and end apart: 52, of which 26 were waited for; matrix products, arithmetic and copies ran while one was open for 14% of the time, Pallas kernels for 2%

profile of v4, /device:TPU:0, one launch (start us, length us, event | category | flops | bytes accessed | tf_op | source)
XLA Modules:
  0.0 163.8 jit_solution(1904477305669691484)
XLA Ops:
  0.7 1.0 select_bitcast_fusion
  2.2 1.8 %slice.72 = bf16[224,896]{1,0:T(8,128)(2,1)} slice(bf16[512,896]{1,0:T(8,128)(2,1)} %param.10), slice={[0:224], [0:896]} | slice | bytes 802816 | tf_op jit(solution)/shard_map/slice | solution.py:103
  4.0 2.6 %collective-permute-start.5 = (bf16[224,896]{1,0:T(8,128)(2,1)}, bf16[224,896]{1,0:T(8,128)(2,1)}, u32[]{:S(2)}, u32[]{:S(2)}) collective-permute-start(bf16[224,896]{1,0:T(8,128)(2,1)} %slice.72), channel_id=1, source_target_pairs={{0,4},{4,0},{8,12},{12,8},{16,20},{20,16},{24,28},{28,24},{1,5},{5... | collective-permute-start | bytes 1204232 | tf_op jit(solution)/shard_map/ppermute | solution.py:18
  7.5 1.6 collective-permute-start.3
  11.7 4.2 %collective-permute-done.3 = bf16[2,128,512]{2,1,0:T(8,128)(2,1)S(1)} collective-permute-done((bf16[2,128,512]{2,1,0:T(8,128)(2,1)S(1)}, bf16[2,128,512]{2,1,0:T(8,128)(2,1)S(1)}, u32[]{:S(2)}, u32[]{:S(2)}) %collective-permute-start.3) | collective-permute-done | bytes 262176 | tf_op jit(solution)/shard_map/ppermute | solution.py:18
  16.8 1.8 %collective-permute-start.6 = (bf16[288,896]{1,0:T(8,128)(2,1)}, bf16[288,896]{1,0:T(8,128)(2,1)S(1)}, u32[]{:S(2)}, u32[]{:S(2)}) collective-permute-start(bf16[288,896]{1,0:T(8,128)(2,1)} %slice.71), channel_id=1, source_target_pairs={{0,4},{4,0},{8,12},{12,8},{16,20},{20,16},{24,28},{28,24},{1,5},{5... | collective-permute-start | bytes 1548296 | tf_op jit(solution)/shard_map/ppermute | solution.py:18
  18.6 1.6 collective-permute-start.2
  20.3 3.7 %collective-permute-start.4 = (bf16[128,512]{1,0:T(8,128)(2,1)S(1)}, bf16[128,512]{1,0:T(8,128)(2,1)S(1)}, u32[]{:S(2)}, u32[]{:S(2)}) collective-permute-start(bf16[128,512]{1,0:T(8,128)(2,1)S(1)} %get-tuple-element.141), channel_id=1, source_target_pairs={{0,24},{4,28},{8,16},{12,20},{16,8},{20,12},{24,0},{28,4},{1,25},{... | collective-permute-start | bytes 393224 | tf_op jit(solution)/shard_map/ppermute | solution.py:18
  24.8 1.0 constant_dynamic-update-slice_fusion.1
  25.8 5.8 %collective-permute-done.8 = bf16[128,512]{1,0:T(8,128)(2,1)S(1)} collective-permute-done((bf16[128,512]{1,0:T(8,128)(2,1)S(1)}, bf16[128,512]{1,0:T(8,128)(2,1)S(1)}, u32[]{:S(2)}, u32[]{:S(2)}) %collective-permute-start.8) | collective-permute-done | bytes 131104 | tf_op jit(solution)/shard_map/ppermute | solution.py:18
  31.6 2.7 %collective-permute-done.7 = bf16[128,512]{1,0:T(8,128)(2,1)S(1)} collective-permute-done((bf16[128,512]{1,0:T(8,128)(2,1)S(1)}, bf16[128,512]{1,0:T(8,128)(2,1)S(1)}, u32[]{:S(2)}, u32[]{:S(2)}) %collective-permute-start.7) | collective-permute-done | bytes 131104 | tf_op jit(solution)/shard_map/ppermute | solution.py:18
  35.1 3.0 %collective-permute-start.19 = (bf16[128,512]{1,0:T(8,128)(2,1)S(1)}, bf16[128,512]{1,0:T(8,128)(2,1)S(1)}, u32[]{:S(2)}, u32[]{:S(2)}) collective-permute-start(bf16[128,512]{1,0:T(8,128)(2,1)S(1)} %get-tuple-element.135), channel_id=1, source_target_pairs={{0,8},{4,12},{8,0},{12,4},{16,24},{20,28},{24,16},{28,20},{1,9},{5... | collective-permute-start | bytes 393224 | tf_op jit(solution)/shard_map/ppermute | solution.py:18
  38.7 1.3 collective-permute-start.17
  41.7 5.9 %collective-permute-done.19 = bf16[128,512]{1,0:T(8,128)(2,1)S(1)} collective-permute-done((bf16[128,512]{1,0:T(8,128)(2,1)S(1)}, bf16[128,512]{1,0:T(8,128)(2,1)S(1)}, u32[]{:S(2)}, u32[]{:S(2)}) %collective-permute-start.19) | collective-permute-done | bytes 131104 | tf_op jit(solution)/shard_map/ppermute | solution.py:18
  47.6 1.3 collective-permute-start.10
  49.9 7.4 %collective-permute-done.16 = bf16[2,128,896]{2,1,0:T(8,128)(2,1)S(1)} collective-permute-done((bf16[2,128,896]{2,1,0:T(8,128)(2,1)S(1)}, bf16[2,128,896]{2,1,0:T(8,128)(2,1)S(1)}, u32[]{:S(2)}, u32[]{:S(2)}) %collective-permute-start.16) | collective-permute-done | bytes 458784 | tf_op jit(solution)/shard_map/ppermute | solution.py:18
  59.2 2.6 %collective-permute-start.23 = (bf16[2,128,256]{2,1,0:T(8,128)(2,1)S(1)}, bf16[2,128,256]{2,1,0:T(8,128)(2,1)S(1)}, u32[]{:S(2)}, u32[]{:S(2)}) collective-permute-start(bf16[2,128,256]{2,1,0:T(8,128)(2,1)S(1)} %fusion.117), channel_id=1, source_target_pairs={{0,2},{1,3},{4,6},{5,7},{8,10},{9,11},{12,14},{13,15},{16,18},{17,... | collective-permute-start | bytes 393224 | tf_op jit(solution)/shard_map/ppermute | solution.py:175
  63.5 0.9 collective-permute-done.23
  64.4 5.4 %collective-permute-done.22 = bf16[384,512]{1,0:T(8,128)(2,1)S(1)} collective-permute-done((bf16[384,512]{1,0:T(8,128)(2,1)S(1)}, bf16[384,512]{1,0:T(8,128)(2,1)S(1)}, u32[]{:S(2)}, u32[]{:S(2)}) %collective-permute-start.22) | collective-permute-done | bytes 393248 | tf_op jit(solution)/shard_map/ppermute | solution.py:18
  70.5 3.7 %collective-permute-done.26 = bf16[1,128,896]{2,1,0:T(8,128)(2,1)S(1)} collective-permute-done((bf16[1,128,896]{2,1,0:T(8,128)(2,1)S(1)}, bf16[1,128,896]{2,1,0:T(8,128)(2,1)S(1)}, u32[]{:S(2)}, u32[]{:S(2)}) %collective-permute-start.26) | collective-permute-done | bytes 229408 | tf_op jit(solution)/shard_map/ppermute | solution.py:18
  74.5 0.9 copy-done.3
  76.0 1.5 collective-permute-start.28
  78.0 5.9 %collective-permute-done.25 = bf16[2,128,896]{2,1,0:T(8,128)(2,1)S(1)} collective-permute-done((bf16[2,128,896]{2,1,0:T(8,128)(2,1)S(1)}, bf16[2,128,896]{2,1,0:T(8,128)(2,1)S(1)}, u32[]{:S(2)}, u32[]{:S(2)}) %collective-permute-start.25) | collective-permute-done | bytes 458784 | tf_op jit(solution)/shard_map/ppermute | solution.py:18
  84.0 0.9 copy-done.8
  86.0 2.5 %collective-permute-start.29 = (f32[32,896]{1,0:T(8,128)S(1)}, f32[32,896]{1,0:T(8,128)S(1)}, u32[]{:S(2)}, u32[]{:S(2)}) collective-permute-start(f32[32,896]{1,0:T(8,128)S(1)} %add.147), channel_id=1, source_target_pairs={{0,8},{4,12},{8,0},{12,4},{16,24},{20,28},{24,16},{28,20},{1,9},{5... | collective-permute-start | bytes 344072 | tf_op jit(solution)/shard_map/ppermute | solution.py:18
  88.5 5.2 %collective-permute-done.29 = f32[32,896]{1,0:T(8,128)S(1)} collective-permute-done((f32[32,896]{1,0:T(8,128)S(1)}, f32[32,896]{1,0:T(8,128)S(1)}, u32[]{:S(2)}, u32[]{:S(2)}) %collective-permute-start.29) | collective-permute-done | bytes 114720 | tf_op jit(solution)/shard_map/ppermute | solution.py:18
  93.7 3.3 %collective-permute-start.31 = (f32[32,896]{1,0:T(8,128)S(1)}, f32[32,896]{1,0:T(8,128)S(1)}, u32[]{:S(2)}, u32[]{:S(2)}) collective-permute-start(f32[32,896]{1,0:T(8,128)S(1)} %add.152), channel_id=1, source_target_pairs={{0,16},{4,20},{8,24},{12,28},{16,0},{20,4},{24,8},{28,12},{1,17},{... | collective-permute-start | bytes 344072 | tf_op jit(solution)/shard_map/ppermute | solution.py:18
  97.0 3.2 %collective-permute-done.27 = bf16[1,128,896]{2,1,0:T(8,128)(2,1)} collective-permute-done((bf16[1,128,896]{2,1,0:T(8,128)(2,1)}, bf16[1,128,896]{2,1,0:T(8,128)(2,1)}, u32[]{:S(2)}, u32[]{:S(2)}) %collective-permute-start.27) | collective-permute-done | bytes 229408 | tf_op jit(solution)/shard_map/ppermute | solution.py:18
  100.2 1.3 fusion.8
  102.0 0.9 collective-permute-start.35
  103.8 4.7 %collective-permute-done.31 = f32[32,896]{1,0:T(8,128)S(1)} collective-permute-done((f32[32,896]{1,0:T(8,128)S(1)}, f32[32,896]{1,0:T(8,128)S(1)}, u32[]{:S(2)}, u32[]{:S(2)}) %collective-permute-start.31) | collective-permute-done | bytes 114720 | tf_op jit(solution)/shard_map/ppermute | solution.py:18
  111.3 2.4 %collective-permute-done.33 = bf16[128,896]{1,0:T(8,128)(2,1)S(1)} collective-permute-done((bf16[128,896]{1,0:T(8,128)(2,1)S(1)}, bf16[128,896]{1,0:T(8,128)(2,1)S(1)}, u32[]{:S(2)}, u32[]{:S(2)}) %collective-permute-start.33) | collective-permute-done | bytes 229408 | tf_op jit(solution)/shard_map/ppermute | solution.py:18
  116.1 1.6 collective-permute-start.38
  117.8 3.0 %collective-permute-done.38 = f32[32,544]{1,0:T(8,128)S(1)} collective-permute-done((f32[32,544]{1,0:T(8,128)S(1)}, f32[32,544]{1,0:T(8,128)S(1)}, u32[]{:S(2)}, u32[]{:S(2)}) %collective-permute-start.38) | collective-permute-done | bytes 69664 | tf_op jit(solution)/shard_map/ppermute | solution.py:18
  120.9 2.6 %collective-permute-start.39 = (bf16[128,512]{1,0:T(8,128)(2,1)S(1)}, bf16[128,512]{1,0:T(8,128)(2,1)S(1)}, u32[]{:S(2)}, u32[]{:S(2)}) collective-permute-start(bf16[128,512]{1,0:T(8,128)(2,1)S(1)} %add_convert_fusion.2), channel_id=1, source_target_pairs={{0,16},{4,20},{8,24},{12,28},{16,0},{20,4},{24,8},{28,12},{1,17},{... | collective-permute-start | bytes 393224 | tf_op jit(solution)/shard_map/ppermute | solution.py:18
  123.5 5.4 %collective-permute-done.41 = bf16[128,896]{1,0:T(8,128)(2,1)S(1)} collective-permute-done((bf16[128,896]{1,0:T(8,128)(2,1)S(1)}, bf16[128,896]{1,0:T(8,128)(2,1)S(1)}, u32[]{:S(2)}, u32[]{:S(2)}) %collective-permute-start.41) | collective-permute-done | bytes 229408 | tf_op jit(solution)/shard_map/ppermute | solution.py:18
  130.5 2.5 %collective-permute-start.47 = (bf16[128,512]{1,0:T(8,128)(2,1)S(1)}, bf16[128,512]{1,0:T(8,128)(2,1)S(1)}, u32[]{:S(2)}, u32[]{:S(2)}) collective-permute-start(bf16[128,512]{1,0:T(8,128)(2,1)S(1)} %add_convert_fusion), channel_id=1, source_target_pairs={{0,8},{4,12},{8,0},{12,4},{16,24},{20,28},{24,16},{28,20},{1,9},{5... | collective-permute-start | bytes 393224 | tf_op jit(solution)/shard_map/ppermute | solution.py:18
  133.0 2.3 %collective-permute-done.42 = f32[32,544]{1,0:T(8,128)S(1)} collective-permute-done((f32[32,544]{1,0:T(8,128)S(1)}, f32[32,544]{1,0:T(8,128)S(1)}, u32[]{:S(2)}, u32[]{:S(2)}) %collective-permute-start.42) | collective-permute-done | bytes 69664 | tf_op jit(solution)/shard_map/ppermute | solution.py:18
  136.9 4.0 %inverse_factors.1 = (f32[32,32]{1,0:T(8,128)}, f32[32,32]{1,0:T(8,128)}) custom-call(f32[32,32]{1,0:T(8,128)} %fusion.57.up_ref, f32[32,32]{1,0:T(8,128)} %slice_multiply_fusion.down_ref), custom_call_target="tpu_custom_call" | custom-call | flops 1000000 | bytes 20000 | tf_op jit(solution)/shard_map/inverse_factors/pallas_call | solution.py:51
  140.9 0.9 fusion.55
  142.3 2.0 %collective-permute-start.46 = (bf16[128,512]{1,0:T(8,128)(2,1)S(1)}, bf16[128,512]{1,0:T(8,128)(2,1)S(1)}, u32[]{:S(2)}, u32[]{:S(2)}) collective-permute-start(bf16[128,512]{1,0:T(8,128)(2,1)S(1)} %add_convert_fusion.1), channel_id=1, source_target_pairs={{0,24},{4,28},{8,16},{12,20},{16,8},{20,12},{24,0},{28,4},{1,25},{... | collective-permute-start | bytes 393224 | tf_op jit(solution)/shard_map/ppermute | solution.py:18
  144.8 4.3 %collective-permute-done.46 = bf16[128,512]{1,0:T(8,128)(2,1)S(1)} collective-permute-done((bf16[128,512]{1,0:T(8,128)(2,1)S(1)}, bf16[128,512]{1,0:T(8,128)(2,1)S(1)}, u32[]{:S(2)}, u32[]{:S(2)}) %collective-permute-start.46) | collective-permute-done | bytes 131104 | tf_op jit(solution)/shard_map/ppermute | solution.py:18
  149.2 2.1 %collective-permute-start.48 = (bf16[1,128,512]{2,1,0:T(8,128)(2,1)S(1)}, bf16[1,128,512]{2,1,0:T(8,128)(2,1)S(1)}, u32[]{:S(2)}, u32[]{:S(2)}) collective-permute-start(bf16[1,128,512]{2,1,0:T(8,128)(2,1)S(1)} %fusion.46), channel_id=1, source_target_pairs={{0,2},{1,3},{2,0},{3,1},{4,6},{5,7},{6,4},{7,5},{8,10},{9,11},{10,... | collective-permute-start | bytes 393224 | tf_op jit(solution)/shard_map/ppermute | solution.py:18
  151.5 2.8 %collective-permute-done.48 = bf16[1,128,512]{2,1,0:T(8,128)(2,1)S(1)} collective-permute-done((bf16[1,128,512]{2,1,0:T(8,128)(2,1)S(1)}, bf16[1,128,512]{2,1,0:T(8,128)(2,1)S(1)}, u32[]{:S(2)}, u32[]{:S(2)}) %collective-permute-start.48) | collective-permute-done | bytes 131104 | tf_op jit(solution)/shard_map/ppermute | solution.py:18
  154.6 1.1 collective-permute-done.50
  156.3 1.5 fusion
  157.8 3.0 %collective-permute-done.51 = bf16[32,896]{1,0:T(8,128)(2,1)S(1)} collective-permute-done((bf16[32,896]{1,0:T(8,128)(2,1)S(1)}, bf16[32,896]{1,0:T(8,128)(2,1)S(1)}, u32[]{:S(2)}, u32[]{:S(2)}) %collective-permute-start.51) | collective-permute-done | bytes 57376 | tf_op jit(solution)/shard_map/ppermute | solution.py:18
  160.9 1.5 fusion.1
  (177 shorter events, 29.3 us)
Async XLA Ops:
  1.7 5.8 %collective-permute-start = (bf16[128,512]{1,0:T(8,128)(2,1)S(1)}, bf16[128,512]{1,0:T(8,128)(2,1)S(1)}, u32[]{:S(2)}, u32[]{:S(2)}) collective-permute-start(bf16[128,512]{1,0:T(8,128)(2,1)S(1)} %get-tuple-element.161), channel_id=1, source_target_pairs={{0,1},{1,0},{2,3},{3,2},{4,5},{5,4},{6,7},{7,6},{8,9},{9,8},{10,11... | collective-permute-start | bytes 393224 | tf_op jit(solution)/shard_map/ppermute | solution.py:18
  4.0 12.8 %collective-permute-start.5 = (bf16[224,896]{1,0:T(8,128)(2,1)}, bf16[224,896]{1,0:T(8,128)(2,1)}, u32[]{:S(2)}, u32[]{:S(2)}) collective-permute-start(bf16[224,896]{1,0:T(8,128)(2,1)} %slice.72), channel_id=1, source_target_pairs={{0,4},{4,0},{8,12},{12,8},{16,20},{20,16},{24,28},{28,24},{1,5},{5... | collective-permute-start | bytes 1204232 | tf_op jit(solution)/shard_map/ppermute | solution.py:18
  7.5 8.4 %collective-permute-start.3 = (bf16[2,128,512]{2,1,0:T(8,128)(2,1)S(1)}, bf16[2,128,512]{2,1,0:T(8,128)(2,1)S(1)}, u32[]{:S(2)}, u32[]{:S(2)}) collective-permute-start(bf16[2,128,512]{2,1,0:T(8,128)(2,1)S(1)} %pad_maximum_fusion.3), channel_id=1, source_target_pairs={{0,2},{1,3},{2,0},{3,1},{4,6},{5,7},{6,4},{7,5},{8,10},{9,11},{10,... | collective-permute-start | bytes 786440 | tf_op jit(solution)/shard_map/ppermute | solution.py:18
  16.8 17.5 %collective-permute-start.6 = (bf16[288,896]{1,0:T(8,128)(2,1)}, bf16[288,896]{1,0:T(8,128)(2,1)S(1)}, u32[]{:S(2)}, u32[]{:S(2)}) collective-permute-start(bf16[288,896]{1,0:T(8,128)(2,1)} %slice.71), channel_id=1, source_target_pairs={{0,4},{4,0},{8,12},{12,8},{16,20},{20,16},{24,28},{28,24},{1,5},{5... | collective-permute-start | bytes 1548296 | tf_op jit(solution)/shard_map/ppermute | solution.py:18
  18.6 16.3 %collective-permute-start.2 = (bf16[2,128,512]{2,1,0:T(8,128)(2,1)S(1)}, bf16[2,128,512]{2,1,0:T(8,128)(2,1)S(1)}, u32[]{:S(2)}, u32[]{:S(2)}) collective-permute-start(bf16[2,128,512]{2,1,0:T(8,128)(2,1)S(1)} %pad_maximum_fusion.2), channel_id=1, source_target_pairs={{0,2},{1,3},{2,0},{3,1},{4,6},{5,7},{6,4},{7,5},{8,10},{9,11},{10,... | collective-permute-start | bytes 786440 | tf_op jit(solution)/shard_map/ppermute | solution.py:18
  20.3 14.5 %collective-permute-start.4 = (bf16[128,512]{1,0:T(8,128)(2,1)S(1)}, bf16[128,512]{1,0:T(8,128)(2,1)S(1)}, u32[]{:S(2)}, u32[]{:S(2)}) collective-permute-start(bf16[128,512]{1,0:T(8,128)(2,1)S(1)} %get-tuple-element.141), channel_id=1, source_target_pairs={{0,24},{4,28},{8,16},{12,20},{16,8},{20,12},{24,0},{28,4},{1,25},{... | collective-permute-start | bytes 393224 | tf_op jit(solution)/shard_map/ppermute | solution.py:18
  24.0 10.3 %collective-permute-start.7 = (bf16[128,512]{1,0:T(8,128)(2,1)S(1)}, bf16[128,512]{1,0:T(8,128)(2,1)S(1)}, u32[]{:S(2)}, u32[]{:S(2)}) collective-permute-start(bf16[128,512]{1,0:T(8,128)(2,1)S(1)} %get-tuple-element.140), channel_id=1, source_target_pairs={{0,16},{4,20},{8,24},{12,28},{16,0},{20,4},{24,8},{28,12},{1,17},{... | collective-permute-start | bytes 393224 | tf_op jit(solution)/shard_map/ppermute | solution.py:18
  24.0 7.7 %collective-permute-start.8 = (bf16[128,512]{1,0:T(8,128)(2,1)S(1)}, bf16[128,512]{1,0:T(8,128)(2,1)S(1)}, u32[]{:S(2)}, u32[]{:S(2)}) collective-permute-start(bf16[128,512]{1,0:T(8,128)(2,1)S(1)} %get-tuple-element.139), channel_id=1, source_target_pairs={{0,8},{4,12},{8,0},{12,4},{16,24},{20,28},{24,16},{28,20},{1,9},{5... | collective-permute-start | bytes 393224 | tf_op jit(solution)/shard_map/ppermute | solution.py:18
  31.6 3.5 %collective-permute-start.13 = (bf16[128,512]{1,0:T(8,128)(2,1)S(1)}, bf16[128,512]{1,0:T(8,128)(2,1)S(1)}, u32[]{:S(2)}, u32[]{:S(2)}) collective-permute-start(bf16[128,512]{1,0:T(8,128)(2,1)S(1)} %get-tuple-element.138), channel_id=1, source_target_pairs={{0,1},{1,0},{2,3},{3,2},{4,5},{5,4},{6,7},{7,6},{8,9},{9,8},{10,11... | collective-permute-start | bytes 393224 | tf_op jit(solution)/shard_map/ppermute | solution.py:18
  34.3 3.8 %collective-permute-start.12 = (bf16[128,512]{1,0:T(8,128)(2,1)S(1)}, bf16[128,512]{1,0:T(8,128)(2,1)S(1)}, u32[]{:S(2)}, u32[]{:S(2)}) collective-permute-start(bf16[128,512]{1,0:T(8,128)(2,1)S(1)} %collective-permute-done.8), channel_id=1, source_target_pairs={{0,1},{1,0},{2,3},{3,2},{4,5},{5,4},{6,7},{7,6},{8,9},{9,8},{10,11... | collective-permute-start | bytes 393224 | tf_op jit(solution)/shard_map/ppermute | solution.py:18
  34.3 3.8 %collective-permute-start.15 = (bf16[128,512]{1,0:T(8,128)(2,1)S(1)}, bf16[128,512]{1,0:T(8,128)(2,1)S(1)}, u32[]{:S(2)}, u32[]{:S(2)}) collective-permute-start(bf16[128,512]{1,0:T(8,128)(2,1)S(1)} %collective-permute-done.7), channel_id=1, source_target_pairs={{0,1},{1,0},{2,3},{3,2},{4,5},{5,4},{6,7},{7,6},{8,9},{9,8},{10,11... | collective-permute-start | bytes 393224 | tf_op jit(solution)/shard_map/ppermute | solution.py:18
  34.8 5.4 %collective-permute-start.14 = (bf16[128,512]{1,0:T(8,128)(2,1)S(1)}, bf16[128,512]{1,0:T(8,128)(2,1)S(1)}, u32[]{:S(2)}, u32[]{:S(2)}) collective-permute-start(bf16[128,512]{1,0:T(8,128)(2,1)S(1)} %collective-permute-done.4), channel_id=1, source_target_pairs={{0,1},{1,0},{2,3},{3,2},{4,5},{5,4},{6,7},{7,6},{8,9},{9,8},{10,11... | collective-permute-start | bytes 393224 | tf_op jit(solution)/shard_map/ppermute | solution.py:18
  35.0 13.9 %collective-permute-start.18 = (bf16[128,512]{1,0:T(8,128)(2,1)S(1)}, bf16[128,512]{1,0:T(8,128)(2,1)S(1)}, u32[]{:S(2)}, u32[]{:S(2)}) collective-permute-start(bf16[128,512]{1,0:T(8,128)(2,1)S(1)} %get-tuple-element.136), channel_id=1, source_target_pairs={{0,16},{4,20},{8,24},{12,28},{16,0},{20,4},{24,8},{28,12},{1,17},{... | collective-permute-start | bytes 393224 | tf_op jit(solution)/shard_map/ppermute | solution.py:18
  35.1 12.5 %collective-permute-start.19 = (bf16[128,512]{1,0:T(8,128)(2,1)S(1)}, bf16[128,512]{1,0:T(8,128)(2,1)S(1)}, u32[]{:S(2)}, u32[]{:S(2)}) collective-permute-start(bf16[128,512]{1,0:T(8,128)(2,1)S(1)} %get-tuple-element.135), channel_id=1, source_target_pairs={{0,8},{4,12},{8,0},{12,4},{16,24},{20,28},{24,16},{28,20},{1,9},{5... | collective-permute-start | bytes 393224 | tf_op jit(solution)/shard_map/ppermute | solution.py:18
  38.1 19.3 %collective-permute-start.11 = (bf16[512,512]{1,0:T(8,128)(2,1)S(1)}, bf16[512,512]{1,0:T(8,128)(2,1)S(1)}, u32[]{:S(2)}, u32[]{:S(2)}) collective-permute-start(bf16[512,512]{1,0:T(8,128)(2,1)S(1)} %copy-done.10), channel_id=1, source_target_pairs={{0,4},{4,0},{8,12},{12,8},{16,20},{20,16},{24,28},{28,24},{1,5},{5... | collective-permute-start | bytes 1572872 | tf_op jit(solution)/shard_map/ppermute | solution.py:18
  38.7 10.3 %collective-permute-start.17 = (bf16[128,512]{1,0:T(8,128)(2,1)S(1)}, bf16[128,512]{1,0:T(8,128)(2,1)S(1)}, u32[]{:S(2)}, u32[]{:S(2)}) collective-permute-start(bf16[128,512]{1,0:T(8,128)(2,1)S(1)} %get-tuple-element.134), channel_id=1, source_target_pairs={{0,24},{4,28},{8,16},{12,20},{16,8},{20,12},{24,0},{28,4},{1,25},{... | collective-permute-start | bytes 393224 | tf_op jit(solution)/shard_map/ppermute | solution.py:18
  41.1 16.2 %collective-permute-start.16 = (bf16[2,128,896]{2,1,0:T(8,128)(2,1)S(1)}, bf16[2,128,896]{2,1,0:T(8,128)(2,1)S(1)}, u32[]{:S(2)}, u32[]{:S(2)}) collective-permute-start(bf16[2,128,896]{2,1,0:T(8,128)(2,1)S(1)} %bitcast.156), channel_id=1, source_target_pairs={{0,8},{4,12},{8,0},{12,4},{16,24},{20,28},{24,16},{28,20},{1,9},{5... | collective-permute-start | bytes 1376264 | tf_op jit(solution)/shard_map/ppermute | solution.py:18
  47.6 10.3 %collective-permute-start.10 = (bf16[2,128,256]{2,1,0:T(8,128)(2,1)S(1)}, bf16[2,128,256]{2,1,0:T(8,128)(2,1)S(1)}, u32[]{:S(2)}, u32[]{:S(2)}) collective-permute-start(bf16[2,128,256]{2,1,0:T(8,128)(2,1)S(1)} %maximum_select_fusion), channel_id=1, source_target_pairs={{0,1},{4,5},{8,9},{12,13},{16,17},{20,21},{24,25},{28,29}} | collective-permute-start | bytes 393224 | tf_op jit(solution)/shard_map/ppermute | solution.py:114
  48.9 9.0 %collective-permute-start.9 = (bf16[128,512]{1,0:T(8,128)(2,1)S(1)}, bf16[128,512]{1,0:T(8,128)(2,1)S(1)}, u32[]{:S(2)}, u32[]{:S(2)}) collective-permute-start(bf16[128,512]{1,0:T(8,128)(2,1)S(1)} %get-tuple-element.137), channel_id=1, source_target_pairs={{0,1},{1,0},{2,3},{3,2},{4,5},{5,4},{6,7},{7,6},{8,9},{9,8},{10,11... | collective-permute-start | bytes 393224 | tf_op jit(solution)/shard_map/ppermute | solution.py:18
  49.0 8.9 %collective-permute-start.21 = (bf16[128,512]{1,0:T(8,128)(2,1)S(1)}, bf16[128,512]{1,0:T(8,128)(2,1)S(1)}, u32[]{:S(2)}, u32[]{:S(2)}) collective-permute-start(bf16[128,512]{1,0:T(8,128)(2,1)S(1)} %collective-permute-done.19), channel_id=1, source_target_pairs={{0,1},{1,0},{2,3},{3,2},{4,5},{5,4},{6,7},{7,6},{8,9},{9,8},{10,11... | collective-permute-start | bytes 393224 | tf_op jit(solution)/shard_map/ppermute | solution.py:18
  57.4 4.5 %collective-permute-start.24 = (bf16[128,512]{1,0:T(8,128)(2,1)S(1)}, bf16[128,512]{1,0:T(8,128)(2,1)S(1)}, u32[]{:S(2)}, u32[]{:S(2)}) collective-permute-start(bf16[128,512]{1,0:T(8,128)(2,1)S(1)} %collective-permute-done.17), channel_id=1, source_target_pairs={{0,1},{1,0},{2,3},{3,2},{4,5},{5,4},{6,7},{7,6},{8,9},{9,8},{10,11... | collective-permute-start | bytes 393224 | tf_op jit(solution)/shard_map/ppermute | solution.py:18
  58.7 11.2 %collective-permute-start.22 = (bf16[384,512]{1,0:T(8,128)(2,1)S(1)}, bf16[384,512]{1,0:T(8,128)(2,1)S(1)}, u32[]{:S(2)}, u32[]{:S(2)}) collective-permute-start(bf16[384,512]{1,0:T(8,128)(2,1)S(1)} %copy-done.13), channel_id=1, source_target_pairs={{0,4},{4,0},{8,12},{12,8},{16,20},{20,16},{24,28},{28,24},{1,5},{5... | collective-permute-start | bytes 1179656 | tf_op jit(solution)/shard_map/ppermute | solution.py:18
  59.2 5.2 %collective-permute-start.23 = (bf16[2,128,256]{2,1,0:T(8,128)(2,1)S(1)}, bf16[2,128,256]{2,1,0:T(8,128)(2,1)S(1)}, u32[]{:S(2)}, u32[]{:S(2)}) collective-permute-start(bf16[2,128,256]{2,1,0:T(8,128)(2,1)S(1)} %fusion.117), channel_id=1, source_target_pairs={{0,2},{1,3},{4,6},{5,7},{8,10},{9,11},{12,14},{13,15},{16,18},{17,... | collective-permute-start | bytes 393224 | tf_op jit(solution)/shard_map/ppermute | solution.py:175
  62.1 12.1 %collective-permute-start.26 = (bf16[1,128,896]{2,1,0:T(8,128)(2,1)S(1)}, bf16[1,128,896]{2,1,0:T(8,128)(2,1)S(1)}, u32[]{:S(2)}, u32[]{:S(2)}) collective-permute-start(bf16[1,128,896]{2,1,0:T(8,128)(2,1)S(1)} %slice.130), channel_id=1, source_target_pairs={{0,16},{4,20},{8,24},{12,28},{16,0},{20,4},{24,8},{28,12},{1,17},{... | collective-permute-start | bytes 688136 | tf_op jit(solution)/shard_map/ppermute | solution.py:18
  70.4 13.5 %collective-permute-start.25 = (bf16[2,128,896]{2,1,0:T(8,128)(2,1)S(1)}, bf16[2,128,896]{2,1,0:T(8,128)(2,1)S(1)}, u32[]{:S(2)}, u32[]{:S(2)}) collective-permute-start(bf16[2,128,896]{2,1,0:T(8,128)(2,1)S(1)} %bitcast.157), channel_id=1, source_target_pairs={{0,8},{4,12},{8,0},{12,4},{16,24},{20,28},{24,16},{28,20},{1,9},{5... | collective-permute-start | bytes 1376264 | tf_op jit(solution)/shard_map/ppermute | solution.py:18
  76.0 10.0 %collective-permute-start.28 = (f32[32,896]{1,0:T(8,128)S(1)}, f32[32,896]{1,0:T(8,128)S(1)}, u32[]{:S(2)}, u32[]{:S(2)}) collective-permute-start(f32[32,896]{1,0:T(8,128)S(1)} %convolution_bitcast_fusion), channel_id=1, source_target_pairs={{0,4},{4,0},{8,12},{12,8},{16,20},{20,16},{24,28},{28,24},{1,5},{5... | collective-permute-start | bytes 344072 | tf_op jit(solution)/shard_map/ppermute | solution.py:18
  85.6 14.6 %collective-permute-start.27 = (bf16[1,128,896]{2,1,0:T(8,128)(2,1)}, bf16[1,128,896]{2,1,0:T(8,128)(2,1)}, u32[]{:S(2)}, u32[]{:S(2)}) collective-permute-start(bf16[1,128,896]{2,1,0:T(8,128)(2,1)} %slice.129), channel_id=1, source_target_pairs={{0,16},{4,20},{8,24},{12,28},{16,0},{20,4},{24,8},{28,12},{1,17},{... | collective-permute-start | bytes 688136 | tf_op jit(solution)/shard_map/ppermute | solution.py:18
  86.0 7.7 %collective-permute-start.29 = (f32[32,896]{1,0:T(8,128)S(1)}, f32[32,896]{1,0:T(8,128)S(1)}, u32[]{:S(2)}, u32[]{:S(2)}) collective-permute-start(f32[32,896]{1,0:T(8,128)S(1)} %add.147), channel_id=1, source_target_pairs={{0,8},{4,12},{8,0},{12,4},{16,24},{20,28},{24,16},{28,20},{1,9},{5... | collective-permute-start | bytes 344072 | tf_op jit(solution)/shard_map/ppermute | solution.py:18
  93.7 14.8 %collective-permute-start.31 = (f32[32,896]{1,0:T(8,128)S(1)}, f32[32,896]{1,0:T(8,128)S(1)}, u32[]{:S(2)}, u32[]{:S(2)}) collective-permute-start(f32[32,896]{1,0:T(8,128)S(1)} %add.152), channel_id=1, source_target_pairs={{0,16},{4,20},{8,24},{12,28},{16,0},{20,4},{24,8},{28,12},{1,17},{... | collective-permute-start | bytes 344072 | tf_op jit(solution)/shard_map/ppermute | solution.py:18
  102.0 11.7 %collective-permute-start.33 = (bf16[128,896]{1,0:T(8,128)(2,1)S(1)}, bf16[128,896]{1,0:T(8,128)(2,1)S(1)}, u32[]{:S(2)}, u32[]{:S(2)}) collective-permute-start(bf16[128,896]{1,0:T(8,128)(2,1)S(1)} %fusion.8), channel_id=1, source_target_pairs={{0,16},{4,20},{8,24},{12,28},{16,0},{20,4},{24,8},{28,12},{1,17},{... | collective-permute-start | bytes 688136 | tf_op jit(solution)/shard_map/ppermute | solution.py:18
  102.0 12.8 %collective-permute-start.35 = (bf16[128,896]{1,0:T(8,128)(2,1)S(1)}, bf16[128,896]{1,0:T(8,128)(2,1)S(1)}, u32[]{:S(2)}, u32[]{:S(2)}) collective-permute-start(bf16[128,896]{1,0:T(8,128)(2,1)S(1)} %fusion.8), channel_id=1, source_target_pairs={{0,8},{4,12},{8,0},{12,4},{16,24},{20,28},{24,16},{28,20},{1,9},{5... | collective-permute-start | bytes 688136 | tf_op jit(solution)/shard_map/ppermute | solution.py:18
  110.6 5.5 %collective-permute-start.37 = (f32[32,544]{1,0:T(8,128)S(1)}, f32[32,544]{1,0:T(8,128)S(1)}, u32[]{:S(2)}, u32[]{:S(2)}) collective-permute-start(f32[32,544]{1,0:T(8,128)S(1)} %fusion.69), channel_id=1, source_target_pairs={{0,2},{1,3},{2,0},{3,1},{4,6},{5,7},{6,4},{7,5},{8,10},{9,11},{10,... | collective-permute-start | bytes 208904 | tf_op jit(solution)/shard_map/ppermute | solution.py:18
  114.5 6.3 %collective-permute-start.34 = (bf16[128,512]{1,0:T(8,128)(2,1)S(1)}, bf16[128,512]{1,0:T(8,128)(2,1)S(1)}, u32[]{:S(2)}, u32[]{:S(2)}) collective-permute-start(bf16[128,512]{1,0:T(8,128)(2,1)S(1)} %get-tuple-element.166), channel_id=1, source_target_pairs={{0,1},{1,0},{2,3},{3,2},{4,5},{5,4},{6,7},{7,6},{8,9},{9,8},{10,11... | collective-permute-start | bytes 393224 | tf_op jit(solution)/shard_map/ppermute | solution.py:18
  115.7 5.1 %collective-permute-start.36 = (bf16[128,512]{1,0:T(8,128)(2,1)S(1)}, bf16[128,512]{1,0:T(8,128)(2,1)S(1)}, u32[]{:S(2)}, u32[]{:S(2)}) collective-permute-start(bf16[128,512]{1,0:T(8,128)(2,1)S(1)} %get-tuple-element.168), channel_id=1, source_target_pairs={{0,1},{1,0},{2,3},{3,2},{4,5},{5,4},{6,7},{7,6},{8,9},{9,8},{10,11... | collective-permute-start | bytes 393224 | tf_op jit(solution)/shard_map/ppermute | solution.py:18
  116.1 4.7 %collective-permute-start.38 = (f32[32,544]{1,0:T(8,128)S(1)}, f32[32,544]{1,0:T(8,128)S(1)}, u32[]{:S(2)}, u32[]{:S(2)}) collective-permute-start(f32[32,544]{1,0:T(8,128)S(1)} %add.156), channel_id=1, source_target_pairs={{0,4},{4,0},{8,12},{12,8},{16,20},{20,16},{24,28},{28,24},{1,5},{5... | collective-permute-start | bytes 208904 | tf_op jit(solution)/shard_map/ppermute | solution.py:18
  117.7 11.2 %collective-permute-start.41 = (bf16[128,896]{1,0:T(8,128)(2,1)S(1)}, bf16[128,896]{1,0:T(8,128)(2,1)S(1)}, u32[]{:S(2)}, u32[]{:S(2)}) collective-permute-start(bf16[128,896]{1,0:T(8,128)(2,1)S(1)} %collective-permute-done.33), channel_id=1, source_target_pairs={{0,8},{4,12},{8,0},{12,4},{16,24},{20,28},{24,16},{28,20},{1,9},{5... | collective-permute-start | bytes 688136 | tf_op jit(solution)/shard_map/ppermute | solution.py:18
  120.8 9.0 %collective-permute-start.40 = (f32[32,544]{1,0:T(8,128)S(1)}, f32[32,544]{1,0:T(8,128)S(1)}, u32[]{:S(2)}, u32[]{:S(2)}) collective-permute-start(f32[32,544]{1,0:T(8,128)S(1)} %add.158), channel_id=1, source_target_pairs={{0,8},{4,12},{8,0},{12,4},{16,24},{20,28},{24,16},{28,20},{1,9},{5... | collective-permute-start | bytes 208904 | tf_op jit(solution)/shard_map/ppermute | solution.py:18
  120.9 15.8 %collective-permute-start.39 = (bf16[128,512]{1,0:T(8,128)(2,1)S(1)}, bf16[128,512]{1,0:T(8,128)(2,1)S(1)}, u32[]{:S(2)}, u32[]{:S(2)}) collective-permute-start(bf16[128,512]{1,0:T(8,128)(2,1)S(1)} %add_convert_fusion.2), channel_id=1, source_target_pairs={{0,16},{4,20},{8,24},{12,28},{16,0},{20,4},{24,8},{28,12},{1,17},{... | collective-permute-start | bytes 393224 | tf_op jit(solution)/shard_map/ppermute | solution.py:18
  129.8 5.5 %collective-permute-start.42 = (f32[32,544]{1,0:T(8,128)S(1)}, f32[32,544]{1,0:T(8,128)S(1)}, u32[]{:S(2)}, u32[]{:S(2)}) collective-permute-start(f32[32,544]{1,0:T(8,128)S(1)} %add.159), channel_id=1, source_target_pairs={{0,16},{4,20},{8,24},{12,28},{16,0},{20,4},{24,8},{28,12},{1,17},{... | collective-permute-start | bytes 208904 | tf_op jit(solution)/shard_map/ppermute | solution.py:18
  130.3 2.7 %collective-permute-start.43 = (bf16[128,512]{1,0:T(8,128)(2,1)S(1)}, bf16[128,512]{1,0:T(8,128)(2,1)S(1)}, u32[]{:S(2)}, u32[]{:S(2)}) collective-permute-start(bf16[128,512]{1,0:T(8,128)(2,1)S(1)} %get-tuple-element.170), channel_id=1, source_target_pairs={{0,1},{1,0},{2,3},{3,2},{4,5},{5,4},{6,7},{7,6},{8,9},{9,8},{10,11... | collective-permute-start | bytes 393224 | tf_op jit(solution)/shard_map/ppermute | solution.py:18
  130.5 14.3 %collective-permute-start.47 = (bf16[128,512]{1,0:T(8,128)(2,1)S(1)}, bf16[128,512]{1,0:T(8,128)(2,1)S(1)}, u32[]{:S(2)}, u32[]{:S(2)}) collective-permute-start(bf16[128,512]{1,0:T(8,128)(2,1)S(1)} %add_convert_fusion), channel_id=1, source_target_pairs={{0,8},{4,12},{8,0},{12,4},{16,24},{20,28},{24,16},{28,20},{1,9},{5... | collective-permute-start | bytes 393224 | tf_op jit(solution)/shard_map/ppermute | solution.py:18
  136.8 12.4 %collective-permute-start.44 = (bf16[1,128,512]{2,1,0:T(8,128)(2,1)S(1)}, bf16[1,128,512]{2,1,0:T(8,128)(2,1)S(1)}, u32[]{:S(2)}, u32[]{:S(2)}) collective-permute-start(bf16[1,128,512]{2,1,0:T(8,128)(2,1)S(1)} %fusion.49), channel_id=1, source_target_pairs={{0,2},{1,3},{2,0},{3,1},{4,6},{5,7},{6,4},{7,5},{8,10},{9,11},{10,... | collective-permute-start | bytes 393224 | tf_op jit(solution)/shard_map/ppermute | solution.py:18
  142.2 7.0 %collective-permute-start.45 = (bf16[32,896]{1,0:T(8,128)(2,1)S(1)}, bf16[32,896]{1,0:T(8,128)(2,1)S(1)}, u32[]{:S(2)}, u32[]{:S(2)}) collective-permute-start(bf16[32,896]{1,0:T(8,128)(2,1)S(1)} %convolution_convert_fusion.8), channel_id=1, source_target_pairs={{0,4},{4,0},{8,12},{12,8},{16,20},{20,16},{24,28},{28,24},{1,5},{5... | collective-permute-start | bytes 172040 | tf_op jit(solution)/shard_map/ppermute | solution.py:18
  142.3 6.8 %collective-permute-start.46 = (bf16[128,512]{1,0:T(8,128)(2,1)S(1)}, bf16[128,512]{1,0:T(8,128)(2,1)S(1)}, u32[]{:S(2)}, u32[]{:S(2)}) collective-permute-start(bf16[128,512]{1,0:T(8,128)(2,1)S(1)} %add_convert_fusion.1), channel_id=1, source_target_pairs={{0,24},{4,28},{8,16},{12,20},{16,8},{20,12},{24,0},{28,4},{1,25},{... | collective-permute-start | bytes 393224 | tf_op jit(solution)/shard_map/ppermute | solution.py:18
  149.2 5.1 %collective-permute-start.48 = (bf16[1,128,512]{2,1,0:T(8,128)(2,1)S(1)}, bf16[1,128,512]{2,1,0:T(8,128)(2,1)S(1)}, u32[]{:S(2)}, u32[]{:S(2)}) collective-permute-start(bf16[1,128,512]{2,1,0:T(8,128)(2,1)S(1)} %fusion.46), channel_id=1, source_target_pairs={{0,2},{1,3},{2,0},{3,1},{4,6},{5,7},{6,4},{7,5},{8,10},{9,11},{10,... | collective-permute-start | bytes 393224 | tf_op jit(solution)/shard_map/ppermute | solution.py:18
  151.4 4.2 %collective-permute-start.50 = (bf16[32,896]{1,0:T(8,128)(2,1)S(1)}, bf16[32,896]{1,0:T(8,128)(2,1)S(1)}, u32[]{:S(2)}, u32[]{:S(2)}) collective-permute-start(bf16[32,896]{1,0:T(8,128)(2,1)S(1)} %add_convert_fusion.5), channel_id=1, source_target_pairs={{0,8},{4,12},{8,0},{12,4},{16,24},{20,28},{24,16},{28,20},{1,9},{5... | collective-permute-start | bytes 172040 | tf_op jit(solution)/shard_map/ppermute | solution.py:18
  154.5 3.3 %collective-permute-start.49 = (bf16[128,512]{1,0:T(8,128)(2,1)S(1)}, bf16[128,512]{1,0:T(8,128)(2,1)S(1)}, u32[]{:S(2)}, u32[]{:S(2)}) collective-permute-start(bf16[128,512]{1,0:T(8,128)(2,1)S(1)} %get-tuple-element.131), channel_id=1, source_target_pairs={{0,1},{1,0},{2,3},{3,2},{4,5},{5,4},{6,7},{7,6},{8,9},{9,8},{10,11... | collective-permute-start | bytes 393224 | tf_op jit(solution)/shard_map/ppermute | solution.py:18
  155.7 5.2 %collective-permute-start.51 = (bf16[32,896]{1,0:T(8,128)(2,1)S(1)}, bf16[32,896]{1,0:T(8,128)(2,1)S(1)}, u32[]{:S(2)}, u32[]{:S(2)}) collective-permute-start(bf16[32,896]{1,0:T(8,128)(2,1)S(1)} %add_convert_fusion.4), channel_id=1, source_target_pairs={{0,16},{4,20},{8,24},{12,28},{16,0},{20,4},{24,8},{28,12},{1,17},{... | collective-permute-start | bytes 172040 | tf_op jit(solution)/shard_map/ppermute | solution.py:18
  (23 other events, 234.5 us)

commit v5 on v4

--- a/solution.py
+++ b/solution.py
@@ -1,3 +1,4 @@
+import functools
 import math
 
 import jax
@@ -26,14 +27,19 @@
     return lax.dot_general(a, b, (dims, ((), ())), preferred_element_type=F32, precision=precision)
 
 
-def factor_kernel(up_ref, down_ref, up_out, down_out):
-    rank = up_ref.shape[0]
+def factor_kernel(replicas, sums_ref, left_out, down_out):
+    rank = down_out.shape[0]
+    window = left_out.shape[1]
+    up_sum = sums_ref[:, :window]
+    grams = (
+        dot(up_sum, up_sum, ((1,), (1,)), HIGHEST),
+        sums_ref[:, 2 * window :] * (1.0 / replicas),
+    )
     row_id = lax.broadcasted_iota(jnp.int32, (rank, 2 * rank), 0)
     col_id = lax.broadcasted_iota(jnp.int32, (rank, 2 * rank), 1)
     eye = (row_id + rank == col_id).astype(F32)
     state = [
-        eye + jnp.concatenate([ref[...], jnp.zeros((rank, rank), F32)], axis=1)
-        for ref in (up_ref, down_ref)
+        eye + jnp.concatenate([gram, jnp.zeros((rank, rank), F32)], axis=1) for gram in grams
     ]
     for j in range(rank):
         for n in range(2):
@@ -42,18 +48,21 @@
             row = aug[j : j + 1, :] * root
             col = aug[:, j : j + 1] * root
             state[n] = jnp.where(row_id > j, aug - col * row, jnp.where(row_id == j, row, aug))
-    up_out[...] = state[0][:, rank:]
+    left_out[...] = dot(state[0][:, rank:], up_sum, precision=HIGHEST)
     down_out[...] = state[1][:, rank:]
 
 
-def inverse_factors(up_gram, down_gram):
-    shape = jax.ShapeDtypeStruct(up_gram.shape, F32)
+def factors(sums, window, replicas):
+    rank = sums.shape[0]
     return pl.pallas_call(
-        factor_kernel,
-        out_shape=(shape, shape),
-        name="inverse_factors",
+        functools.partial(factor_kernel, replicas),
+        out_shape=(
+            jax.ShapeDtypeStruct((rank, window), F32),
+            jax.ShapeDtypeStruct((rank, rank), F32),
+        ),
+        name="factors",
         cost_estimate=pl.CostEstimate(flops=10**6, bytes_accessed=20000, transcendentals=64),
-    )(up_gram, down_gram)
+    )(sums)
 
 
 class Order:
@@ -189,11 +198,15 @@
     slope = squash * (1.0 + preact * (1.0 - squash))
     down_matrix = down_accum[0] + dot(act_out, grad_win, ((0,), (0,))) * scale
     down_sum = dot(down_q, down_matrix, ((0,), (1,)), HIGH)
+    down_sum = down_sum.astype(BF)
     down_got = flip(down_sum, "dp", 1)
     back_acc = back_acc + wait(back_got).astype(F32)
-    down_sum = down_sum + wait(down_got)
+    slope, back_acc = tie(slope, back_acc)
+    down_sum = down_sum.astype(F32) + wait(down_got).astype(F32)
     for mask in dbits[1:-1]:
-        down_sum = down_sum + wait(flip(down_sum, "dp", mask))
+        down_sum = down_sum.astype(BF)
+        down_sum = down_sum.astype(F32) + wait(flip(down_sum, "dp", mask)).astype(F32)
+    down_sum = down_sum.astype(BF)
     down_got = flip(down_sum, "dp", dbits[-1])
     back_act = later_stages(back_acc)
     hidden = wait((back_act * slope).astype(BF))
@@ -237,7 +250,7 @@
     coming = forward(first)
     up_matrix = up_accum[0] + dot(tok_win, hidden, ((0,), (0,))) * scale
     both = dot(up_q, up_matrix, ((0,), (1,)), HIGH)
-    down_sum = down_sum + wait(down_got)
+    down_sum = down_sum.astype(F32) + wait(down_got).astype(F32)
     down_gram = dot(down_sum, down_sum, ((1,), (1,)), HIGHEST)
     down_term = dot(down_sum, down_matrix, ((1,), (0,)), HIGH)
     both = jnp.concatenate([both, down_term, down_gram], axis=1)
@@ -271,16 +284,13 @@
         mine, got = pending[k]
         send_back(k, mine, wait(got))
     both = both + wait(both_got)
-    up_sum, down_term, down_gram = both[:, :window], both[:, window : 2 * window], both[:, 2 * window :]
-    up_inv, down_inv = inverse_factors(
-        dot(up_sum, up_sum, ((1,), (1,)), HIGHEST), down_gram / replicas
-    )
+    down_term = both[:, window : 2 * window]
+    up_left, down_inv = factors(both, window, replicas)
 
     def scaled(inv, arr):
         return dot(inv, arr, precision=HIGHEST)
 
     outer = ((0,), (0,))
-    up_left = scaled(up_inv, up_sum)
     up_right = dot(up_left, up_matrix, ((1,), (0,)), HIGH).astype(BF)
     right_got = flip(up_right, "dp", 1)
     level = after
@@ -295,20 +305,21 @@
         level = after
     returned.update({k: wait(returned[k]) for k in even[1:]})
     pair_a = settle(even)
-    returned.update({k: wait(returned[k]) for k in odd})
-    pair_b = settle(odd)
     up_right = up_right.astype(F32) + wait(right_got).astype(F32)
+    down_inv, wait.last = tie(down_inv, wait.last)
+    low = zrel & 1
     for n, mask in enumerate(dbits[1:]):
         up_right = up_right.astype(BF)
         right_got = flip(up_right, "dp", mask)
         if n == 0:
+            returned.update({k: wait(returned[k]) for k in odd})
+            pair_b = settle(odd)
+        if n == 1:
             sum_a, sum_b = add_pair(pair_a), add_pair(pair_b)
-            low = zrel & 1
             got = flip(jnp.where(low == 0, sum_b, sum_a), "tensor", 1)
-        if n == 1:
-            got = wait(got)
         up_right = up_right.astype(F32) + wait(right_got).astype(F32)
     own = jnp.where(low == 0, sum_a, sum_b)
+    got = wait(got)
     input_grad = jnp.concatenate(
         [jnp.where(half == 0, own, got), jnp.where(half == 0, got, own)], axis=1
     )

time: 164 us -> 164 us (level)
  waiting for transfers between devices: 82.8 us -> 68.1 us
  starting transfers between devices: 46.1 us -> 52.9 us
  other arithmetic: 5.53 us -> 10.5 us
  matrix products: 14.7 us -> 16.8 us
    ppermute x50, waiting for transfers between devices: 81.9 us -> 66.5 us  [flip(): return lax.ppermute(arr, axis, [(i, i ^ mask) for i in range(size)])]
    ppermute x50, starting transfers between devices: 42.3 us -> 47.4 us  [flip(): return lax.ppermute(arr, axis, [(i, i ^ mask) for i in range(size)])]
    add x4, other arithmetic: 0.04 us -> 2.24 us  [shards(): both = both + wait(both_got)]
    dot_general x29 -> x27, matrix products: 14.7 us -> 16.8 us  [dot(): lax.dot_general(a, b, (dims, ((), ())), preferred_element_type=F32, preci...]
    convert_element_type x3, other arithmetic: 0.16 us -> 2.02 us  [send_back(): mine = (mine.astype(F32) + got.astype(F32)).astype(BF)]
  transfers between devices with their start and end apart: 52 -> 52, of which waited for: 26 -> 25; matrix products, arithmetic and copies ran while one was open for 14% -> 19% of each run, Pallas kernels for 2% -> 3%
where the time goes in v5:
time: 164 us; the launch traced here: 163 us
  waiting for transfers between devices  68.1 us (42%)
  starting transfers between devices  52.9 us (32%)
  matrix products  16.8 us (10%)
  other arithmetic  10.5 us (6%)
  local copies, waits for them, and re-layouts  8.81 us (5%)
  Pallas kernels  4.62 us (3%)
    ppermute x50, waiting for transfers between devices, flip(): return lax.ppermute(arr, axis, [(i, i ^ mask) for i in range(size)])  66.5 us
    ppermute x50, starting transfers between devices, flip(): return lax.ppermute(arr, axis, [(i, i ^ mask) for i in range(size)])  47.4 us
    dot_general x27, matrix products, dot(): lax.dot_general(a, b, (dims, ((), ())), preferred_element_type=F32, preci...  16.8 us
    pallas_call x1, Pallas kernels, factors(): pl.pallas_call(functools.partial(factor_kernel, replicas), out_shape=(jax...  4.62 us
    ppermute x1, starting transfers between devices, shards(): lax.ppermute(windows, 'tensor', [(i, i + mask) for i in range(mask)])  3.68 us
  transfers between devices with their start and end apart: 52, of which 25 were waited for; matrix products, arithmetic and copies ran while one was open for 19% of the time, Pallas kernels for 3%

profile of v5, /device:TPU:0, one launch (start us, length us, event | category | flops | bytes accessed | tf_op | source)
XLA Modules:
  0.0 163.2 jit_solution(1619063621499396359)
XLA Ops:
  3.3 2.6 %collective-permute-start.6 = (bf16[224,896]{1,0:T(8,128)(2,1)S(1)}, bf16[224,896]{1,0:T(8,128)(2,1)S(1)}, u32[]{:S(2)}, u32[]{:S(2)}) collective-permute-start(bf16[224,896]{1,0:T(8,128)(2,1)S(1)} %slice.66), channel_id=1, source_target_pairs={{0,4},{4,0},{8,12},{12,8},{16,20},{20,16},{24,28},{28,24},{1,5},{5... | collective-permute-start | bytes 1204232 | tf_op jit(solution)/shard_map/ppermute | solution.py:19
  6.8 1.6 collective-permute-start.1
  9.8 5.4 %collective-permute-done.1 = bf16[2,128,512]{2,1,0:T(8,128)(2,1)S(1)} collective-permute-done((bf16[2,128,512]{2,1,0:T(8,128)(2,1)S(1)}, bf16[2,128,512]{2,1,0:T(8,128)(2,1)S(1)}, u32[]{:S(2)}, u32[]{:S(2)}) %collective-permute-start.1) | collective-permute-done | bytes 262176 | tf_op jit(solution)/shard_map/ppermute | solution.py:19
  15.8 1.8 %collective-permute-start.7 = (bf16[288,896]{1,0:T(8,128)(2,1)}, bf16[288,896]{1,0:T(8,128)(2,1)}, u32[]{:S(2)}, u32[]{:S(2)}) collective-permute-start(bf16[288,896]{1,0:T(8,128)(2,1)} %slice.65), channel_id=1, source_target_pairs={{0,4},{4,0},{8,12},{12,8},{16,20},{20,16},{24,28},{28,24},{1,5},{5... | collective-permute-start | bytes 1548296 | tf_op jit(solution)/shard_map/ppermute | solution.py:19
  18.3 2.6 %collective-permute-start.8 = (bf16[128,512]{1,0:T(8,128)(2,1)S(1)}, bf16[128,512]{1,0:T(8,128)(2,1)}, u32[]{:S(2)}, u32[]{:S(2)}) collective-permute-start(bf16[128,512]{1,0:T(8,128)(2,1)S(1)} %get-tuple-element.144), channel_id=1, source_target_pairs={{0,16},{4,20},{8,24},{12,28},{16,0},{20,4},{24,8},{28,12},{1,17},{... | collective-permute-start | bytes 393224 | tf_op jit(solution)/shard_map/ppermute | solution.py:19
  20.9 1.6 collective-permute-start.9
  23.2 1.5 collective-permute-start.4
  27.1 1.4 collective-permute-start.5
  28.5 1.1 collective-permute-done.7
  30.6 3.7 %collective-permute-done.5 = bf16[128,512]{1,0:T(8,128)(2,1)S(1)} collective-permute-done((bf16[128,512]{1,0:T(8,128)(2,1)}, bf16[128,512]{1,0:T(8,128)(2,1)S(1)}, u32[]{:S(2)}, u32[]{:S(2)}) %collective-permute-start.5) | collective-permute-done | bytes 131104 | tf_op jit(solution)/shard_map/ppermute | solution.py:19
  36.4 1.2 collective-permute-start.14
  37.7 2.1 %collective-permute-start.15 = (bf16[128,512]{1,0:T(8,128)(2,1)S(1)}, bf16[128,512]{1,0:T(8,128)(2,1)S(1)}, u32[]{:S(2)}, u32[]{:S(2)}) collective-permute-start(bf16[128,512]{1,0:T(8,128)(2,1)S(1)} %get-tuple-element.140), channel_id=1, source_target_pairs={{0,16},{4,20},{8,24},{12,28},{16,0},{20,4},{24,8},{28,12},{1,17},{... | collective-permute-start | bytes 393224 | tf_op jit(solution)/shard_map/ppermute | solution.py:19
  39.8 1.1 collective-permute-start.16
  41.7 1.1 constant_dynamic-update-slice_fusion
  45.6 1.6 collective-permute-done.16
  47.2 1.8 %collective-permute-start.20 = (bf16[2,128,256]{2,1,0:T(8,128)(2,1)S(1)}, bf16[2,128,256]{2,1,0:T(8,128)(2,1)S(1)}, u32[]{:S(2)}, u32[]{:S(2)}) collective-permute-start(bf16[2,128,256]{2,1,0:T(8,128)(2,1)S(1)} %maximum_select_fusion), channel_id=1, source_target_pairs={{0,1},{4,5},{8,9},{12,13},{16,17},{20,21},{24,25},{28,29}} | collective-permute-start | bytes 393224 | tf_op jit(solution)/shard_map/ppermute | solution.py:123
  49.0 3.2 %collective-permute-done.15 = bf16[128,512]{1,0:T(8,128)(2,1)S(1)} collective-permute-done((bf16[128,512]{1,0:T(8,128)(2,1)S(1)}, bf16[128,512]{1,0:T(8,128)(2,1)S(1)}, u32[]{:S(2)}, u32[]{:S(2)}) %collective-permute-start.15) | collective-permute-done | bytes 131104 | tf_op jit(solution)/shard_map/ppermute | solution.py:19
  52.8 7.0 %collective-permute-done.13 = bf16[2,128,896]{2,1,0:T(8,128)(2,1)S(1)} collective-permute-done((bf16[2,128,896]{2,1,0:T(8,128)(2,1)S(1)}, bf16[2,128,896]{2,1,0:T(8,128)(2,1)S(1)}, u32[]{:S(2)}, u32[]{:S(2)}) %collective-permute-start.13) | collective-permute-done | bytes 458784 | tf_op jit(solution)/shard_map/ppermute | solution.py:19
  61.9 3.7 %collective-permute-start.21 = (bf16[2,128,256]{2,1,0:T(8,128)(2,1)S(1)}, bf16[2,128,256]{2,1,0:T(8,128)(2,1)S(1)}, u32[]{:S(2)}, u32[]{:S(2)}) collective-permute-start(bf16[2,128,256]{2,1,0:T(8,128)(2,1)S(1)} %fusion.107), channel_id=1, source_target_pairs={{0,2},{1,3},{4,6},{5,7},{8,10},{9,11},{12,14},{13,15},{16,18},{17,... | collective-permute-start | bytes 393224 | tf_op jit(solution)/shard_map/ppermute | solution.py:184
  66.7 1.6 %collective-permute-done.21 = bf16[2,128,256]{2,1,0:T(8,128)(2,1)S(1)} collective-permute-done((bf16[2,128,256]{2,1,0:T(8,128)(2,1)S(1)}, bf16[2,128,256]{2,1,0:T(8,128)(2,1)S(1)}, u32[]{:S(2)}, u32[]{:S(2)}) %collective-permute-start.21) | collective-permute-done | bytes 131104 | tf_op jit(solution)/shard_map/ppermute | solution.py:184
  68.3 4.0 %collective-permute-done.19 = bf16[384,512]{1,0:T(8,128)(2,1)S(1)} collective-permute-done((bf16[384,512]{1,0:T(8,128)(2,1)S(1)}, bf16[384,512]{1,0:T(8,128)(2,1)S(1)}, u32[]{:S(2)}, u32[]{:S(2)}) %collective-permute-start.19) | collective-permute-done | bytes 393248 | tf_op jit(solution)/shard_map/ppermute | solution.py:19
  76.5 9.4 %collective-permute-done.26 = bf16[2,128,896]{2,1,0:T(8,128)(2,1)S(1)} collective-permute-done((bf16[2,128,896]{2,1,0:T(8,128)(2,1)S(1)}, bf16[2,128,896]{2,1,0:T(8,128)(2,1)S(1)}, u32[]{:S(2)}, u32[]{:S(2)}) %collective-permute-start.26) | collective-permute-done | bytes 458784 | tf_op jit(solution)/shard_map/ppermute | solution.py:19
  86.4 2.3 %collective-permute-start.27 = (bf16[1,128,896]{2,1,0:T(8,128)(2,1)S(1)}, bf16[1,128,896]{2,1,0:T(8,128)(2,1)S(1)}, u32[]{:S(2)}, u32[]{:S(2)}) collective-permute-start(bf16[1,128,896]{2,1,0:T(8,128)(2,1)S(1)} %slice.107), channel_id=1, source_target_pairs={{0,16},{4,20},{8,24},{12,28},{16,0},{20,4},{24,8},{28,12},{1,17},{... | collective-permute-start | bytes 688136 | tf_op jit(solution)/shard_map/ppermute | solution.py:19
  88.7 2.4 %collective-permute-done.29 = bf16[32,896]{1,0:T(8,128)(2,1)S(1)} collective-permute-done((bf16[32,896]{1,0:T(8,128)(2,1)S(1)}, bf16[32,896]{1,0:T(8,128)(2,1)S(1)}, u32[]{:S(2)}, u32[]{:S(2)}) %collective-permute-start.29) | collective-permute-done | bytes 57376 | tf_op jit(solution)/shard_map/ppermute | solution.py:19
  91.4 9.3 %collective-permute-done.27 = bf16[1,128,896]{2,1,0:T(8,128)(2,1)S(1)} collective-permute-done((bf16[1,128,896]{2,1,0:T(8,128)(2,1)S(1)}, bf16[1,128,896]{2,1,0:T(8,128)(2,1)S(1)}, u32[]{:S(2)}, u32[]{:S(2)}) %collective-permute-start.27) | collective-permute-done | bytes 229408 | tf_op jit(solution)/shard_map/ppermute | solution.py:19
  102.3 2.1 %collective-permute-start.35 = (bf16[128,896]{1,0:T(8,128)(2,1)S(1)}, bf16[128,896]{1,0:T(8,128)(2,1)S(1)}, u32[]{:S(2)}, u32[]{:S(2)}) collective-permute-start(bf16[128,896]{1,0:T(8,128)(2,1)S(1)} %fusion.7), channel_id=1, source_target_pairs={{0,8},{4,12},{8,0},{12,4},{16,24},{20,28},{24,16},{28,20},{1,9},{5... | collective-permute-start | bytes 688136 | tf_op jit(solution)/shard_map/ppermute | solution.py:19
  105.4 1.1 broadcast_select_fusion.3
  107.0 1.9 %collective-permute-start.37 = (f32[32,544]{1,0:T(8,128)S(1)}, f32[32,544]{1,0:T(8,128)S(1)}, u32[]{:S(2)}, u32[]{:S(2)}) collective-permute-start(f32[32,544]{1,0:T(8,128)S(1)} %fusion.67), channel_id=1, source_target_pairs={{0,2},{1,3},{2,0},{3,1},{4,6},{5,7},{6,4},{7,5},{8,10},{9,11},{10,... | collective-permute-start | bytes 208904 | tf_op jit(solution)/shard_map/ppermute | solution.py:19
  108.9 4.1 %collective-permute-done.33 = bf16[128,896]{1,0:T(8,128)(2,1)S(1)} collective-permute-done((bf16[128,896]{1,0:T(8,128)(2,1)S(1)}, bf16[128,896]{1,0:T(8,128)(2,1)S(1)}, u32[]{:S(2)}, u32[]{:S(2)}) %collective-permute-start.33) | collective-permute-done | bytes 229408 | tf_op jit(solution)/shard_map/ppermute | solution.py:19
  113.8 1.1 broadcast_select_fusion.1
  115.0 1.2 broadcast_select_fusion.2
  117.3 1.6 collective-permute-start.38
  119.1 3.0 %collective-permute-done.38 = f32[32,544]{1,0:T(8,128)} collective-permute-done((f32[32,544]{1,0:T(8,128)}, f32[32,544]{1,0:T(8,128)}, u32[]{:S(2)}, u32[]{:S(2)}) %collective-permute-start.38) | collective-permute-done | bytes 69664 | tf_op jit(solution)/shard_map/ppermute | solution.py:19
  124.2 3.0 %collective-permute-start.39 = (bf16[128,512]{1,0:T(8,128)(2,1)S(1)}, bf16[128,512]{1,0:T(8,128)(2,1)S(1)}, u32[]{:S(2)}, u32[]{:S(2)}) collective-permute-start(bf16[128,512]{1,0:T(8,128)(2,1)S(1)} %add_convert_fusion.2), channel_id=1, source_target_pairs={{0,16},{4,20},{8,24},{12,28},{16,0},{20,4},{24,8},{28,12},{1,17},{... | collective-permute-start | bytes 393224 | tf_op jit(solution)/shard_map/ppermute | solution.py:19
  128.7 1.3 collective-permute-done.40
  130.1 2.0 %collective-permute-start.42 = (f32[32,544]{1,0:T(8,128)S(1)}, f32[32,544]{1,0:T(8,128)S(1)}, u32[]{:S(2)}, u32[]{:S(2)}) collective-permute-start(f32[32,544]{1,0:T(8,128)S(1)} %add.159), channel_id=1, source_target_pairs={{0,16},{4,20},{8,24},{12,28},{16,0},{20,4},{24,8},{28,12},{1,17},{... | collective-permute-start | bytes 208904 | tf_op jit(solution)/shard_map/ppermute | solution.py:19
  132.6 1.7 %collective-permute-done.48 = bf16[128,512]{1,0:T(8,128)(2,1)S(1)} collective-permute-done((bf16[128,512]{1,0:T(8,128)(2,1)S(1)}, bf16[128,512]{1,0:T(8,128)(2,1)S(1)}, u32[]{:S(2)}, u32[]{:S(2)}) %collective-permute-start.48) | collective-permute-done | bytes 131104 | tf_op jit(solution)/shard_map/ppermute | solution.py:19
  134.4 1.1 collective-permute-done.42
  136.8 2.5 %collective-permute-start.44 = (bf16[1,128,512]{2,1,0:T(8,128)(2,1)S(1)}, bf16[1,128,512]{2,1,0:T(8,128)(2,1)S(1)}, u32[]{:S(2)}, u32[]{:S(2)}) collective-permute-start(bf16[1,128,512]{2,1,0:T(8,128)(2,1)S(1)} %fusion.48), channel_id=1, source_target_pairs={{0,2},{1,3},{2,0},{3,1},{4,6},{5,7},{6,4},{7,5},{8,10},{9,11},{10,... | collective-permute-start | bytes 393224 | tf_op jit(solution)/shard_map/ppermute | solution.py:19
  139.3 4.6 %factors.1 = (f32[32,256]{1,0:T(8,128)}, f32[32,32]{1,0:T(8,128)}) custom-call(f32[32,544]{1,0:T(8,128)} %add.162.sums_ref), custom_call_target="tpu_custom_call" | custom-call | flops 1000000 | bytes 20000 | tf_op jit(solution)/shard_map/factors/pallas_call | solution.py:57
  143.9 1.2 convolution_convert_fusion.8
  145.1 1.2 collective-permute-start.45
  146.4 2.5 %collective-permute-start.47 = (bf16[128,512]{1,0:T(8,128)(2,1)S(1)}, bf16[128,512]{1,0:T(8,128)(2,1)S(1)}, u32[]{:S(2)}, u32[]{:S(2)}) collective-permute-start(bf16[128,512]{1,0:T(8,128)(2,1)S(1)} %add_convert_fusion.1), channel_id=1, source_target_pairs={{0,24},{4,28},{8,16},{12,20},{16,8},{20,12},{24,0},{28,4},{1,25},{... | collective-permute-start | bytes 393224 | tf_op jit(solution)/shard_map/ppermute | solution.py:19
  151.0 1.5 fusion
  153.2 1.6 %collective-permute-done.46 = bf16[32,896]{1,0:T(8,128)(2,1)S(1)} collective-permute-done((bf16[32,896]{1,0:T(8,128)(2,1)S(1)}, bf16[32,896]{1,0:T(8,128)(2,1)S(1)}, u32[]{:S(2)}, u32[]{:S(2)}) %collective-permute-start.46) | collective-permute-done | bytes 57376 | tf_op jit(solution)/shard_map/ppermute | solution.py:19
  155.1 2.0 %collective-permute-start.51 = (bf16[32,896]{1,0:T(8,128)(2,1)S(1)}, bf16[32,896]{1,0:T(8,128)(2,1)S(1)}, u32[]{:S(2)}, u32[]{:S(2)}) collective-permute-start(bf16[32,896]{1,0:T(8,128)(2,1)S(1)} %add_convert_fusion.4), channel_id=1, source_target_pairs={{0,16},{4,20},{8,24},{12,28},{16,0},{20,4},{24,8},{28,12},{1,17},{... | collective-permute-start | bytes 172040 | tf_op jit(solution)/shard_map/ppermute | solution.py:19
  157.1 2.9 %collective-permute-done.49 = bf16[1,128,512]{2,1,0:T(8,128)(2,1)S(1)} collective-permute-done((bf16[1,128,512]{2,1,0:T(8,128)(2,1)S(1)}, bf16[1,128,512]{2,1,0:T(8,128)(2,1)S(1)}, u32[]{:S(2)}, u32[]{:S(2)}) %collective-permute-start.49) | collective-permute-done | bytes 131104 | tf_op jit(solution)/shard_map/ppermute | solution.py:19
  160.9 1.5 fusion.1
  (190 shorter events, 40.0 us)
Async XLA Ops:
  1.7 5.1 %collective-permute-start = (bf16[128,512]{1,0:T(8,128)(2,1)S(1)}, bf16[128,512]{1,0:T(8,128)(2,1)S(1)}, u32[]{:S(2)}, u32[]{:S(2)}) collective-permute-start(bf16[128,512]{1,0:T(8,128)(2,1)S(1)} %get-tuple-element.167), channel_id=1, source_target_pairs={{0,1},{1,0},{2,3},{3,2},{4,5},{5,4},{6,7},{7,6},{8,9},{9,8},{10,11... | collective-permute-start | bytes 393224 | tf_op jit(solution)/shard_map/ppermute | solution.py:19
  3.3 12.5 %collective-permute-start.6 = (bf16[224,896]{1,0:T(8,128)(2,1)S(1)}, bf16[224,896]{1,0:T(8,128)(2,1)S(1)}, u32[]{:S(2)}, u32[]{:S(2)}) collective-permute-start(bf16[224,896]{1,0:T(8,128)(2,1)S(1)} %slice.66), channel_id=1, source_target_pairs={{0,4},{4,0},{8,12},{12,8},{16,20},{20,16},{24,28},{28,24},{1,5},{5... | collective-permute-start | bytes 1204232 | tf_op jit(solution)/shard_map/ppermute | solution.py:19
  6.8 8.4 %collective-permute-start.1 = (bf16[2,128,512]{2,1,0:T(8,128)(2,1)S(1)}, bf16[2,128,512]{2,1,0:T(8,128)(2,1)S(1)}, u32[]{:S(2)}, u32[]{:S(2)}) collective-permute-start(bf16[2,128,512]{2,1,0:T(8,128)(2,1)S(1)} %pad_maximum_fusion.2), channel_id=1, source_target_pairs={{0,2},{1,3},{2,0},{3,1},{4,6},{5,7},{6,4},{7,5},{8,10},{9,11},{10,... | collective-permute-start | bytes 786440 | tf_op jit(solution)/shard_map/ppermute | solution.py:19
  15.8 13.8 %collective-permute-start.7 = (bf16[288,896]{1,0:T(8,128)(2,1)}, bf16[288,896]{1,0:T(8,128)(2,1)}, u32[]{:S(2)}, u32[]{:S(2)}) collective-permute-start(bf16[288,896]{1,0:T(8,128)(2,1)} %slice.65), channel_id=1, source_target_pairs={{0,4},{4,0},{8,12},{12,8},{16,20},{20,16},{24,28},{28,24},{1,5},{5... | collective-permute-start | bytes 1548296 | tf_op jit(solution)/shard_map/ppermute | solution.py:19
  18.3 10.1 %collective-permute-start.8 = (bf16[128,512]{1,0:T(8,128)(2,1)S(1)}, bf16[128,512]{1,0:T(8,128)(2,1)}, u32[]{:S(2)}, u32[]{:S(2)}) collective-permute-start(bf16[128,512]{1,0:T(8,128)(2,1)S(1)} %get-tuple-element.144), channel_id=1, source_target_pairs={{0,16},{4,20},{8,24},{12,28},{16,0},{20,4},{24,8},{28,12},{1,17},{... | collective-permute-start | bytes 393224 | tf_op jit(solution)/shard_map/ppermute | solution.py:19
  20.9 6.2 %collective-permute-start.9 = (bf16[128,512]{1,0:T(8,128)(2,1)S(1)}, bf16[128,512]{1,0:T(8,128)(2,1)S(1)}, u32[]{:S(2)}, u32[]{:S(2)}) collective-permute-start(bf16[128,512]{1,0:T(8,128)(2,1)S(1)} %get-tuple-element.143), channel_id=1, source_target_pairs={{0,8},{4,12},{8,0},{12,4},{16,24},{20,28},{24,16},{28,20},{1,9},{5... | collective-permute-start | bytes 393224 | tf_op jit(solution)/shard_map/ppermute | solution.py:19
  23.2 11.2 %collective-permute-start.4 = (bf16[2,128,512]{2,1,0:T(8,128)(2,1)}, bf16[2,128,512]{2,1,0:T(8,128)(2,1)}, u32[]{:S(2)}, u32[]{:S(2)}) collective-permute-start(bf16[2,128,512]{2,1,0:T(8,128)(2,1)} %pad_maximum_fusion.3), channel_id=1, source_target_pairs={{0,2},{1,3},{2,0},{3,1},{4,6},{5,7},{6,4},{7,5},{8,10},{9,11},{10,... | collective-permute-start | bytes 786440 | tf_op jit(solution)/shard_map/ppermute | solution.py:19
  26.3 8.0 %collective-permute-start.3 = (bf16[128,512]{1,0:T(8,128)(2,1)S(1)}, bf16[128,512]{1,0:T(8,128)(2,1)S(1)}, u32[]{:S(2)}, u32[]{:S(2)}) collective-permute-start(bf16[128,512]{1,0:T(8,128)(2,1)S(1)} %get-tuple-element.145), channel_id=1, source_target_pairs={{0,1},{1,0},{2,3},{3,2},{4,5},{5,4},{6,7},{7,6},{8,9},{9,8},{10,11... | collective-permute-start | bytes 393224 | tf_op jit(solution)/shard_map/ppermute | solution.py:19
  27.1 7.3 %collective-permute-start.5 = (bf16[128,512]{1,0:T(8,128)(2,1)}, bf16[128,512]{1,0:T(8,128)(2,1)S(1)}, u32[]{:S(2)}, u32[]{:S(2)}) collective-permute-start(bf16[128,512]{1,0:T(8,128)(2,1)} %get-tuple-element.142), channel_id=1, source_target_pairs={{0,24},{4,28},{8,16},{12,20},{16,8},{20,12},{24,0},{28,4},{1,25},{... | collective-permute-start | bytes 393224 | tf_op jit(solution)/shard_map/ppermute | solution.py:19
  28.5 5.9 %collective-permute-start.11 = (bf16[128,512]{1,0:T(8,128)(2,1)S(1)}, bf16[128,512]{1,0:T(8,128)(2,1)S(1)}, u32[]{:S(2)}, u32[]{:S(2)}) collective-permute-start(bf16[128,512]{1,0:T(8,128)(2,1)S(1)} %collective-permute-done.9), channel_id=1, source_target_pairs={{0,1},{1,0},{2,3},{3,2},{4,5},{5,4},{6,7},{7,6},{8,9},{9,8},{10,11... | collective-permute-start | bytes 393224 | tf_op jit(solution)/shard_map/ppermute | solution.py:19
  29.6 5.8 %collective-permute-start.10 = (bf16[128,512]{1,0:T(8,128)(2,1)}, bf16[128,512]{1,0:T(8,128)(2,1)S(1)}, u32[]{:S(2)}, u32[]{:S(2)}) collective-permute-start(bf16[128,512]{1,0:T(8,128)(2,1)} %collective-permute-done.8), channel_id=1, source_target_pairs={{0,1},{1,0},{2,3},{3,2},{4,5},{5,4},{6,7},{7,6},{8,9},{9,8},{10,11... | collective-permute-start | bytes 393224 | tf_op jit(solution)/shard_map/ppermute | solution.py:19
  34.4 8.5 %collective-permute-start.12 = (bf16[128,512]{1,0:T(8,128)(2,1)S(1)}, bf16[128,512]{1,0:T(8,128)(2,1)S(1)}, u32[]{:S(2)}, u32[]{:S(2)}) collective-permute-start(bf16[128,512]{1,0:T(8,128)(2,1)S(1)} %collective-permute-done.5), channel_id=1, source_target_pairs={{0,1},{1,0},{2,3},{3,2},{4,5},{5,4},{6,7},{7,6},{8,9},{9,8},{10,11... | collective-permute-start | bytes 393224 | tf_op jit(solution)/shard_map/ppermute | solution.py:19
  36.4 15.8 %collective-permute-start.14 = (bf16[128,512]{1,0:T(8,128)(2,1)S(1)}, bf16[128,512]{1,0:T(8,128)(2,1)S(1)}, u32[]{:S(2)}, u32[]{:S(2)}) collective-permute-start(bf16[128,512]{1,0:T(8,128)(2,1)S(1)} %get-tuple-element.141), channel_id=1, source_target_pairs={{0,24},{4,28},{8,16},{12,20},{16,8},{20,12},{24,0},{28,4},{1,25},{... | collective-permute-start | bytes 393224 | tf_op jit(solution)/shard_map/ppermute | solution.py:19
  37.7 14.6 %collective-permute-start.15 = (bf16[128,512]{1,0:T(8,128)(2,1)S(1)}, bf16[128,512]{1,0:T(8,128)(2,1)S(1)}, u32[]{:S(2)}, u32[]{:S(2)}) collective-permute-start(bf16[128,512]{1,0:T(8,128)(2,1)S(1)} %get-tuple-element.140), channel_id=1, source_target_pairs={{0,16},{4,20},{8,24},{12,28},{16,0},{20,4},{24,8},{28,12},{1,17},{... | collective-permute-start | bytes 393224 | tf_op jit(solution)/shard_map/ppermute | solution.py:19
  39.8 7.4 %collective-permute-start.16 = (bf16[128,512]{1,0:T(8,128)(2,1)S(1)}, bf16[128,512]{1,0:T(8,128)(2,1)S(1)}, u32[]{:S(2)}, u32[]{:S(2)}) collective-permute-start(bf16[128,512]{1,0:T(8,128)(2,1)S(1)} %get-tuple-element.139), channel_id=1, source_target_pairs={{0,8},{4,12},{8,0},{12,4},{16,24},{20,28},{24,16},{28,20},{1,9},{5... | collective-permute-start | bytes 393224 | tf_op jit(solution)/shard_map/ppermute | solution.py:19
  40.9 19.0 %collective-permute-start.18 = (bf16[512,512]{1,0:T(8,128)(2,1)S(1)}, bf16[512,512]{1,0:T(8,128)(2,1)S(1)}, u32[]{:S(2)}, u32[]{:S(2)}) collective-permute-start(bf16[512,512]{1,0:T(8,128)(2,1)S(1)} %copy-done.6), channel_id=1, source_target_pairs={{0,4},{4,0},{8,12},{12,8},{16,20},{20,16},{24,28},{28,24},{1,5},{5... | collective-permute-start | bytes 1572872 | tf_op jit(solution)/shard_map/ppermute | solution.py:19
  43.8 16.0 %collective-permute-start.13 = (bf16[2,128,896]{2,1,0:T(8,128)(2,1)S(1)}, bf16[2,128,896]{2,1,0:T(8,128)(2,1)S(1)}, u32[]{:S(2)}, u32[]{:S(2)}) collective-permute-start(bf16[2,128,896]{2,1,0:T(8,128)(2,1)S(1)} %bitcast.147), channel_id=1, source_target_pairs={{0,8},{4,12},{8,0},{12,4},{16,24},{20,28},{24,16},{28,20},{1,9},{5... | collective-permute-start | bytes 1376264 | tf_op jit(solution)/shard_map/ppermute | solution.py:19
  47.2 13.3 %collective-permute-start.20 = (bf16[2,128,256]{2,1,0:T(8,128)(2,1)S(1)}, bf16[2,128,256]{2,1,0:T(8,128)(2,1)S(1)}, u32[]{:S(2)}, u32[]{:S(2)}) collective-permute-start(bf16[2,128,256]{2,1,0:T(8,128)(2,1)S(1)} %maximum_select_fusion), channel_id=1, source_target_pairs={{0,1},{4,5},{8,9},{12,13},{16,17},{20,21},{24,25},{28,29}} | collective-permute-start | bytes 393224 | tf_op jit(solution)/shard_map/ppermute | solution.py:123
  52.2 8.8 %collective-permute-start.25 = (bf16[128,512]{1,0:T(8,128)(2,1)S(1)}, bf16[128,512]{1,0:T(8,128)(2,1)S(1)}, u32[]{:S(2)}, u32[]{:S(2)}) collective-permute-start(bf16[128,512]{1,0:T(8,128)(2,1)S(1)} %get-tuple-element.138), channel_id=1, source_target_pairs={{0,1},{1,0},{2,3},{3,2},{4,5},{5,4},{6,7},{7,6},{8,9},{9,8},{10,11... | collective-permute-start | bytes 393224 | tf_op jit(solution)/shard_map/ppermute | solution.py:19
  52.3 13.3 %collective-permute-start.23 = (bf16[128,512]{1,0:T(8,128)(2,1)S(1)}, bf16[128,512]{1,0:T(8,128)(2,1)S(1)}, u32[]{:S(2)}, u32[]{:S(2)}) collective-permute-start(bf16[128,512]{1,0:T(8,128)(2,1)S(1)} %collective-permute-done.15), channel_id=1, source_target_pairs={{0,1},{1,0},{2,3},{3,2},{4,5},{5,4},{6,7},{7,6},{8,9},{9,8},{10,11... | collective-permute-start | bytes 393224 | tf_op jit(solution)/shard_map/ppermute | solution.py:19
  59.8 5.9 %collective-permute-start.22 = (bf16[128,512]{1,0:T(8,128)(2,1)S(1)}, bf16[128,512]{1,0:T(8,128)(2,1)S(1)}, u32[]{:S(2)}, u32[]{:S(2)}) collective-permute-start(bf16[128,512]{1,0:T(8,128)(2,1)S(1)} %collective-permute-done.14), channel_id=1, source_target_pairs={{0,1},{1,0},{2,3},{3,2},{4,5},{5,4},{6,7},{7,6},{8,9},{9,8},{10,11... | collective-permute-start | bytes 393224 | tf_op jit(solution)/shard_map/ppermute | solution.py:19
  60.5 12.4 %collective-permute-start.17 = (bf16[1,128,896]{2,1,0:T(8,128)(2,1)S(1)}, bf16[1,128,896]{2,1,0:T(8,128)(2,1)S(1)}, u32[]{:S(2)}, u32[]{:S(2)}) collective-permute-start(bf16[1,128,896]{2,1,0:T(8,128)(2,1)S(1)} %slice.108), channel_id=1, source_target_pairs={{0,16},{4,20},{8,24},{12,28},{16,0},{20,4},{24,8},{28,12},{1,17},{... | collective-permute-start | bytes 688136 | tf_op jit(solution)/shard_map/ppermute | solution.py:19
  61.0 11.4 %collective-permute-start.19 = (bf16[384,512]{1,0:T(8,128)(2,1)S(1)}, bf16[384,512]{1,0:T(8,128)(2,1)S(1)}, u32[]{:S(2)}, u32[]{:S(2)}) collective-permute-start(bf16[384,512]{1,0:T(8,128)(2,1)S(1)} %copy-done.19), channel_id=1, source_target_pairs={{0,4},{4,0},{8,12},{12,8},{16,20},{20,16},{24,28},{28,24},{1,5},{5... | collective-permute-start | bytes 1179656 | tf_op jit(solution)/shard_map/ppermute | solution.py:19
  61.9 6.4 %collective-permute-start.21 = (bf16[2,128,256]{2,1,0:T(8,128)(2,1)S(1)}, bf16[2,128,256]{2,1,0:T(8,128)(2,1)S(1)}, u32[]{:S(2)}, u32[]{:S(2)}) collective-permute-start(bf16[2,128,256]{2,1,0:T(8,128)(2,1)S(1)} %fusion.107), channel_id=1, source_target_pairs={{0,2},{1,3},{4,6},{5,7},{8,10},{9,11},{12,14},{13,15},{16,18},{17,... | collective-permute-start | bytes 393224 | tf_op jit(solution)/shard_map/ppermute | solution.py:184
  73.4 12.5 %collective-permute-start.26 = (bf16[2,128,896]{2,1,0:T(8,128)(2,1)S(1)}, bf16[2,128,896]{2,1,0:T(8,128)(2,1)S(1)}, u32[]{:S(2)}, u32[]{:S(2)}) collective-permute-start(bf16[2,128,896]{2,1,0:T(8,128)(2,1)S(1)} %bitcast.148), channel_id=1, source_target_pairs={{0,8},{4,12},{8,0},{12,4},{16,24},{20,28},{24,16},{28,20},{1,9},{5... | collective-permute-start | bytes 1376264 | tf_op jit(solution)/shard_map/ppermute | solution.py:19
  75.0 10.9 %collective-permute-start.28 = (bf16[32,896]{1,0:T(8,128)(2,1)S(1)}, bf16[32,896]{1,0:T(8,128)(2,1)S(1)}, u32[]{:S(2)}, u32[]{:S(2)}) collective-permute-start(bf16[32,896]{1,0:T(8,128)(2,1)S(1)} %fusion.6), channel_id=1, source_target_pairs={{0,4},{4,0},{8,12},{12,8},{16,20},{20,16},{24,28},{28,24},{1,5},{5... | collective-permute-start | bytes 172040 | tf_op jit(solution)/shard_map/ppermute | solution.py:19
  85.9 5.2 %collective-permute-start.29 = (bf16[32,896]{1,0:T(8,128)(2,1)S(1)}, bf16[32,896]{1,0:T(8,128)(2,1)S(1)}, u32[]{:S(2)}, u32[]{:S(2)}) collective-permute-start(bf16[32,896]{1,0:T(8,128)(2,1)S(1)} %add_convert_fusion.7), channel_id=1, source_target_pairs={{0,8},{4,12},{8,0},{12,4},{16,24},{20,28},{24,16},{28,20},{1,9},{5... | collective-permute-start | bytes 172040 | tf_op jit(solution)/shard_map/ppermute | solution.py:19
  86.4 14.2 %collective-permute-start.27 = (bf16[1,128,896]{2,1,0:T(8,128)(2,1)S(1)}, bf16[1,128,896]{2,1,0:T(8,128)(2,1)S(1)}, u32[]{:S(2)}, u32[]{:S(2)}) collective-permute-start(bf16[1,128,896]{2,1,0:T(8,128)(2,1)S(1)} %slice.107), channel_id=1, source_target_pairs={{0,16},{4,20},{8,24},{12,28},{16,0},{20,4},{24,8},{28,12},{1,17},{... | collective-permute-start | bytes 688136 | tf_op jit(solution)/shard_map/ppermute | solution.py:19
  91.1 10.1 %collective-permute-start.31 = (bf16[32,896]{1,0:T(8,128)(2,1)S(1)}, bf16[32,896]{1,0:T(8,128)(2,1)S(1)}, u32[]{:S(2)}, u32[]{:S(2)}) collective-permute-start(bf16[32,896]{1,0:T(8,128)(2,1)S(1)} %add_convert_fusion.6), channel_id=1, source_target_pairs={{0,16},{4,20},{8,24},{12,28},{16,0},{20,4},{24,8},{28,12},{1,17},{... | collective-permute-start | bytes 172040 | tf_op jit(solution)/shard_map/ppermute | solution.py:19
  102.2 10.7 %collective-permute-start.33 = (bf16[128,896]{1,0:T(8,128)(2,1)S(1)}, bf16[128,896]{1,0:T(8,128)(2,1)S(1)}, u32[]{:S(2)}, u32[]{:S(2)}) collective-permute-start(bf16[128,896]{1,0:T(8,128)(2,1)S(1)} %fusion.7), channel_id=1, source_target_pairs={{0,16},{4,20},{8,24},{12,28},{16,0},{20,4},{24,8},{28,12},{1,17},{... | collective-permute-start | bytes 688136 | tf_op jit(solution)/shard_map/ppermute | solution.py:19
  102.3 11.1 %collective-permute-start.35 = (bf16[128,896]{1,0:T(8,128)(2,1)S(1)}, bf16[128,896]{1,0:T(8,128)(2,1)S(1)}, u32[]{:S(2)}, u32[]{:S(2)}) collective-permute-start(bf16[128,896]{1,0:T(8,128)(2,1)S(1)} %fusion.7), channel_id=1, source_target_pairs={{0,8},{4,12},{8,0},{12,4},{16,24},{20,28},{24,16},{28,20},{1,9},{5... | collective-permute-start | bytes 688136 | tf_op jit(solution)/shard_map/ppermute | solution.py:19
  106.5 2.4 %collective-permute-start.30 = (bf16[128,512]{1,0:T(8,128)(2,1)S(1)}, bf16[128,512]{1,0:T(8,128)(2,1)S(1)}, u32[]{:S(2)}, u32[]{:S(2)}) collective-permute-start(bf16[128,512]{1,0:T(8,128)(2,1)S(1)} %get-tuple-element.168), channel_id=1, source_target_pairs={{0,1},{1,0},{2,3},{3,2},{4,5},{5,4},{6,7},{7,6},{8,9},{9,8},{10,11... | collective-permute-start | bytes 393224 | tf_op jit(solution)/shard_map/ppermute | solution.py:19
  107.0 9.7 %collective-permute-start.37 = (f32[32,544]{1,0:T(8,128)S(1)}, f32[32,544]{1,0:T(8,128)S(1)}, u32[]{:S(2)}, u32[]{:S(2)}) collective-permute-start(f32[32,544]{1,0:T(8,128)S(1)} %fusion.67), channel_id=1, source_target_pairs={{0,2},{1,3},{2,0},{3,1},{4,6},{5,7},{6,4},{7,5},{8,10},{9,11},{10,... | collective-permute-start | bytes 208904 | tf_op jit(solution)/shard_map/ppermute | solution.py:19
  115.0 8.3 %collective-permute-start.36 = (bf16[128,512]{1,0:T(8,128)(2,1)}, bf16[128,512]{1,0:T(8,128)(2,1)}, u32[]{:S(2)}, u32[]{:S(2)}) collective-permute-start(bf16[128,512]{1,0:T(8,128)(2,1)} %get-tuple-element.172), channel_id=1, source_target_pairs={{0,1},{1,0},{2,3},{3,2},{4,5},{5,4},{6,7},{7,6},{8,9},{9,8},{10,11... | collective-permute-start | bytes 393224 | tf_op jit(solution)/shard_map/ppermute | solution.py:19
  116.1 7.1 %collective-permute-start.34 = (bf16[128,512]{1,0:T(8,128)(2,1)}, bf16[128,512]{1,0:T(8,128)(2,1)}, u32[]{:S(2)}, u32[]{:S(2)}) collective-permute-start(bf16[128,512]{1,0:T(8,128)(2,1)} %get-tuple-element.170), channel_id=1, source_target_pairs={{0,1},{1,0},{2,3},{3,2},{4,5},{5,4},{6,7},{7,6},{8,9},{9,8},{10,11... | collective-permute-start | bytes 393224 | tf_op jit(solution)/shard_map/ppermute | solution.py:19
  117.3 4.8 %collective-permute-start.38 = (f32[32,544]{1,0:T(8,128)}, f32[32,544]{1,0:T(8,128)}, u32[]{:S(2)}, u32[]{:S(2)}) collective-permute-start(f32[32,544]{1,0:T(8,128)} %add.156), channel_id=1, source_target_pairs={{0,4},{4,0},{8,12},{12,8},{16,20},{20,16},{24,28},{28,24},{1,5},{5... | collective-permute-start | bytes 208904 | tf_op jit(solution)/shard_map/ppermute | solution.py:19
  118.9 9.4 %collective-permute-start.41 = (bf16[128,896]{1,0:T(8,128)(2,1)S(1)}, bf16[128,896]{1,0:T(8,128)(2,1)S(1)}, u32[]{:S(2)}, u32[]{:S(2)}) collective-permute-start(bf16[128,896]{1,0:T(8,128)(2,1)S(1)} %collective-permute-done.33), channel_id=1, source_target_pairs={{0,8},{4,12},{8,0},{12,4},{16,24},{20,28},{24,16},{28,20},{1,9},{5... | collective-permute-start | bytes 688136 | tf_op jit(solution)/shard_map/ppermute | solution.py:19
  123.0 7.0 %collective-permute-start.40 = (f32[32,544]{1,0:T(8,128)S(1)}, f32[32,544]{1,0:T(8,128)S(1)}, u32[]{:S(2)}, u32[]{:S(2)}) collective-permute-start(f32[32,544]{1,0:T(8,128)S(1)} %add.158), channel_id=1, source_target_pairs={{0,8},{4,12},{8,0},{12,4},{16,24},{20,28},{24,16},{28,20},{1,9},{5... | collective-permute-start | bytes 208904 | tf_op jit(solution)/shard_map/ppermute | solution.py:19
  124.2 11.9 %collective-permute-start.39 = (bf16[128,512]{1,0:T(8,128)(2,1)S(1)}, bf16[128,512]{1,0:T(8,128)(2,1)S(1)}, u32[]{:S(2)}, u32[]{:S(2)}) collective-permute-start(bf16[128,512]{1,0:T(8,128)(2,1)S(1)} %add_convert_fusion.2), channel_id=1, source_target_pairs={{0,16},{4,20},{8,24},{12,28},{16,0},{20,4},{24,8},{28,12},{1,17},{... | collective-permute-start | bytes 393224 | tf_op jit(solution)/shard_map/ppermute | solution.py:19
  128.2 6.2 %collective-permute-start.48 = (bf16[128,512]{1,0:T(8,128)(2,1)S(1)}, bf16[128,512]{1,0:T(8,128)(2,1)S(1)}, u32[]{:S(2)}, u32[]{:S(2)}) collective-permute-start(bf16[128,512]{1,0:T(8,128)(2,1)S(1)} %add_convert_fusion), channel_id=1, source_target_pairs={{0,8},{4,12},{8,0},{12,4},{16,24},{20,28},{24,16},{28,20},{1,9},{5... | collective-permute-start | bytes 393224 | tf_op jit(solution)/shard_map/ppermute | solution.py:19
  130.1 5.4 %collective-permute-start.42 = (f32[32,544]{1,0:T(8,128)S(1)}, f32[32,544]{1,0:T(8,128)S(1)}, u32[]{:S(2)}, u32[]{:S(2)}) collective-permute-start(f32[32,544]{1,0:T(8,128)S(1)} %add.159), channel_id=1, source_target_pairs={{0,16},{4,20},{8,24},{12,28},{16,0},{20,4},{24,8},{28,12},{1,17},{... | collective-permute-start | bytes 208904 | tf_op jit(solution)/shard_map/ppermute | solution.py:19
  136.8 18.1 %collective-permute-start.44 = (bf16[1,128,512]{2,1,0:T(8,128)(2,1)S(1)}, bf16[1,128,512]{2,1,0:T(8,128)(2,1)S(1)}, u32[]{:S(2)}, u32[]{:S(2)}) collective-permute-start(bf16[1,128,512]{2,1,0:T(8,128)(2,1)S(1)} %fusion.48), channel_id=1, source_target_pairs={{0,2},{1,3},{2,0},{3,1},{4,6},{5,7},{6,4},{7,5},{8,10},{9,11},{10,... | collective-permute-start | bytes 393224 | tf_op jit(solution)/shard_map/ppermute | solution.py:19
  145.1 4.2 %collective-permute-start.45 = (bf16[32,896]{1,0:T(8,128)(2,1)S(1)}, bf16[32,896]{1,0:T(8,128)(2,1)S(1)}, u32[]{:S(2)}, u32[]{:S(2)}) collective-permute-start(bf16[32,896]{1,0:T(8,128)(2,1)S(1)} %convolution_convert_fusion.8), channel_id=1, source_target_pairs={{0,4},{4,0},{8,12},{12,8},{16,20},{20,16},{24,28},{28,24},{1,5},{5... | collective-permute-start | bytes 172040 | tf_op jit(solution)/shard_map/ppermute | solution.py:19
  146.4 6.8 %collective-permute-start.47 = (bf16[128,512]{1,0:T(8,128)(2,1)S(1)}, bf16[128,512]{1,0:T(8,128)(2,1)S(1)}, u32[]{:S(2)}, u32[]{:S(2)}) collective-permute-start(bf16[128,512]{1,0:T(8,128)(2,1)S(1)} %add_convert_fusion.1), channel_id=1, source_target_pairs={{0,24},{4,28},{8,16},{12,20},{16,8},{20,12},{24,0},{28,4},{1,25},{... | collective-permute-start | bytes 393224 | tf_op jit(solution)/shard_map/ppermute | solution.py:19
  150.6 4.3 %collective-permute-start.46 = (bf16[32,896]{1,0:T(8,128)(2,1)S(1)}, bf16[32,896]{1,0:T(8,128)(2,1)S(1)}, u32[]{:S(2)}, u32[]{:S(2)}) collective-permute-start(bf16[32,896]{1,0:T(8,128)(2,1)S(1)} %add_convert_fusion.5), channel_id=1, source_target_pairs={{0,8},{4,12},{8,0},{12,4},{16,24},{20,28},{24,16},{28,20},{1,9},{5... | collective-permute-start | bytes 172040 | tf_op jit(solution)/shard_map/ppermute | solution.py:19
  154.9 5.0 %collective-permute-start.49 = (bf16[1,128,512]{2,1,0:T(8,128)(2,1)S(1)}, bf16[1,128,512]{2,1,0:T(8,128)(2,1)S(1)}, u32[]{:S(2)}, u32[]{:S(2)}) collective-permute-start(bf16[1,128,512]{2,1,0:T(8,128)(2,1)S(1)} %fusion.45), channel_id=1, source_target_pairs={{0,2},{1,3},{2,0},{3,1},{4,6},{5,7},{6,4},{7,5},{8,10},{9,11},{10,... | collective-permute-start | bytes 393224 | tf_op jit(solution)/shard_map/ppermute | solution.py:19
  155.1 5.2 %collective-permute-start.51 = (bf16[32,896]{1,0:T(8,128)(2,1)S(1)}, bf16[32,896]{1,0:T(8,128)(2,1)S(1)}, u32[]{:S(2)}, u32[]{:S(2)}) collective-permute-start(bf16[32,896]{1,0:T(8,128)(2,1)S(1)} %add_convert_fusion.4), channel_id=1, source_target_pairs={{0,16},{4,20},{8,24},{12,28},{16,0},{20,4},{24,8},{28,12},{1,17},{... | collective-permute-start | bytes 172040 | tf_op jit(solution)/shard_map/ppermute | solution.py:19
  160.1 2.3 %collective-permute-start.50 = (bf16[128,512]{1,0:T(8,128)(2,1)S(1)}, bf16[128,512]{1,0:T(8,128)(2,1)S(1)}, u32[]{:S(2)}, u32[]{:S(2)}) collective-permute-start(bf16[128,512]{1,0:T(8,128)(2,1)S(1)} %get-tuple-element.135), channel_id=1, source_target_pairs={{0,1},{1,0},{2,3},{3,2},{4,5},{5,4},{6,7},{7,6},{8,9},{9,8},{10,11... | collective-permute-start | bytes 393224 | tf_op jit(solution)/shard_map/ppermute | solution.py:19
  (31 other events, 219.5 us)

commit v6 on v5

--- a/solution.py
+++ b/solution.py
@@ -108,26 +108,22 @@
         return kept
 
     ucut = (up_weight.shape[0] * 7 // 16 + 31) // 32 * 32
-    dcut = (down_weight.shape[0] // 2 + 127) // 128 * 128
+    dcut = (down_weight.shape[0] * 2 // 3 + 127) // 128 * 128
     up_a = flip(up_weight[:ucut], "dp", 1)
     mine, swap = split_half(tokens, half)
     tok_blocks = [mine, wait(flip(swap, "tensor", 1))]
     got = flip(jnp.stack(tok_blocks), "tensor", tbits[1])
-    grad_in, tok_win, grad_win, wait.last = tie(
-        out_grad, tokens[:, :window], out_grad[:, :window], wait.last
-    )
+    grad_in, wait.last = tie(out_grad, wait.last)
     mine, swap = split_half(grad_in, half)
     swap = flip(swap, "tensor", 1)
-    windows = jnp.stack([tok_win, grad_win])
-    windows = jnp.where(t_i == 0, windows, jnp.zeros_like(windows))
-    win_got = lax.ppermute(windows, "tensor", [(0, 1)])
     grad_blocks = [mine, wait(swap)]
     for mask in tbits[1:]:
         if mask > tbits[1]:
             got = flip(jnp.stack(tok_blocks), "tensor", mask)
         got = wait(got)
         tok_blocks = tok_blocks + [got[n] for n in range(len(tok_blocks))]
-    tok_keep = send_z(jnp.stack(tok_blocks))
+    tok_blocks = jnp.stack(tok_blocks)
+    tok_keep = send_z(tok_blocks)
     up_a = wait(up_a)
     up_b_in, up_a = tie(up_weight[ucut:], up_a)
     up_b = flip(up_b_in, "dp", 1)
@@ -142,7 +138,8 @@
             grad_got = flip(jnp.stack(grad_blocks), "tensor", mask)
         grad_got = wait(grad_got)
         grad_blocks = grad_blocks + [grad_got[n] for n in range(len(grad_blocks))]
-    grad_keep = send_z(jnp.stack(grad_blocks))
+    grad_blocks = jnp.stack(grad_blocks)
+    grad_keep = send_z(grad_blocks)
     tok_other = [wait(flip(piece, "tensor", 1)) for piece in tok_keep]
     up_other = jnp.concatenate([up_a, up_b])
 
@@ -179,13 +176,23 @@
     down_a = wait(down_a)
     down_b_in, down_a = tie(down_weight[dcut:], down_a)
     down_b = flip(down_b_in, "dp", 1)
-    windows = windows + wait(win_got)
-    for n, mask in enumerate(tbits[1:]):
-        win_got = lax.ppermute(windows, "tensor", [(i, i + mask) for i in range(mask)])
-        if n == 0:
-            grad_other = other_halves(grad_keep)
-        windows = windows + wait(win_got)
+    if 2 * window <= tokens.shape[1]:
+        windows = jnp.stack(
+            [
+                lax.dynamic_index_in_dim(blocks, t_i, 0, keepdims=False)[:, :window]
+                for blocks in (tok_blocks, grad_blocks)
+            ]
+        )
+        windows = jnp.where(half == 0, windows, wait(flip(windows, "tensor", 1)))
+    else:
+        windows = jnp.stack([tokens[:, :window], out_grad[:, :window]])
+        windows = jnp.where(t_i == 0, windows, jnp.zeros_like(windows))
+        for mask in tbits:
+            windows = windows + wait(
+                lax.ppermute(windows, "tensor", [(i, i + mask) for i in range(mask)])
+            )
     tok_win, grad_win = windows[0], windows[1]
+    grad_other = other_halves(grad_keep)
     down_b = wait(down_b)
     down_other = jnp.concatenate([down_a, down_b])
     part_of = partial(grad_keep, grad_other, down_weight, down_other, ((1,), (1,)))

time: 164 us -> 163 us (level)
  waiting for transfers between devices: 68.1 us -> 79.3 us
  starting transfers between devices: 52.9 us -> 45.9 us
  other arithmetic: 10.5 us -> 7.88 us
  local copies, waits for them, and re-layouts: 8.81 us -> 6.4 us
    ppermute x50 -> x51, waiting for transfers between devices: 66.5 us -> 79.3 us  [flip(): return lax.ppermute(arr, axis, [(i, i ^ mask) for i in range(size)])]
    ppermute x2 -> x0, starting transfers between devices: 5.51 us -> none  [the longest x1 3.68 us: shards(): lax.ppermute(windows, 'tensor', [(i, i + mask) for i in range(mask)])]
    ppermute x2 -> x0, waiting for transfers between devices: 1.64 us -> none  [the longest x1 1.64 us: shards(): lax.ppermute(windows, 'tensor', [(i, i + mask) for i in range(mask)])]
    ppermute x50 -> x51, starting transfers between devices: 47.4 us -> 45.9 us  [flip(): return lax.ppermute(arr, axis, [(i, i ^ mask) for i in range(size)])]
  transfers between devices with their start and end apart: 52 -> 51, of which waited for: 25 -> 25; matrix products, arithmetic and copies ran while one was open for 19% -> 16% of each run, Pallas kernels for 3% -> 3%
where the time goes in v6:
time: 163 us; the launch traced here: 162 us
  waiting for transfers between devices  79.3 us (49%)
  starting transfers between devices  45.9 us (28%)
  matrix products  16.8 us (10%)
  other arithmetic  7.88 us (5%)
  local copies, waits for them, and re-layouts  6.4 us (4%)
  Pallas kernels  4.74 us (3%)
    ppermute x51, waiting for transfers between devices, flip(): return lax.ppermute(arr, axis, [(i, i ^ mask) for i in range(size)])  79.3 us
    ppermute x51, starting transfers between devices, flip(): return lax.ppermute(arr, axis, [(i, i ^ mask) for i in range(size)])  45.9 us
    dot_general x27, matrix products, dot(): lax.dot_general(a, b, (dims, ((), ())), preferred_element_type=F32, preci...  16.8 us
    pallas_call x1, Pallas kernels, factors(): pl.pallas_call(functools.partial(factor_kernel, replicas), out_shape=(jax...  4.74 us
  transfers between devices with their start and end apart: 51, of which 25 were waited for; matrix products, arithmetic and copies ran while one was open for 16% of the time, Pallas kernels for 3%

profile of v6, /device:TPU:0, one launch (start us, length us, event | category | flops | bytes accessed | tf_op | source)
XLA Modules:
  0.0 162.5 jit_solution(8314496803824951451)
XLA Ops:
  0.7 1.0 select_bitcast_fusion.1
  2.2 1.0 slice.64
  3.3 2.6 %collective-permute-start.6 = (bf16[224,896]{1,0:T(8,128)(2,1)S(1)}, bf16[224,896]{1,0:T(8,128)(2,1)S(1)}, u32[]{:S(2)}, u32[]{:S(2)}) collective-permute-start(bf16[224,896]{1,0:T(8,128)(2,1)S(1)} %slice.64), channel_id=1, source_target_pairs={{0,4},{4,0},{8,12},{12,8},{16,20},{20,16},{24,28},{28,24},{1,5},{5... | collective-permute-start | bytes 1204232 | tf_op jit(solution)/shard_map/ppermute | solution.py:19
  5.9 1.6 collective-permute-start.1
  9.0 5.4 %collective-permute-done.1 = bf16[2,128,512]{2,1,0:T(8,128)(2,1)S(1)} collective-permute-done((bf16[2,128,512]{2,1,0:T(8,128)(2,1)S(1)}, bf16[2,128,512]{2,1,0:T(8,128)(2,1)S(1)}, u32[]{:S(2)}, u32[]{:S(2)}) %collective-permute-start.1) | collective-permute-done | bytes 262176 | tf_op jit(solution)/shard_map/ppermute | solution.py:19
  14.4 1.4 collective-permute-done.6
  16.5 1.8 %collective-permute-start.7 = (bf16[288,896]{1,0:T(8,128)(2,1)}, bf16[288,896]{1,0:T(8,128)(2,1)}, u32[]{:S(2)}, u32[]{:S(2)}) collective-permute-start(bf16[288,896]{1,0:T(8,128)(2,1)} %slice.63), channel_id=1, source_target_pairs={{0,4},{4,0},{8,12},{12,8},{16,20},{20,16},{24,28},{28,24},{1,5},{5... | collective-permute-start | bytes 1548296 | tf_op jit(solution)/shard_map/ppermute | solution.py:19
  19.1 1.6 collective-permute-start.9
  20.7 2.6 %collective-permute-start.8 = (bf16[128,512]{1,0:T(8,128)(2,1)S(1)}, bf16[128,512]{1,0:T(8,128)(2,1)S(1)}, u32[]{:S(2)}, u32[]{:S(2)}) collective-permute-start(bf16[128,512]{1,0:T(8,128)(2,1)S(1)} %get-tuple-element.134), channel_id=1, source_target_pairs={{0,16},{4,20},{8,24},{12,28},{16,0},{20,4},{24,8},{28,12},{1,17},{... | collective-permute-start | bytes 393224 | tf_op jit(solution)/shard_map/ppermute | solution.py:19
  23.4 1.6 collective-permute-start.4
  25.7 3.4 %collective-permute-start.5 = (bf16[128,512]{1,0:T(8,128)(2,1)}, bf16[128,512]{1,0:T(8,128)(2,1)S(1)}, u32[]{:S(2)}, u32[]{:S(2)}) collective-permute-start(bf16[128,512]{1,0:T(8,128)(2,1)} %get-tuple-element.135), channel_id=1, source_target_pairs={{0,24},{4,28},{8,16},{12,20},{16,8},{20,12},{24,0},{28,4},{1,25},{... | collective-permute-start | bytes 393224 | tf_op jit(solution)/shard_map/ppermute | solution.py:19
  29.1 1.2 collective-permute-done.7
  30.4 2.6 %collective-permute-done.5 = bf16[128,512]{1,0:T(8,128)(2,1)S(1)} collective-permute-done((bf16[128,512]{1,0:T(8,128)(2,1)}, bf16[128,512]{1,0:T(8,128)(2,1)S(1)}, u32[]{:S(2)}, u32[]{:S(2)}) %collective-permute-start.5) | collective-permute-done | bytes 131104 | tf_op jit(solution)/shard_map/ppermute | solution.py:19
  33.2 3.3 %collective-permute-start.14 = (bf16[128,512]{1,0:T(8,128)(2,1)S(1)}, bf16[128,512]{1,0:T(8,128)(2,1)S(1)}, u32[]{:S(2)}, u32[]{:S(2)}) collective-permute-start(bf16[128,512]{1,0:T(8,128)(2,1)S(1)} %get-tuple-element.141), channel_id=1, source_target_pairs={{0,24},{4,28},{8,16},{12,20},{16,8},{20,12},{24,0},{28,4},{1,25},{... | collective-permute-start | bytes 393224 | tf_op jit(solution)/shard_map/ppermute | solution.py:19
  38.7 1.1 constant_dynamic-update-slice_fusion
  40.7 1.3 collective-permute-start.13
  42.5 3.5 %collective-permute-done.16 = bf16[128,512]{1,0:T(8,128)(2,1)S(1)} collective-permute-done((bf16[128,512]{1,0:T(8,128)(2,1)S(1)}, bf16[128,512]{1,0:T(8,128)(2,1)S(1)}, u32[]{:S(2)}, u32[]{:S(2)}) %collective-permute-start.16) | collective-permute-done | bytes 131104 | tf_op jit(solution)/shard_map/ppermute | solution.py:19
  46.0 3.2 %collective-permute-done.15 = bf16[128,512]{1,0:T(8,128)(2,1)S(1)} collective-permute-done((bf16[128,512]{1,0:T(8,128)(2,1)S(1)}, bf16[128,512]{1,0:T(8,128)(2,1)S(1)}, u32[]{:S(2)}, u32[]{:S(2)}) %collective-permute-start.15) | collective-permute-done | bytes 131104 | tf_op jit(solution)/shard_map/ppermute | solution.py:19
  49.8 6.8 %collective-permute-done.13 = bf16[2,128,896]{2,1,0:T(8,128)(2,1)S(1)} collective-permute-done((bf16[2,128,896]{2,1,0:T(8,128)(2,1)S(1)}, bf16[2,128,896]{2,1,0:T(8,128)(2,1)S(1)}, u32[]{:S(2)}, u32[]{:S(2)}) %collective-permute-start.13) | collective-permute-done | bytes 458784 | tf_op jit(solution)/shard_map/ppermute | solution.py:19
  57.2 1.3 collective-permute-start.17
  60.2 6.4 %collective-permute-done.19 = bf16[256,512]{1,0:T(8,128)(2,1)S(1)} collective-permute-done((bf16[256,512]{1,0:T(8,128)(2,1)S(1)}, bf16[256,512]{1,0:T(8,128)(2,1)S(1)}, u32[]{:S(2)}, u32[]{:S(2)}) %collective-permute-start.19) | collective-permute-done | bytes 262176 | tf_op jit(solution)/shard_map/ppermute | solution.py:19
  66.6 4.1 %collective-permute-done.17 = bf16[1,128,896]{2,1,0:T(8,128)(2,1)S(1)} collective-permute-done((bf16[1,128,896]{2,1,0:T(8,128)(2,1)S(1)}, bf16[1,128,896]{2,1,0:T(8,128)(2,1)S(1)}, u32[]{:S(2)}, u32[]{:S(2)}) %collective-permute-start.17) | collective-permute-done | bytes 229408 | tf_op jit(solution)/shard_map/ppermute | solution.py:19
  74.0 8.9 %collective-permute-done.25 = bf16[2,128,896]{2,1,0:T(8,128)(2,1)S(1)} collective-permute-done((bf16[2,128,896]{2,1,0:T(8,128)(2,1)S(1)}, bf16[2,128,896]{2,1,0:T(8,128)(2,1)S(1)}, u32[]{:S(2)}, u32[]{:S(2)}) %collective-permute-start.25) | collective-permute-done | bytes 458784 | tf_op jit(solution)/shard_map/ppermute | solution.py:19
  83.4 3.3 %collective-permute-start.26 = (bf16[1,128,896]{2,1,0:T(8,128)(2,1)S(1)}, bf16[1,128,896]{2,1,0:T(8,128)(2,1)S(1)}, u32[]{:S(2)}, u32[]{:S(2)}) collective-permute-start(bf16[1,128,896]{2,1,0:T(8,128)(2,1)S(1)} %slice.111), channel_id=1, source_target_pairs={{0,16},{4,20},{8,24},{12,28},{16,0},{20,4},{24,8},{28,12},{1,17},{... | collective-permute-start | bytes 688136 | tf_op jit(solution)/shard_map/ppermute | solution.py:19
  87.7 2.1 %collective-permute-start.30 = (bf16[32,896]{1,0:T(8,128)(2,1)S(1)}, bf16[32,896]{1,0:T(8,128)(2,1)S(1)}, u32[]{:S(2)}, u32[]{:S(2)}) collective-permute-start(bf16[32,896]{1,0:T(8,128)(2,1)S(1)} %add_convert_fusion.6), channel_id=1, source_target_pairs={{0,16},{4,20},{8,24},{12,28},{16,0},{20,4},{24,8},{28,12},{1,17},{... | collective-permute-start | bytes 172040 | tf_op jit(solution)/shard_map/ppermute | solution.py:19
  89.7 8.4 %collective-permute-done.26 = bf16[1,128,896]{2,1,0:T(8,128)(2,1)S(1)} collective-permute-done((bf16[1,128,896]{2,1,0:T(8,128)(2,1)S(1)}, bf16[1,128,896]{2,1,0:T(8,128)(2,1)S(1)}, u32[]{:S(2)}, u32[]{:S(2)}) %collective-permute-start.26) | collective-permute-done | bytes 229408 | tf_op jit(solution)/shard_map/ppermute | solution.py:19
  99.8 3.2 %collective-permute-start.34 = (bf16[128,896]{1,0:T(8,128)(2,1)S(1)}, bf16[128,896]{1,0:T(8,128)(2,1)S(1)}, u32[]{:S(2)}, u32[]{:S(2)}) collective-permute-start(bf16[128,896]{1,0:T(8,128)(2,1)S(1)} %fusion.7), channel_id=1, source_target_pairs={{0,8},{4,12},{8,0},{12,4},{16,24},{20,28},{24,16},{28,20},{1,9},{5... | collective-permute-start | bytes 688136 | tf_op jit(solution)/shard_map/ppermute | solution.py:19
  104.0 1.1 broadcast_select_fusion.4
  105.6 1.6 collective-permute-start.36
  107.2 5.2 %collective-permute-done.32 = bf16[128,896]{1,0:T(8,128)(2,1)S(1)} collective-permute-done((bf16[128,896]{1,0:T(8,128)(2,1)S(1)}, bf16[128,896]{1,0:T(8,128)(2,1)S(1)}, u32[]{:S(2)}, u32[]{:S(2)}) %collective-permute-start.32) | collective-permute-done | bytes 229408 | tf_op jit(solution)/shard_map/ppermute | solution.py:19
  113.3 1.1 broadcast_select_fusion.2
  114.4 1.1 broadcast_select_fusion.3
  117.2 4.2 %collective-permute-done.37 = f32[32,544]{1,0:T(8,128)} collective-permute-done((f32[32,544]{1,0:T(8,128)}, f32[32,544]{1,0:T(8,128)}, u32[]{:S(2)}, u32[]{:S(2)}) %collective-permute-start.37) | collective-permute-done | bytes 69664 | tf_op jit(solution)/shard_map/ppermute | solution.py:19
  123.5 2.0 %collective-permute-start.38 = (bf16[128,512]{1,0:T(8,128)(2,1)S(1)}, bf16[128,512]{1,0:T(8,128)(2,1)S(1)}, u32[]{:S(2)}, u32[]{:S(2)}) collective-permute-start(bf16[128,512]{1,0:T(8,128)(2,1)S(1)} %add_convert_fusion.2), channel_id=1, source_target_pairs={{0,16},{4,20},{8,24},{12,28},{16,0},{20,4},{24,8},{28,12},{1,17},{... | collective-permute-start | bytes 393224 | tf_op jit(solution)/shard_map/ppermute | solution.py:19
  127.1 1.6 collective-permute-done.39
  128.7 1.4 collective-permute-start.41
  130.7 1.5 collective-permute-done.47
  132.2 2.9 %collective-permute-done.41 = f32[32,544]{1,0:T(8,128)S(1)} collective-permute-done((f32[32,544]{1,0:T(8,128)S(1)}, f32[32,544]{1,0:T(8,128)S(1)}, u32[]{:S(2)}, u32[]{:S(2)}) %collective-permute-start.41) | collective-permute-done | bytes 69664 | tf_op jit(solution)/shard_map/ppermute | solution.py:19
  136.4 1.5 collective-permute-start.43
  137.9 4.7 %factors.1 = (f32[32,256]{1,0:T(8,128)}, f32[32,32]{1,0:T(8,128)}) custom-call(f32[32,544]{1,0:T(8,128)} %add.159.sums_ref), custom_call_target="tpu_custom_call" | custom-call | flops 1000000 | bytes 20000 | tf_op jit(solution)/shard_map/factors/pallas_call | solution.py:57
  142.6 1.2 convolution_convert_fusion.8
  143.8 1.5 collective-permute-start.44
  145.5 2.5 %collective-permute-done.44 = bf16[32,896]{1,0:T(8,128)(2,1)S(1)} collective-permute-done((bf16[32,896]{1,0:T(8,128)(2,1)S(1)}, bf16[32,896]{1,0:T(8,128)(2,1)S(1)}, u32[]{:S(2)}, u32[]{:S(2)}) %collective-permute-start.44) | collective-permute-done | bytes 57376 | tf_op jit(solution)/shard_map/ppermute | solution.py:19
  149.5 1.5 fusion
  151.0 1.3 collective-permute-done.46
  152.3 1.3 collective-permute-done.45
  154.8 3.9 %collective-permute-done.48 = bf16[1,128,512]{2,1,0:T(8,128)(2,1)S(1)} collective-permute-done((bf16[1,128,512]{2,1,0:T(8,128)(2,1)S(1)}, bf16[1,128,512]{2,1,0:T(8,128)(2,1)S(1)}, u32[]{:S(2)}, u32[]{:S(2)}) %collective-permute-start.48) | collective-permute-done | bytes 131104 | tf_op jit(solution)/shard_map/ppermute | solution.py:19
  160.2 1.5 fusion.1
  (186 shorter events, 31.6 us)
Async XLA Ops:
  1.7 4.2 %collective-permute-start = (bf16[128,512]{1,0:T(8,128)(2,1)S(1)}, bf16[128,512]{1,0:T(8,128)(2,1)S(1)}, u32[]{:S(2)}, u32[]{:S(2)}) collective-permute-start(bf16[128,512]{1,0:T(8,128)(2,1)S(1)} %get-tuple-element.163), channel_id=1, source_target_pairs={{0,1},{1,0},{2,3},{3,2},{4,5},{5,4},{6,7},{7,6},{8,9},{9,8},{10,11... | collective-permute-start | bytes 393224 | tf_op jit(solution)/shard_map/ppermute | solution.py:19
  3.3 12.5 %collective-permute-start.6 = (bf16[224,896]{1,0:T(8,128)(2,1)S(1)}, bf16[224,896]{1,0:T(8,128)(2,1)S(1)}, u32[]{:S(2)}, u32[]{:S(2)}) collective-permute-start(bf16[224,896]{1,0:T(8,128)(2,1)S(1)} %slice.64), channel_id=1, source_target_pairs={{0,4},{4,0},{8,12},{12,8},{16,20},{20,16},{24,28},{28,24},{1,5},{5... | collective-permute-start | bytes 1204232 | tf_op jit(solution)/shard_map/ppermute | solution.py:19
  5.9 8.4 %collective-permute-start.1 = (bf16[2,128,512]{2,1,0:T(8,128)(2,1)S(1)}, bf16[2,128,512]{2,1,0:T(8,128)(2,1)S(1)}, u32[]{:S(2)}, u32[]{:S(2)}) collective-permute-start(bf16[2,128,512]{2,1,0:T(8,128)(2,1)S(1)} %pad_maximum_fusion.2), channel_id=1, source_target_pairs={{0,2},{1,3},{2,0},{3,1},{4,6},{5,7},{6,4},{7,5},{8,10},{9,11},{10,... | collective-permute-start | bytes 786440 | tf_op jit(solution)/shard_map/ppermute | solution.py:19
  16.5 13.8 %collective-permute-start.7 = (bf16[288,896]{1,0:T(8,128)(2,1)}, bf16[288,896]{1,0:T(8,128)(2,1)}, u32[]{:S(2)}, u32[]{:S(2)}) collective-permute-start(bf16[288,896]{1,0:T(8,128)(2,1)} %slice.63), channel_id=1, source_target_pairs={{0,4},{4,0},{8,12},{12,8},{16,20},{20,16},{24,28},{28,24},{1,5},{5... | collective-permute-start | bytes 1548296 | tf_op jit(solution)/shard_map/ppermute | solution.py:19
  19.1 6.7 %collective-permute-start.9 = (bf16[128,512]{1,0:T(8,128)(2,1)S(1)}, bf16[128,512]{1,0:T(8,128)(2,1)S(1)}, u32[]{:S(2)}, u32[]{:S(2)}) collective-permute-start(bf16[128,512]{1,0:T(8,128)(2,1)S(1)} %get-tuple-element.133), channel_id=1, source_target_pairs={{0,8},{4,12},{8,0},{12,4},{16,24},{20,28},{24,16},{28,20},{1,9},{5... | collective-permute-start | bytes 393224 | tf_op jit(solution)/shard_map/ppermute | solution.py:19
  20.7 8.5 %collective-permute-start.8 = (bf16[128,512]{1,0:T(8,128)(2,1)S(1)}, bf16[128,512]{1,0:T(8,128)(2,1)S(1)}, u32[]{:S(2)}, u32[]{:S(2)}) collective-permute-start(bf16[128,512]{1,0:T(8,128)(2,1)S(1)} %get-tuple-element.134), channel_id=1, source_target_pairs={{0,16},{4,20},{8,24},{12,28},{16,0},{20,4},{24,8},{28,12},{1,17},{... | collective-permute-start | bytes 393224 | tf_op jit(solution)/shard_map/ppermute | solution.py:19
  23.4 9.6 %collective-permute-start.4 = (bf16[2,128,512]{2,1,0:T(8,128)(2,1)S(1)}, bf16[2,128,512]{2,1,0:T(8,128)(2,1)S(1)}, u32[]{:S(2)}, u32[]{:S(2)}) collective-permute-start(bf16[2,128,512]{2,1,0:T(8,128)(2,1)S(1)} %pad_maximum_fusion.3), channel_id=1, source_target_pairs={{0,2},{1,3},{2,0},{3,1},{4,6},{5,7},{6,4},{7,5},{8,10},{9,11},{10,... | collective-permute-start | bytes 786440 | tf_op jit(solution)/shard_map/ppermute | solution.py:19
  25.0 8.0 %collective-permute-start.3 = (bf16[128,512]{1,0:T(8,128)(2,1)S(1)}, bf16[128,512]{1,0:T(8,128)(2,1)S(1)}, u32[]{:S(2)}, u32[]{:S(2)}) collective-permute-start(bf16[128,512]{1,0:T(8,128)(2,1)S(1)} %get-tuple-element.136), channel_id=1, source_target_pairs={{0,1},{1,0},{2,3},{3,2},{4,5},{5,4},{6,7},{7,6},{8,9},{9,8},{10,11... | collective-permute-start | bytes 393224 | tf_op jit(solution)/shard_map/ppermute | solution.py:19
  25.7 7.3 %collective-permute-start.5 = (bf16[128,512]{1,0:T(8,128)(2,1)}, bf16[128,512]{1,0:T(8,128)(2,1)S(1)}, u32[]{:S(2)}, u32[]{:S(2)}) collective-permute-start(bf16[128,512]{1,0:T(8,128)(2,1)} %get-tuple-element.135), channel_id=1, source_target_pairs={{0,24},{4,28},{8,16},{12,20},{16,8},{20,12},{24,0},{28,4},{1,25},{... | collective-permute-start | bytes 393224 | tf_op jit(solution)/shard_map/ppermute | solution.py:19
  29.1 3.9 %collective-permute-start.11 = (bf16[128,512]{1,0:T(8,128)(2,1)S(1)}, bf16[128,512]{1,0:T(8,128)(2,1)S(1)}, u32[]{:S(2)}, u32[]{:S(2)}) collective-permute-start(bf16[128,512]{1,0:T(8,128)(2,1)S(1)} %collective-permute-done.9), channel_id=1, source_target_pairs={{0,1},{1,0},{2,3},{3,2},{4,5},{5,4},{6,7},{7,6},{8,9},{9,8},{10,11... | collective-permute-start | bytes 393224 | tf_op jit(solution)/shard_map/ppermute | solution.py:19
  30.3 2.7 %collective-permute-start.10 = (bf16[128,512]{1,0:T(8,128)(2,1)S(1)}, bf16[128,512]{1,0:T(8,128)(2,1)S(1)}, u32[]{:S(2)}, u32[]{:S(2)}) collective-permute-start(bf16[128,512]{1,0:T(8,128)(2,1)S(1)} %collective-permute-done.8), channel_id=1, source_target_pairs={{0,1},{1,0},{2,3},{3,2},{4,5},{5,4},{6,7},{7,6},{8,9},{9,8},{10,11... | collective-permute-start | bytes 393224 | tf_op jit(solution)/shard_map/ppermute | solution.py:19
  33.0 6.8 %collective-permute-start.12 = (bf16[128,512]{1,0:T(8,128)(2,1)S(1)}, bf16[128,512]{1,0:T(8,128)(2,1)S(1)}, u32[]{:S(2)}, u32[]{:S(2)}) collective-permute-start(bf16[128,512]{1,0:T(8,128)(2,1)S(1)} %collective-permute-done.5), channel_id=1, source_target_pairs={{0,1},{1,0},{2,3},{3,2},{4,5},{5,4},{6,7},{7,6},{8,9},{9,8},{10,11... | collective-permute-start | bytes 393224 | tf_op jit(solution)/shard_map/ppermute | solution.py:19
  33.2 16.0 %collective-permute-start.14 = (bf16[128,512]{1,0:T(8,128)(2,1)S(1)}, bf16[128,512]{1,0:T(8,128)(2,1)S(1)}, u32[]{:S(2)}, u32[]{:S(2)}) collective-permute-start(bf16[128,512]{1,0:T(8,128)(2,1)S(1)} %get-tuple-element.141), channel_id=1, source_target_pairs={{0,24},{4,28},{8,16},{12,20},{16,8},{20,12},{24,0},{28,4},{1,25},{... | collective-permute-start | bytes 393224 | tf_op jit(solution)/shard_map/ppermute | solution.py:19
  36.5 12.8 %collective-permute-start.15 = (bf16[128,512]{1,0:T(8,128)(2,1)S(1)}, bf16[128,512]{1,0:T(8,128)(2,1)S(1)}, u32[]{:S(2)}, u32[]{:S(2)}) collective-permute-start(bf16[128,512]{1,0:T(8,128)(2,1)S(1)} %get-tuple-element.140), channel_id=1, source_target_pairs={{0,16},{4,20},{8,24},{12,28},{16,0},{20,4},{24,8},{28,12},{1,17},{... | collective-permute-start | bytes 393224 | tf_op jit(solution)/shard_map/ppermute | solution.py:19
  36.9 9.2 %collective-permute-start.16 = (bf16[128,512]{1,0:T(8,128)(2,1)S(1)}, bf16[128,512]{1,0:T(8,128)(2,1)S(1)}, u32[]{:S(2)}, u32[]{:S(2)}) collective-permute-start(bf16[128,512]{1,0:T(8,128)(2,1)S(1)} %get-tuple-element.139), channel_id=1, source_target_pairs={{0,8},{4,12},{8,0},{12,4},{16,24},{20,28},{24,16},{28,20},{1,9},{5... | collective-permute-start | bytes 393224 | tf_op jit(solution)/shard_map/ppermute | solution.py:19
  37.7 19.0 %collective-permute-start.18 = (bf16[640,512]{1,0:T(8,128)(2,1)S(1)}, bf16[640,512]{1,0:T(8,128)(2,1)S(1)}, u32[]{:S(2)}, u32[]{:S(2)}) collective-permute-start(bf16[640,512]{1,0:T(8,128)(2,1)S(1)} %slice.65), channel_id=1, source_target_pairs={{0,4},{4,0},{8,12},{12,8},{16,20},{20,16},{24,28},{28,24},{1,5},{5... | collective-permute-start | bytes 1966088 | tf_op jit(solution)/shard_map/ppermute | solution.py:19
  40.7 15.8 %collective-permute-start.13 = (bf16[2,128,896]{2,1,0:T(8,128)(2,1)S(1)}, bf16[2,128,896]{2,1,0:T(8,128)(2,1)S(1)}, u32[]{:S(2)}, u32[]{:S(2)}) collective-permute-start(bf16[2,128,896]{2,1,0:T(8,128)(2,1)S(1)} %bitcast.147), channel_id=1, source_target_pairs={{0,8},{4,12},{8,0},{12,4},{16,24},{20,28},{24,16},{28,20},{1,9},{5... | collective-permute-start | bytes 1376264 | tf_op jit(solution)/shard_map/ppermute | solution.py:19
  46.0 12.5 %collective-permute-start.23 = (bf16[128,512]{1,0:T(8,128)(2,1)S(1)}, bf16[128,512]{1,0:T(8,128)(2,1)S(1)}, u32[]{:S(2)}, u32[]{:S(2)}) collective-permute-start(bf16[128,512]{1,0:T(8,128)(2,1)S(1)} %get-tuple-element.138), channel_id=1, source_target_pairs={{0,1},{1,0},{2,3},{3,2},{4,5},{5,4},{6,7},{7,6},{8,9},{9,8},{10,11... | collective-permute-start | bytes 393224 | tf_op jit(solution)/shard_map/ppermute | solution.py:19
  49.3 8.0 %collective-permute-start.24 = (bf16[2,128,256]{2,1,0:T(8,128)(2,1)S(1)}, bf16[2,128,256]{2,1,0:T(8,128)(2,1)S(1)}, u32[]{:S(2)}, u32[]{:S(2)}) collective-permute-start(bf16[2,128,256]{2,1,0:T(8,128)(2,1)S(1)} %pad_maximum_fusion.5), channel_id=1, source_target_pairs={{0,1},{1,0},{2,3},{3,2},{4,5},{5,4},{6,7},{7,6},{8,9},{9,8},{10,11... | collective-permute-start | bytes 393224 | tf_op jit(solution)/shard_map/ppermute | solution.py:19
  49.3 9.8 %collective-permute-start.21 = (bf16[128,512]{1,0:T(8,128)(2,1)S(1)}, bf16[128,512]{1,0:T(8,128)(2,1)S(1)}, u32[]{:S(2)}, u32[]{:S(2)}) collective-permute-start(bf16[128,512]{1,0:T(8,128)(2,1)S(1)} %collective-permute-done.15), channel_id=1, source_target_pairs={{0,1},{1,0},{2,3},{3,2},{4,5},{5,4},{6,7},{7,6},{8,9},{9,8},{10,11... | collective-permute-start | bytes 393224 | tf_op jit(solution)/shard_map/ppermute | solution.py:19
  56.5 2.5 %collective-permute-start.22 = (bf16[128,512]{1,0:T(8,128)(2,1)S(1)}, bf16[128,512]{1,0:T(8,128)(2,1)S(1)}, u32[]{:S(2)}, u32[]{:S(2)}) collective-permute-start(bf16[128,512]{1,0:T(8,128)(2,1)S(1)} %collective-permute-done.16), channel_id=1, source_target_pairs={{0,1},{1,0},{2,3},{3,2},{4,5},{5,4},{6,7},{7,6},{8,9},{9,8},{10,11... | collective-permute-start | bytes 393224 | tf_op jit(solution)/shard_map/ppermute | solution.py:19
  56.7 2.5 %collective-permute-start.20 = (bf16[128,512]{1,0:T(8,128)(2,1)S(1)}, bf16[128,512]{1,0:T(8,128)(2,1)S(1)}, u32[]{:S(2)}, u32[]{:S(2)}) collective-permute-start(bf16[128,512]{1,0:T(8,128)(2,1)S(1)} %collective-permute-done.14), channel_id=1, source_target_pairs={{0,1},{1,0},{2,3},{3,2},{4,5},{5,4},{6,7},{7,6},{8,9},{9,8},{10,11... | collective-permute-start | bytes 393224 | tf_op jit(solution)/shard_map/ppermute | solution.py:19
  57.2 13.4 %collective-permute-start.17 = (bf16[1,128,896]{2,1,0:T(8,128)(2,1)S(1)}, bf16[1,128,896]{2,1,0:T(8,128)(2,1)S(1)}, u32[]{:S(2)}, u32[]{:S(2)}) collective-permute-start(bf16[1,128,896]{2,1,0:T(8,128)(2,1)S(1)} %slice.112), channel_id=1, source_target_pairs={{0,16},{4,20},{8,24},{12,28},{16,0},{20,4},{24,8},{28,12},{1,17},{... | collective-permute-start | bytes 688136 | tf_op jit(solution)/shard_map/ppermute | solution.py:19
  58.5 8.0 %collective-permute-start.19 = (bf16[256,512]{1,0:T(8,128)(2,1)S(1)}, bf16[256,512]{1,0:T(8,128)(2,1)S(1)}, u32[]{:S(2)}, u32[]{:S(2)}) collective-permute-start(bf16[256,512]{1,0:T(8,128)(2,1)S(1)} %slice.68), channel_id=1, source_target_pairs={{0,4},{4,0},{8,12},{12,8},{16,20},{20,16},{24,28},{28,24},{1,5},{5... | collective-permute-start | bytes 786440 | tf_op jit(solution)/shard_map/ppermute | solution.py:19
  71.2 11.7 %collective-permute-start.25 = (bf16[2,128,896]{2,1,0:T(8,128)(2,1)S(1)}, bf16[2,128,896]{2,1,0:T(8,128)(2,1)S(1)}, u32[]{:S(2)}, u32[]{:S(2)}) collective-permute-start(bf16[2,128,896]{2,1,0:T(8,128)(2,1)S(1)} %bitcast.148), channel_id=1, source_target_pairs={{0,8},{4,12},{8,0},{12,4},{16,24},{20,28},{24,16},{28,20},{1,9},{5... | collective-permute-start | bytes 1376264 | tf_op jit(solution)/shard_map/ppermute | solution.py:19
  72.8 10.2 %collective-permute-start.27 = (bf16[32,896]{1,0:T(8,128)(2,1)S(1)}, bf16[32,896]{1,0:T(8,128)(2,1)S(1)}, u32[]{:S(2)}, u32[]{:S(2)}) collective-permute-start(bf16[32,896]{1,0:T(8,128)(2,1)S(1)} %fusion.6), channel_id=1, source_target_pairs={{0,4},{4,0},{8,12},{12,8},{16,20},{20,16},{24,28},{28,24},{1,5},{5... | collective-permute-start | bytes 172040 | tf_op jit(solution)/shard_map/ppermute | solution.py:19
  82.9 4.7 %collective-permute-start.28 = (bf16[32,896]{1,0:T(8,128)(2,1)S(1)}, bf16[32,896]{1,0:T(8,128)(2,1)S(1)}, u32[]{:S(2)}, u32[]{:S(2)}) collective-permute-start(bf16[32,896]{1,0:T(8,128)(2,1)S(1)} %add_convert_fusion.7), channel_id=1, source_target_pairs={{0,8},{4,12},{8,0},{12,4},{16,24},{20,28},{24,16},{28,20},{1,9},{5... | collective-permute-start | bytes 172040 | tf_op jit(solution)/shard_map/ppermute | solution.py:19
  83.4 14.7 %collective-permute-start.26 = (bf16[1,128,896]{2,1,0:T(8,128)(2,1)S(1)}, bf16[1,128,896]{2,1,0:T(8,128)(2,1)S(1)}, u32[]{:S(2)}, u32[]{:S(2)}) collective-permute-start(bf16[1,128,896]{2,1,0:T(8,128)(2,1)S(1)} %slice.111), channel_id=1, source_target_pairs={{0,16},{4,20},{8,24},{12,28},{16,0},{20,4},{24,8},{28,12},{1,17},{... | collective-permute-start | bytes 688136 | tf_op jit(solution)/shard_map/ppermute | solution.py:19
  87.7 11.1 %collective-permute-start.30 = (bf16[32,896]{1,0:T(8,128)(2,1)S(1)}, bf16[32,896]{1,0:T(8,128)(2,1)S(1)}, u32[]{:S(2)}, u32[]{:S(2)}) collective-permute-start(bf16[32,896]{1,0:T(8,128)(2,1)S(1)} %add_convert_fusion.6), channel_id=1, source_target_pairs={{0,16},{4,20},{8,24},{12,28},{16,0},{20,4},{24,8},{28,12},{1,17},{... | collective-permute-start | bytes 172040 | tf_op jit(solution)/shard_map/ppermute | solution.py:19
  99.7 12.6 %collective-permute-start.32 = (bf16[128,896]{1,0:T(8,128)(2,1)S(1)}, bf16[128,896]{1,0:T(8,128)(2,1)S(1)}, u32[]{:S(2)}, u32[]{:S(2)}) collective-permute-start(bf16[128,896]{1,0:T(8,128)(2,1)S(1)} %fusion.7), channel_id=1, source_target_pairs={{0,16},{4,20},{8,24},{12,28},{16,0},{20,4},{24,8},{28,12},{1,17},{... | collective-permute-start | bytes 688136 | tf_op jit(solution)/shard_map/ppermute | solution.py:19
  99.8 13.0 %collective-permute-start.34 = (bf16[128,896]{1,0:T(8,128)(2,1)S(1)}, bf16[128,896]{1,0:T(8,128)(2,1)S(1)}, u32[]{:S(2)}, u32[]{:S(2)}) collective-permute-start(bf16[128,896]{1,0:T(8,128)(2,1)S(1)} %fusion.7), channel_id=1, source_target_pairs={{0,8},{4,12},{8,0},{12,4},{16,24},{20,28},{24,16},{28,20},{1,9},{5... | collective-permute-start | bytes 688136 | tf_op jit(solution)/shard_map/ppermute | solution.py:19
  105.1 2.1 %collective-permute-start.29 = (bf16[128,512]{1,0:T(8,128)(2,1)S(1)}, bf16[128,512]{1,0:T(8,128)(2,1)S(1)}, u32[]{:S(2)}, u32[]{:S(2)}) collective-permute-start(bf16[128,512]{1,0:T(8,128)(2,1)S(1)} %get-tuple-element.164), channel_id=1, source_target_pairs={{0,1},{1,0},{2,3},{3,2},{4,5},{5,4},{6,7},{7,6},{8,9},{9,8},{10,11... | collective-permute-start | bytes 393224 | tf_op jit(solution)/shard_map/ppermute | solution.py:19
  105.6 10.5 %collective-permute-start.36 = (f32[32,544]{1,0:T(8,128)S(1)}, f32[32,544]{1,0:T(8,128)S(1)}, u32[]{:S(2)}, u32[]{:S(2)}) collective-permute-start(f32[32,544]{1,0:T(8,128)S(1)} %fusion.67), channel_id=1, source_target_pairs={{0,2},{1,3},{2,0},{3,1},{4,6},{5,7},{6,4},{7,5},{8,10},{9,11},{10,... | collective-permute-start | bytes 208904 | tf_op jit(solution)/shard_map/ppermute | solution.py:19
  114.4 8.1 %collective-permute-start.35 = (bf16[128,512]{1,0:T(8,128)(2,1)}, bf16[128,512]{1,0:T(8,128)(2,1)}, u32[]{:S(2)}, u32[]{:S(2)}) collective-permute-start(bf16[128,512]{1,0:T(8,128)(2,1)} %get-tuple-element.168), channel_id=1, source_target_pairs={{0,1},{1,0},{2,3},{3,2},{4,5},{5,4},{6,7},{7,6},{8,9},{9,8},{10,11... | collective-permute-start | bytes 393224 | tf_op jit(solution)/shard_map/ppermute | solution.py:19
  115.5 6.9 %collective-permute-start.33 = (bf16[128,512]{1,0:T(8,128)(2,1)}, bf16[128,512]{1,0:T(8,128)(2,1)}, u32[]{:S(2)}, u32[]{:S(2)}) collective-permute-start(bf16[128,512]{1,0:T(8,128)(2,1)} %get-tuple-element.166), channel_id=1, source_target_pairs={{0,1},{1,0},{2,3},{3,2},{4,5},{5,4},{6,7},{7,6},{8,9},{9,8},{10,11... | collective-permute-start | bytes 393224 | tf_op jit(solution)/shard_map/ppermute | solution.py:19
  116.7 4.8 %collective-permute-start.37 = (f32[32,544]{1,0:T(8,128)}, f32[32,544]{1,0:T(8,128)}, u32[]{:S(2)}, u32[]{:S(2)}) collective-permute-start(f32[32,544]{1,0:T(8,128)} %add.153), channel_id=1, source_target_pairs={{0,4},{4,0},{8,12},{12,8},{16,20},{20,16},{24,28},{28,24},{1,5},{5... | collective-permute-start | bytes 208904 | tf_op jit(solution)/shard_map/ppermute | solution.py:19
  117.2 9.4 %collective-permute-start.40 = (bf16[128,896]{1,0:T(8,128)(2,1)S(1)}, bf16[128,896]{1,0:T(8,128)(2,1)S(1)}, u32[]{:S(2)}, u32[]{:S(2)}) collective-permute-start(bf16[128,896]{1,0:T(8,128)(2,1)S(1)} %collective-permute-done.32), channel_id=1, source_target_pairs={{0,8},{4,12},{8,0},{12,4},{16,24},{20,28},{24,16},{28,20},{1,9},{5... | collective-permute-start | bytes 688136 | tf_op jit(solution)/shard_map/ppermute | solution.py:19
  122.4 6.3 %collective-permute-start.39 = (f32[32,544]{1,0:T(8,128)S(1)}, f32[32,544]{1,0:T(8,128)S(1)}, u32[]{:S(2)}, u32[]{:S(2)}) collective-permute-start(f32[32,544]{1,0:T(8,128)S(1)} %add.155), channel_id=1, source_target_pairs={{0,8},{4,12},{8,0},{12,4},{16,24},{20,28},{24,16},{28,20},{1,9},{5... | collective-permute-start | bytes 208904 | tf_op jit(solution)/shard_map/ppermute | solution.py:19
  123.5 12.2 %collective-permute-start.38 = (bf16[128,512]{1,0:T(8,128)(2,1)S(1)}, bf16[128,512]{1,0:T(8,128)(2,1)S(1)}, u32[]{:S(2)}, u32[]{:S(2)}) collective-permute-start(bf16[128,512]{1,0:T(8,128)(2,1)S(1)} %add_convert_fusion.2), channel_id=1, source_target_pairs={{0,16},{4,20},{8,24},{12,28},{16,0},{20,4},{24,8},{28,12},{1,17},{... | collective-permute-start | bytes 393224 | tf_op jit(solution)/shard_map/ppermute | solution.py:19
  126.5 5.7 %collective-permute-start.47 = (bf16[128,512]{1,0:T(8,128)(2,1)S(1)}, bf16[128,512]{1,0:T(8,128)(2,1)S(1)}, u32[]{:S(2)}, u32[]{:S(2)}) collective-permute-start(bf16[128,512]{1,0:T(8,128)(2,1)S(1)} %add_convert_fusion), channel_id=1, source_target_pairs={{0,8},{4,12},{8,0},{12,4},{16,24},{20,28},{24,16},{28,20},{1,9},{5... | collective-permute-start | bytes 393224 | tf_op jit(solution)/shard_map/ppermute | solution.py:19
  128.7 6.4 %collective-permute-start.41 = (f32[32,544]{1,0:T(8,128)S(1)}, f32[32,544]{1,0:T(8,128)S(1)}, u32[]{:S(2)}, u32[]{:S(2)}) collective-permute-start(f32[32,544]{1,0:T(8,128)S(1)} %add.156), channel_id=1, source_target_pairs={{0,16},{4,20},{8,24},{12,28},{16,0},{20,4},{24,8},{28,12},{1,17},{... | collective-permute-start | bytes 208904 | tf_op jit(solution)/shard_map/ppermute | solution.py:19
  136.4 17.2 %collective-permute-start.43 = (bf16[1,128,512]{2,1,0:T(8,128)(2,1)S(1)}, bf16[1,128,512]{2,1,0:T(8,128)(2,1)S(1)}, u32[]{:S(2)}, u32[]{:S(2)}) collective-permute-start(bf16[1,128,512]{2,1,0:T(8,128)(2,1)S(1)} %fusion.48), channel_id=1, source_target_pairs={{0,2},{1,3},{2,0},{3,1},{4,6},{5,7},{6,4},{7,5},{8,10},{9,11},{10,... | collective-permute-start | bytes 393224 | tf_op jit(solution)/shard_map/ppermute | solution.py:19
  143.8 4.2 %collective-permute-start.44 = (bf16[32,896]{1,0:T(8,128)(2,1)S(1)}, bf16[32,896]{1,0:T(8,128)(2,1)S(1)}, u32[]{:S(2)}, u32[]{:S(2)}) collective-permute-start(bf16[32,896]{1,0:T(8,128)(2,1)S(1)} %convolution_convert_fusion.8), channel_id=1, source_target_pairs={{0,4},{4,0},{8,12},{12,8},{16,20},{20,16},{24,28},{28,24},{1,5},{5... | collective-permute-start | bytes 172040 | tf_op jit(solution)/shard_map/ppermute | solution.py:19
  145.4 6.8 %collective-permute-start.46 = (bf16[128,512]{1,0:T(8,128)(2,1)S(1)}, bf16[128,512]{1,0:T(8,128)(2,1)S(1)}, u32[]{:S(2)}, u32[]{:S(2)}) collective-permute-start(bf16[128,512]{1,0:T(8,128)(2,1)S(1)} %add_convert_fusion.1), channel_id=1, source_target_pairs={{0,24},{4,28},{8,16},{12,20},{16,8},{20,12},{24,0},{28,4},{1,25},{... | collective-permute-start | bytes 393224 | tf_op jit(solution)/shard_map/ppermute | solution.py:19
  149.3 4.2 %collective-permute-start.45 = (bf16[32,896]{1,0:T(8,128)(2,1)S(1)}, bf16[32,896]{1,0:T(8,128)(2,1)S(1)}, u32[]{:S(2)}, u32[]{:S(2)}) collective-permute-start(bf16[32,896]{1,0:T(8,128)(2,1)S(1)} %add_convert_fusion.5), channel_id=1, source_target_pairs={{0,8},{4,12},{8,0},{12,4},{16,24},{20,28},{24,16},{28,20},{1,9},{5... | collective-permute-start | bytes 172040 | tf_op jit(solution)/shard_map/ppermute | solution.py:19
  153.7 5.0 %collective-permute-start.48 = (bf16[1,128,512]{2,1,0:T(8,128)(2,1)S(1)}, bf16[1,128,512]{2,1,0:T(8,128)(2,1)S(1)}, u32[]{:S(2)}, u32[]{:S(2)}) collective-permute-start(bf16[1,128,512]{2,1,0:T(8,128)(2,1)S(1)} %fusion.45), channel_id=1, source_target_pairs={{0,2},{1,3},{2,0},{3,1},{4,6},{5,7},{6,4},{7,5},{8,10},{9,11},{10,... | collective-permute-start | bytes 393224 | tf_op jit(solution)/shard_map/ppermute | solution.py:19
  154.3 5.3 %collective-permute-start.50 = (bf16[32,896]{1,0:T(8,128)(2,1)S(1)}, bf16[32,896]{1,0:T(8,128)(2,1)S(1)}, u32[]{:S(2)}, u32[]{:S(2)}) collective-permute-start(bf16[32,896]{1,0:T(8,128)(2,1)S(1)} %add_convert_fusion.4), channel_id=1, source_target_pairs={{0,16},{4,20},{8,24},{12,28},{16,0},{20,4},{24,8},{28,12},{1,17},{... | collective-permute-start | bytes 172040 | tf_op jit(solution)/shard_map/ppermute | solution.py:19
  158.9 2.8 %collective-permute-start.49 = (bf16[128,512]{1,0:T(8,128)(2,1)S(1)}, bf16[128,512]{1,0:T(8,128)(2,1)S(1)}, u32[]{:S(2)}, u32[]{:S(2)}) collective-permute-start(bf16[128,512]{1,0:T(8,128)(2,1)S(1)} %get-tuple-element.129), channel_id=1, source_target_pairs={{0,1},{1,0},{2,3},{3,2},{4,5},{5,4},{6,7},{7,6},{8,9},{9,8},{10,11... | collective-permute-start | bytes 393224 | tf_op jit(solution)/shard_map/ppermute | solution.py:19
  (29 other events, 211.5 us)
